TPU v7x, 32 devices: a whole 2x2x4 slice. The times are simulated.
32 devices in a mesh: pole: 2 (over y), row: 4 (over x, core), col: 4 (over z).
Axes of the slice: x: 2, y: 2, z: 4, core: 2. Of those that a mesh axis runs over, the one named last changes fastest.
Arguments:
- inverse_block: bfloat16 [16, 8, 256, 256], P(('pole', 'row'), 'col'), parts along dimension 0, may hold values from -6 to 6
- lower_block: bfloat16 [16, 8, 256, 256], P(('pole', 'row'), 'col'), parts along dimension 0, may hold values from -0.1875 to 0.1875
- pattern: int32 [8, 8], P('row', 'col'), may hold values 0 or 1
- diag_inverse: float32 [16, 256, 256], P(('pole', 'col'), 'row'), parts along dimension 0, may hold values from -6 to 6
Outputs:
- inverse_lower: bfloat16 [16, 8, 256, 256], P(('pole', 'row'), 'col'), parts along dimension 0
- inverse_diagonal: float32 [16, 256, 256], P(('pole', 'col'), 'row'), parts along dimension 0
There are 2 independent parts, one for each index of `pole`. A program takes and returns all parts, laid end to end along the dimension named above; an argument that names none is the same for every part. Nothing has to cross between parts.
All inputs are finite; a program needn't handle non-finite values. No bound on the sum of `pattern` on one device may be relied on, other than what follows from the above.
Results may differ from a plain program's by a relative error of at most 0.006.
Values may be sent and summed in bfloat16 or wider, within the bound.
No kernel may reach another device: no remote copies, remote signals or barrier semaphores. Data moves between devices by JAX's collectives and lax.ppermute only.
A program may use at most 64 MiB of HBM per device.

v0:
```python
import jax
import jax.numpy as jnp
from jax import lax
from jax.sharding import PartitionSpec as P


def on_device(inverse_block, lower_block, pattern, diag_inverse):
    keep_mask = pattern.astype(jnp.bfloat16)[:, :, None, None]
    masked = lower_block * keep_mask
    factor_cols = lax.all_gather(masked, "row", axis=0, tiled=True)
    gathered = lax.all_gather(inverse_block, "col", axis=1, tiled=True)
    totals = jnp.einsum(
        "ijab,jkbc->ikac", gathered, factor_cols, preferred_element_type=jnp.float32
    )
    inverse_lower = (-(keep_mask.astype(jnp.float32) * totals)).astype(jnp.bfloat16)
    diag_terms = jnp.einsum(
        "ikba,ikbc->kac", masked, inverse_lower, preferred_element_type=jnp.float32
    )
    summed = lax.psum_scatter(
        diag_terms.astype(jnp.bfloat16), "row", scatter_dimension=1, tiled=True
    ).astype(jnp.float32)
    inverse_diagonal = diag_inverse - summed
    return (inverse_lower, inverse_diagonal)


def solution(mesh):
    placed = (
        P(("pole", "row"), "col", None, None),
        P(("pole", "row"), "col", None, None),
        P("row", "col"),
        P(("pole", "col"), "row", None),
    )
    return jax.shard_map(
        on_device,
        mesh=mesh,
        in_specs=placed,
        out_specs=(P(("pole", "row"), "col", None, None), P(("pole", "col"), "row", None)),
        check_vma=False,
    )
```

profile of v0, /device:TPU:0, one launch (start us, length us, event | category | flops | bytes accessed | tf_op | source)
XLA Modules:
  0.0 114.5 jit_solution(3047192775130388619)
XLA Ops:
  7.2 0.0 all-gather.5.cloned.1.call-start
  7.2 0.7 all-gather.5.cloned.1.call-update
  7.9 0.0 all-gather.3.cloned.1.call-start
  7.9 0.7 convert_element_type.16
  8.6 0.1 copy.7
  8.7 1.2 %copy.8 = bf16[2,2,256,256]{2,3,0,1:T(8,128)(2,1)S(1)} copy(bf16[2,2,256,256]{3,2,1,0:T(8,128)(2,1)} %param.5) | data formatting | bytes 1048576 | tf_op args[1]
  10.0 0.9 broadcast_multiply_fusion
  10.9 0.0 all-gather.3.cloned.1.call-update
  10.9 0.0 reduce-scatter.2.cloned.1.call-start
  11.0 0.1 copy.6
  11.1 0.0 copy-start
  11.1 47.2 %all-gather.5.cloned.1.call-done = bf16[2,8,256,256]{3,2,1,0:T(8,128)(2,1)} async-done(((bf16[2,2,256,256]{3,2,1,0:T(8,128)(2,1)}), bf16[2,8,256,256]{3,2,1,0:T(8,128)(2,1)}) %all-gather.5.cloned.1.call-update) | async-done | bytes 2097168 | tf_op jit(solution)/shard_map/all_gather | solution.py:11
  58.2 23.5 %all-gather.3.cloned.1.call-done = bf16[8,2,256,256]{2,3,0,1:T(8,128)(2,1)} async-done(((bf16[2,2,256,256]{2,3,0,1:T(8,128)(2,1)}), bf16[8,2,256,256]{2,3,0,1:T(8,128)(2,1)}) %all-gather.3.cloned.1.call-update) | async-done | bytes 2097168 | tf_op jit(solution)/shard_map/all_gather | solution.py:10
  81.7 3.5 %fusion.18 = bf16[2,2,256,256]{2,3,0,1:T(8,128)(2,1)S(1)} fusion(bf16[2,8,256,256]{3,2,1,0:T(8,128)(2,1)} %all-gather.5.cloned.1.call-done, bf16[8,2,256,256]{2,3,0,1:T(8,128)(2,1)} %all-gather.3.cloned.1.call-done, f32[2,2]{0,1:T(2,128)S(1)} %copy.6), kind=kOutput, calls=%fused_computation.6 | convolution fusion | flops 1074528256 | bytes 4718608 | tf_op jit(solution)/shard_map/ijab,jkbc->ikac/dot_general | solution.py:12
  85.2 0.0 copy-done
  85.2 0.0 copy-start.1
  85.2 1.0 fusion.23
  86.3 0.0 reduce-scatter.2.cloned.1.call-update
  86.3 1.0 copy.10
  87.3 19.2 %reduce-scatter.2.cloned.1.call-done = bf16[2,64,256]{2,1,0:T(8,128)(2,1)} async-done(((bf16[2,256,256]{2,1,0:T(8,128)(2,1)}), bf16[2,64,256]{2,1,0:T(8,128)(2,1)}) %reduce-scatter.2.cloned.1.call-update) | async-done | bytes 65552 | tf_op jit(solution)/shard_map/reduce_scatter | solution.py:19
  106.5 0.0 copy-done.1
  106.5 1.5 %convert_subtract_fusion = f32[2,64,256]{2,1,0:T(8,128)} fusion(f32[2,64,256]{2,1,0:T(8,128)S(1)} %copy-done.1, bf16[2,64,256]{2,1,0:T(8,128)(2,1)} %reduce-scatter.2.cloned.1.call-done), kind=kLoop, calls=%fused_computation.10 | loop fusion | flops 65536 | bytes 327680 | tf_op jit(solution)/shard_map/sub | solution.py:22
Async XLA Ops:
  7.2 51.1 %all-gather.5.cloned.1.call-start = ((), (), s32[]{:S(2)}) async-start(), calls=%async_computation.2 | async-start | bytes 2621440 | tf_op jit(solution)/shard_map/all_gather | solution.py:11
  7.9 73.8 %all-gather.3.cloned.1.call-start = ((), (), s32[]{:S(2)}) async-start(), calls=%async_computation.1 | async-start | bytes 2621440 | tf_op jit(solution)/shard_map/all_gather | solution.py:10
  10.9 95.6 %reduce-scatter.2.cloned.1.call-start = ((), (), s32[]{:S(2)}) async-start(), calls=%async_computation.3 | async-start | bytes 327680 | tf_op jit(solution)/shard_map/reduce_scatter | solution.py:19
  11.1 74.2 %copy-start = (bf16[2,2,256,256]{2,3,0,1:T(8,128)(2,1)S(1)}, bf16[2,2,256,256]{2,3,0,1:T(8,128)(2,1)}, u32[]{:S(2)}) copy-start(bf16[2,2,256,256]{2,3,0,1:T(8,128)(2,1)} %broadcast_multiply_fusion) | copy-start | bytes 1572868
  85.2 21.3 %copy-start.1 = (f32[2,64,256]{2,1,0:T(8,128)S(1)}, f32[2,64,256]{2,1,0:T(8,128)}, u32[]{:S(2)}) copy-start(f32[2,64,256]{2,1,0:T(8,128)} %param.7) | copy-start | bytes 393220
Sparse Core Ops, SparseCore 0:
  9.6 48.6 all-gather.4
  60.4 21.2 all-gather.2
  86.4 20.0 reduce-scatter.1
where the time goes:
time: 115 us
  waiting for transfers between devices  90.6 us (79%)
  between operations  13.8 us (12%)
  matrix products  4.53 us (4%)
  other arithmetic  3.09 us (3%)
  local copies, waits for them, and re-layouts  2.46 us (2%)
    all_gather x1, waiting for transfers between devices, on_device(): gathered = lax.all_gather(inverse_block, 'col', axis=1, tiled=True)  47.2 us
    all_gather x1, waiting for transfers between devices, on_device(): factor_cols = lax.all_gather(masked, 'row', axis=0, tiled=True)  23.5 us
    reduce_scatter x1, waiting for transfers between devices, on_device(): lax.psum_scatter(diag_terms.astype(jnp.bfloat16), 'row', scatter_dimensio...  19.2 us
    dot_general x1, matrix products, on_device(): jnp.einsum('ijab,jkbc->ikac', gathered, factor_cols, preferred_element_ty...  3.5 us
  transfers between devices with their start and end apart: 3, of which 3 were waited for; matrix products, arithmetic and copies ran while one was open for 4% of the time, Pallas kernels for 0%

commit v1 on v0

v1 whole, which is shorter than its diff:
```python
import functools

import jax
import jax.numpy as jnp
from jax import lax
from jax.experimental import pallas as pl
from jax.experimental.pallas import tpu as pltpu
from jax.sharding import PartitionSpec as P

F32, BF16 = jnp.float32, jnp.bfloat16
VMEM = pl.BlockSpec(memory_space=pltpu.VMEM)
SMEM = pl.BlockSpec(memory_space=pltpu.SMEM)


def link_pairs(n, parity, step):
    pairs = []
    for i in range(parity, n - 1, 2):
        if i - step >= 0:
            pairs.append((i, i + 1))
        if i + 1 + step <= n - 1:
            pairs.append((i + 1, i))
    return pairs


def line_gather(own, axis, n, spread):
    me = lax.axis_index(axis) // spread
    even = lax.rem(me, 2) == 0
    rounds = []
    via = [own, own]
    for step in range(n - 1):
        arrived = [None, None]
        got = []
        for parity in (0, 1):
            pairs = link_pairs(n, parity, step)
            if not pairs:
                continue
            wide = [(a * spread + c, b * spread + c) for a, b in pairs for c in range(spread)]
            arrived[parity] = lax.ppermute(via[parity], axis, wide)
            from_above = even if parity == 0 else jnp.logical_not(even)
            source = jnp.where(from_above, me + 1 + step, me - 1 - step)
            source = jnp.where((source >= 0) & (source < n), source, -1)
            got.append((arrived[parity], source))
        rounds.append(got)
        via = [arrived[1], arrived[0]]
    return rounds


def mask_kernel(pattern, lower, masked):
    rows, cols = lower.shape[:2]
    for j in range(rows):
        for k in range(cols):
            keep = pattern[j, k].astype(F32)
            masked[j, k] = (lower[j, k].astype(F32) * keep).astype(BF16)


def mask(pattern, lower):
    return pl.pallas_call(
        mask_kernel,
        out_shape=jax.ShapeDtypeStruct(lower.shape, BF16),
        in_specs=[SMEM, VMEM],
        out_specs=VMEM,
    )(pattern, lower)


def add_products(place, block, factor, total):
    @pl.when(place >= 0)
    def _():
        at = jnp.maximum(place, 0)
        rows, inner = block.shape[:2]
        for i in range(rows):
            for k in range(total.shape[1]):
                partial = total[i, k]
                for j in range(inner):
                    partial += jnp.dot(block[i, j], factor[at, j, k], preferred_element_type=F32)
                total[i, k] = partial


def partial_kernel(count, places, *refs):
    blocks, (factor, total) = refs[:count], refs[count:]
    total[...] = jnp.zeros_like(total)
    for n, block in enumerate(blocks):
        add_products(places[n], block, factor, total)


def finish_kernel(count, n_row, places, *refs):
    blocks, (factor, total_in, pattern, masked, lower_out), sends = (
        refs[:count], refs[count:count + 5], refs[count + 5:]
    )
    total = sends[-1]
    sends = sends[:-1]
    total[...] = total_in[...]
    for n, block in enumerate(blocks):
        add_products(places[n], block, factor, total)
    me = places[count]
    rows, cols, b = total.shape[:3]
    piece = b // n_row
    for k in range(cols):
        update = jnp.zeros((b, b), F32)
        for i in range(rows):
            keep = pattern[i, k].astype(F32)
            value = (-(keep * total[i, k])).astype(BF16)
            lower_out[i, k] = value
            update += lax.dot_general(
                masked[i, k], value, (((0,), (0,)), ((), ())), preferred_element_type=F32
            )
        total[0, k] = update
    for d in range(n_row):
        there = jnp.bitwise_xor(me, d)
        for k in range(cols):
            sends[d][k] = total[0, k, pl.ds(pl.multiple_of(there * piece, 16), piece), :].astype(sends[d].dtype)


def last_kernel(*refs):
    diag, own, got, out = refs[0], refs[1], refs[2:-1], refs[-1]
    update = own[...]
    for part in got:
        update += part[...].astype(F32)
    out[...] = diag[...] - update


def solution(mesh):
    n_row, n_col = mesh.shape["row"], mesh.shape["col"]

    def on_device(inverse_block, lower_block, pattern, diag_inverse):
        row, col = lax.axis_index("row"), lax.axis_index("col")
        n_j = inverse_block.shape[1]
        rows, cols, b = lower_block.shape[:3]
        masked = mask(pattern, lower_block)

        rounds = line_gather(inverse_block, "col", n_col, 1)

        core = [(i, i ^ 1) for i in range(n_row)]
        pieces = [(masked, row)] + [
            (a, jnp.where(s >= 0, 2 * s + lax.rem(row, 2), -1))
            for got in line_gather(masked, "row", n_row // 2, 2)
            for a, s in got
        ]
        factor = jnp.zeros((n_row,) + masked.shape, BF16)
        for piece, source in pieces:
            other = lax.ppermute(piece, "row", core)
            for value, place in ((piece, source), (other, jnp.where(source >= 0, source ^ 1, -1))):
                there = jnp.maximum(place, 0)
                if n_row > 4:
                    kept = lax.dynamic_index_in_dim(factor, there, 0, keepdims=False)
                    value = jnp.where(place >= 0, value, kept)
                factor = lax.dynamic_update_index_in_dim(factor, value, there, 0)
        factor = factor.reshape((n_col, n_j, cols, b, b))

        early = [(inverse_block, col)] + [x for got in rounds[:-1] for x in got]
        late = rounds[-1]
        total = pl.pallas_call(
            functools.partial(partial_kernel, len(early)),
            out_shape=jax.ShapeDtypeStruct((rows, cols, b, b), F32),
            in_specs=[SMEM] + [VMEM] * (len(early) + 1),
            out_specs=VMEM,
            compiler_params=pltpu.CompilerParams(vmem_limit_bytes=48 << 20),
            cost_estimate=pl.CostEstimate(flops=2 * 24 * b**3, bytes_accessed=4 << 20, transcendentals=0),
        )(jnp.stack([p for _, p in early]).astype(jnp.int32), *[x for x, _ in early], factor)
        piece = jax.ShapeDtypeStruct((cols, b // n_row, b), BF16)
        results = pl.pallas_call(
            functools.partial(finish_kernel, len(late), n_row),
            out_shape=[jax.ShapeDtypeStruct(inverse_block.shape[:1] + lower_block.shape[1:], BF16),
                       jax.ShapeDtypeStruct(piece.shape, F32)] + [piece] * (n_row - 1),
            in_specs=[SMEM] + [VMEM] * (len(late) + 2) + [SMEM, VMEM],
            out_specs=[VMEM] * (n_row + 1),
            scratch_shapes=[pltpu.VMEM((rows, cols, b, b), F32)],
            compiler_params=pltpu.CompilerParams(vmem_limit_bytes=48 << 20),
        )(jnp.stack([p for _, p in late] + [row]).astype(jnp.int32), *[x for x, _ in late],
          factor, total, pattern, masked)
        inverse_lower, own, sends = results[0], results[1], results[2:]
        got = [lax.ppermute(s, "row", [(i, i ^ (d + 1)) for i in range(n_row)]) for d, s in enumerate(sends)]
        inverse_diagonal = pl.pallas_call(
            last_kernel,
            out_shape=jax.ShapeDtypeStruct(diag_inverse.shape, F32),
            in_specs=[VMEM] * (2 + len(got)),
            out_specs=VMEM,
        )(diag_inverse, own, *got)
        return inverse_lower, inverse_diagonal

    blocks, diag = P(("pole", "row"), "col", None, None), P(("pole", "col"), "row", None)
    return jax.shard_map(
        on_device,
        mesh=mesh,
        in_specs=(blocks, blocks, P("row", "col"), diag),
        out_specs=(blocks, diag),
        check_vma=False,
    )
```

time: 115 us -> 58.5 us (0.51)
  waiting for transfers between devices: 90.6 us -> 31.7 us
  between operations: 13.8 us -> 0.77 us
  starting transfers between devices: 0.12 us -> 12.2 us
  Pallas kernels: 0 us -> 8.43 us
  matrix products: 4.53 us -> 0 us
  other arithmetic: 3.09 us -> 0.07 us
  local copies, waits for them, and re-layouts: 2.46 us -> 4.88 us
    all_gather x2 -> x0, waiting for transfers between devices: 70.6 us -> none  [the longest x1 47.2 us: on_device(): gathered = lax.all_gather(inverse_block, 'col', axis=1, tiled=True)]
    ppermute x0 -> x11, waiting for transfers between devices: none -> 31.7 us  [the longest x6 28.1 us: line_gather(): arrived[parity] = lax.ppermute(via[parity], axis, wide)]
    reduce_scatter x1 -> x0, waiting for transfers between devices: 19.2 us -> none  [on_device(): lax.psum_scatter(diag_terms.astype(jnp.bfloat16), 'row', scatter_dimensio...]
    ppermute x0 -> x11, starting transfers between devices: none -> 12.2 us  [the longest x6 10.1 us: line_gather(): arrived[parity] = lax.ppermute(via[parity], axis, wide)]
    pallas_call x0 -> x4, Pallas kernels: none -> 8.43 us  [the longest x1 2.78 us: on_device(): pl.pallas_call(functools.partial(partial_kernel, len(early)), out_shape=j...]
    dot_general x2 -> x0, matrix products: 4.53 us -> none  [the longest x1 3.5 us: on_device(): jnp.einsum('ijab,jkbc->ikac', gathered, factor_cols, preferred_element_ty...]
    dynamic_update_slice x0 -> x4, local copies, waits for them, and re-layouts: none -> 3.29 us  [on_device(): factor = lax.dynamic_update_index_in_dim(factor, value, there, 0)]
    sub x1 -> x0, other arithmetic: 1.51 us -> none  [on_device(): inverse_diagonal = diag_inverse - summed]
  transfers between devices with their start and end apart: 3 -> 11, of which waited for: 3 -> 6; matrix products, arithmetic and copies ran while one was open for 4% -> 6% of each run, Pallas kernels for 0% -> 8%
where the time goes in v1:
time: 58.5 us; the launch traced here: 58.1 us
  waiting for transfers between devices  31.7 us (54%)
  starting transfers between devices  12.2 us (21%)
  Pallas kernels  8.43 us (14%)
  local copies, waits for them, and re-layouts  4.88 us (8%)
  between operations  0.77 us (1%)
    ppermute x6, waiting for transfers between devices, line_gather(): arrived[parity] = lax.ppermute(via[parity], axis, wide)  28.1 us
    ppermute x6, starting transfers between devices, line_gather(): arrived[parity] = lax.ppermute(via[parity], axis, wide)  10.1 us
    ppermute x3, waiting for transfers between devices, on_device(): lax.ppermute(s, 'row', [(i, i ^ d + 1) for i in range(n_row)])  3.6 us
    dynamic_update_slice x4, local copies, waits for them, and re-layouts, on_device(): factor = lax.dynamic_update_index_in_dim(factor, value, there, 0)  3.29 us
    pallas_call x1, Pallas kernels, on_device(): pl.pallas_call(functools.partial(partial_kernel, len(early)), out_shape=j...  2.78 us
    ppermute x3, starting transfers between devices, on_device(): lax.ppermute(s, 'row', [(i, i ^ d + 1) for i in range(n_row)])  2.14 us
    pallas_call x1, Pallas kernels, on_device(): pl.pallas_call(functools.partial(finish_kernel, len(late), n_row), out_sh...  2.01 us
    pallas_call x1, Pallas kernels, mask(): pl.pallas_call(mask_kernel, out_shape=jax.ShapeDtypeStruct(lower.shape, B...  1.93 us
  transfers between devices with their start and end apart: 11, of which 6 were waited for; matrix products, arithmetic and copies ran while one was open for 6% of the time, Pallas kernels for 8%

profile of v1, /device:TPU:0, one launch (start us, length us, event | category | flops | bytes accessed | tf_op | source)
XLA Modules:
  0.0 58.1 jit_solution(2622351921182563404)
XLA Ops:
  0.6 3.1 %collective-permute-start = (bf16[2,2,256,256]{3,2,1,0:T(8,128)(2,1)}, bf16[2,2,256,256]{3,2,1,0:T(8,128)(2,1)}, u32[]{:S(2)}, u32[]{:S(2)}) collective-permute-start(bf16[2,2,256,256]{3,2,1,0:T(8,128)(2,1)} %refs_0_.2), channel_id=1, source_target_pairs={{0,1},{1,0},{2,3},{3,2},{4,5},{5,4},{6,7},{7,6},{8,9},{9,8},{10,11... | collective-permute-start | bytes 1572872 | tf_op jit(solution)/shard_map/ppermute | solution.py:38
  3.7 1.9 %shard_map.59.refs_4_ = bf16[2,2,256,256]{3,2,1,0:T(8,128)(2,1)} custom-call(s32[2,2]{1,0:T(2,128)} %refs_3_.1, bf16[2,2,256,256]{3,2,1,0:T(8,128)(2,1)} %lower.1), custom_call_target="tpu_custom_call" | custom-call | tf_op jit(solution)/shard_map/pallas_call | solution.py:57
  5.7 1.5 %collective-permute-start.4 = (bf16[2,2,256,256]{3,2,1,0:T(8,128)(2,1)}, bf16[2,2,256,256]{3,2,1,0:T(8,128)(2,1)}, u32[]{:S(2)}, u32[]{:S(2)}) collective-permute-start(bf16[2,2,256,256]{3,2,1,0:T(8,128)(2,1)} %shard_map.59.refs_4_), channel_id=1, source_target_pairs={{0,8},{4,12},{8,0},{12,4},{1,9},{5,13},{9,1},{13,5},{2,10},{6,14},... | collective-permute-start | bytes 1572872 | tf_op jit(solution)/shard_map/ppermute | solution.py:38
  7.1 1.5 %collective-permute-start.6 = (bf16[2,2,256,256]{3,2,1,0:T(8,128)(2,1)}, bf16[2,2,256,256]{3,2,1,0:T(8,128)(2,1)}, u32[]{:S(2)}, u32[]{:S(2)}) collective-permute-start(bf16[2,2,256,256]{3,2,1,0:T(8,128)(2,1)} %refs_0_.2), channel_id=1, source_target_pairs={{1,2},{2,1},{5,6},{6,5},{9,10},{10,9},{13,14},{14,13},{17,18},{18,... | collective-permute-start | bytes 1572872 | tf_op jit(solution)/shard_map/ppermute | solution.py:38
  8.6 0.0 collective-permute-start.3
  8.6 7.4 %collective-permute-done.refs_1_ = bf16[2,2,256,256]{3,2,1,0:T(8,128)(2,1)} collective-permute-done((bf16[2,2,256,256]{3,2,1,0:T(8,128)(2,1)}, bf16[2,2,256,256]{3,2,1,0:T(8,128)(2,1)}, u32[]{:S(2)}, u32[]{:S(2)}) %collective-permute-start) | collective-permute-done | bytes 524320 | tf_op jit(solution)/shard_map/ppermute | solution.py:38
  16.0 1.5 %collective-permute-start.1 = (bf16[2,2,256,256]{3,2,1,0:T(8,128)(2,1)}, bf16[2,2,256,256]{3,2,1,0:T(8,128)(2,1)}, u32[]{:S(2)}, u32[]{:S(2)}) collective-permute-start(bf16[2,2,256,256]{3,2,1,0:T(8,128)(2,1)} %collective-permute-done.refs_1_), channel_id=1, source_target_pairs={{1,2},{2,1},{5,6},{6,5},{9,10},{10,9},{13,14},{14,13},{17,18},{18,... | collective-permute-start | bytes 1572872 | tf_op jit(solution)/shard_map/ppermute | solution.py:38
  17.4 0.2 broadcast_in_dim.16
  17.6 0.0 copy-start.1
  17.7 1.6 %collective-permute-done.4 = bf16[2,2,256,256]{3,2,1,0:T(8,128)(2,1)} collective-permute-done((bf16[2,2,256,256]{3,2,1,0:T(8,128)(2,1)}, bf16[2,2,256,256]{3,2,1,0:T(8,128)(2,1)}, u32[]{:S(2)}, u32[]{:S(2)}) %collective-permute-start.4) | collective-permute-done | bytes 524320 | tf_op jit(solution)/shard_map/ppermute | solution.py:38
  19.4 0.0 collective-permute-start.5
  19.4 0.1 pad_add_fusion.places
  19.5 0.1 stack.35.places
  19.5 1.3 %collective-permute-start.7 = (bf16[2,2,256,256]{3,2,1,0:T(8,128)(2,1)}, bf16[2,2,256,256]{3,2,1,0:T(8,128)(2,1)S(1)}, u32[]{:S(2)}, u32[]{:S(2)}) collective-permute-start(bf16[2,2,256,256]{3,2,1,0:T(8,128)(2,1)} %collective-permute-done.6.refs_2_), channel_id=1, source_target_pairs={{1,0},{2,3},{5,4},{6,7},{9,8},{10,11},{13,12},{14,15},{17,16},{18,... | collective-permute-start | bytes 1572872 | tf_op jit(solution)/shard_map/ppermute | solution.py:38
  20.8 1.1 %bitcast_dynamic-update-slice_fusion.2 = bf16[4,2,2,256,256]{4,3,2,1,0:T(8,128)(2,1)S(1)} fusion(bf16[4,2,2,256,256]{4,3,2,1,0:T(8,128)(2,1)S(1)} %bitcast_dynamic-update-slice_fusion.3, s32[]{:T(128)S(6)} %max.13, bf16[2,2,256,256]{3,2,1,0:T(8,128)(2,1)} %collective-permute-done.3), kind=kLoop, calls=%fused_computation.2 | loop fusion | bytes 1048580 | tf_op jit(solution)/shard_map/jit(dynamic_update_index_in_dim)/dynamic_update_slice | solution.py:146
  21.9 1.3 %collective-permute-start.2 = (bf16[2,2,256,256]{3,2,1,0:T(8,128)(2,1)}, bf16[2,2,256,256]{3,2,1,0:T(8,128)(2,1)S(1)}, u32[]{:S(2)}, u32[]{:S(2)}) collective-permute-start(bf16[2,2,256,256]{3,2,1,0:T(8,128)(2,1)} %collective-permute-done.1.refs_4_), channel_id=1, source_target_pairs={{1,0},{2,3},{5,4},{6,7},{9,8},{10,11},{13,12},{14,15},{17,16},{18,... | collective-permute-start | bytes 1572872 | tf_op jit(solution)/shard_map/ppermute | solution.py:38
  23.2 1.1 %bitcast_dynamic-update-slice_fusion.1 = bf16[4,2,2,256,256]{4,3,2,1,0:T(8,128)(2,1)S(1)} fusion(bf16[4,2,2,256,256]{4,3,2,1,0:T(8,128)(2,1)S(1)} %bitcast_dynamic-update-slice_fusion.2, s32[]{:T(128)S(6)} %max.14, bf16[2,2,256,256]{3,2,1,0:T(8,128)(2,1)} %collective-permute-done.4), kind=kLoop, calls=%fused_computation.1 | loop fusion | bytes 1048580 | tf_op jit(solution)/shard_map/jit(dynamic_update_index_in_dim)/dynamic_update_slice | solution.py:146
  24.3 0.0 collective-permute-done.5
  24.3 1.1 %bitcast_dynamic-update-slice_fusion.refs_5_.refs_1_ = bf16[4,2,2,256,256]{4,3,2,1,0:T(8,128)(2,1)S(1)} fusion(bf16[4,2,2,256,256]{4,3,2,1,0:T(8,128)(2,1)S(1)} %bitcast_dynamic-update-slice_fusion.1, s32[]{:T(128)S(6)} %max.15, bf16[2,2,256,256]{3,2,1,0:T(8,128)(2,1)} %collective-permute-done.5), kind=kLoop, calls=%fused_computation | loop fusion | bytes 1048580 | tf_op jit(solution)/shard_map/jit(dynamic_update_index_in_dim)/dynamic_update_slice | solution.py:146
  25.4 0.0 copy-start.3
  25.4 10.6 %collective-permute-done.7.refs_3_ = bf16[2,2,256,256]{3,2,1,0:T(8,128)(2,1)S(1)} collective-permute-done((bf16[2,2,256,256]{3,2,1,0:T(8,128)(2,1)}, bf16[2,2,256,256]{3,2,1,0:T(8,128)(2,1)S(1)}, u32[]{:S(2)}, u32[]{:S(2)}) %collective-permute-start.7) | collective-permute-done | bytes 524320 | tf_op jit(solution)/shard_map/ppermute | solution.py:38
  36.1 2.8 %shard_map.60.refs_2_ = f32[2,2,256,256]{3,2,1,0:T(8,128)S(1)} custom-call(s32[5]{0:T(128)S(1)} %stack.35.places, bf16[2,2,256,256]{3,2,1,0:T(8,128)(2,1)S(1)} %copy-done.1, bf16[2,2,256,256]{3,2,1,0:T(8,128)(2,1)} %collective-permute-done.refs_1_, bf16[2,2,256,256]{3,2,1,0:T(8,128)(2,1)} %collective-permute-done.6.refs_2_, ...), custom_call_target="tpu_custom_call" | custom-call | flops 805306368 | bytes 4194304 | tf_op jit(solution)/shard_map/pallas_call | solution.py:151
  38.9 8.4 %collective-permute-done.2.refs_0_ = bf16[2,2,256,256]{3,2,1,0:T(8,128)(2,1)S(1)} collective-permute-done((bf16[2,2,256,256]{3,2,1,0:T(8,128)(2,1)}, bf16[2,2,256,256]{3,2,1,0:T(8,128)(2,1)S(1)}, u32[]{:S(2)}, u32[]{:S(2)}) %collective-permute-start.2) | collective-permute-done | bytes 524320 | tf_op jit(solution)/shard_map/ppermute | solution.py:38
  47.3 2.0 %shard_map.61 = (bf16[2,2,256,256]{3,2,1,0:T(8,128)(2,1)}, f32[2,64,256]{2,1,0:T(8,128)S(1)}, bf16[2,64,256]{2,1,0:T(8,128)(2,1)S(1)}, bf16[2,64,256]{2,1,0:T(8,128)(2,1)S(1)}, bf16[2,64,256]{2,1,0:T(8,128)(2,1)S(1)}) custom-call(s32[2]{0:T(128)S(1)} %pad_add_fusion.places, bf16[2,2,256,256]{3,2,1,0:T(8,128)(2,1)S(1)} %collective-permute-done.2.refs_0_, ...), custom_call_target="tpu_custom_call" | custom-call | tf_op jit(solution)/shard_map/pallas_call | solution.py:160
  49.3 0.7 %copy-done.2 = f32[2,64,256]{2,1,0:T(8,128)} copy-done((f32[2,64,256]{2,1,0:T(8,128)}, f32[2,64,256]{2,1,0:T(8,128)S(1)}, u32[]{:S(2)}) %copy-start.2) | copy-done | bytes 131096
  50.0 1.5 %collective-permute-start.8 = (bf16[2,64,256]{2,1,0:T(8,128)(2,1)S(1)}, bf16[2,64,256]{2,1,0:T(8,128)(2,1)S(1)}, u32[]{:S(2)}, u32[]{:S(2)}) collective-permute-start(bf16[2,64,256]{2,1,0:T(8,128)(2,1)S(1)} %get-tuple-element.9), channel_id=1, source_target_pairs={{0,4},{4,0},{8,12},{12,8},{1,5},{5,1},{9,13},{13,9},{2,6},{6,2},{1... | collective-permute-start | bytes 196616 | tf_op jit(solution)/shard_map/ppermute | solution.py:171
  51.5 0.7 %collective-permute-start.9 = (bf16[2,64,256]{2,1,0:T(8,128)(2,1)S(1)}, bf16[2,64,256]{2,1,0:T(8,128)(2,1)S(1)}, u32[]{:S(2)}, u32[]{:S(2)}) collective-permute-start(bf16[2,64,256]{2,1,0:T(8,128)(2,1)S(1)} %get-tuple-element.10), channel_id=1, source_target_pairs={{0,8},{4,12},{8,0},{12,4},{1,9},{5,13},{9,1},{13,5},{2,10},{6,14},... | collective-permute-start | bytes 196616 | tf_op jit(solution)/shard_map/ppermute | solution.py:171
  52.1 2.2 %collective-permute-done.10.refs_4_ = bf16[2,64,256]{2,1,0:T(8,128)(2,1)S(1)} collective-permute-done((bf16[2,64,256]{2,1,0:T(8,128)(2,1)S(1)}, bf16[2,64,256]{2,1,0:T(8,128)(2,1)S(1)}, u32[]{:S(2)}, u32[]{:S(2)}) %collective-permute-start.10) | collective-permute-done | bytes 65568 | tf_op jit(solution)/shard_map/ppermute | solution.py:171
  54.3 0.0 collective-permute-done.8.refs_2_
  54.3 1.4 %collective-permute-done.9.refs_3_ = bf16[2,64,256]{2,1,0:T(8,128)(2,1)S(1)} collective-permute-done((bf16[2,64,256]{2,1,0:T(8,128)(2,1)S(1)}, bf16[2,64,256]{2,1,0:T(8,128)(2,1)S(1)}, u32[]{:S(2)}, u32[]{:S(2)}) %collective-permute-start.9) | collective-permute-done | bytes 65568 | tf_op jit(solution)/shard_map/ppermute | solution.py:171
  55.7 0.6 %copy-done.6 = bf16[2,64,256]{2,1,0:T(8,128)(2,1)} copy-done((bf16[2,64,256]{2,1,0:T(8,128)(2,1)}, bf16[2,64,256]{2,1,0:T(8,128)(2,1)S(1)}, u32[]{:S(2)}) %copy-start.6) | copy-done | bytes 65560
  56.4 1.7 %shard_map.62 = f32[2,64,256]{2,1,0:T(8,128)} custom-call(f32[2,64,256]{2,1,0:T(8,128)} %refs_0_.3, f32[2,64,256]{2,1,0:T(8,128)} %copy-done.2, bf16[2,64,256]{2,1,0:T(8,128)(2,1)} %copy-done.5, bf16[2,64,256]{2,1,0:T(8,128)(2,1)} %copy-done.6, bf16[2,64,256]{2,1,0:T(8,128)(2,1)} %copy-done.4), custom_call_target="tpu_custom_call" | custom-call | tf_op jit(solution)/shard_map/pallas_call | solution.py:172
  (15 shorter events, 0.1 us)
Async XLA Ops:
  0.6 15.3 %collective-permute-start = (bf16[2,2,256,256]{3,2,1,0:T(8,128)(2,1)}, bf16[2,2,256,256]{3,2,1,0:T(8,128)(2,1)}, u32[]{:S(2)}, u32[]{:S(2)}) collective-permute-start(bf16[2,2,256,256]{3,2,1,0:T(8,128)(2,1)} %refs_0_.2), channel_id=1, source_target_pairs={{0,1},{1,0},{2,3},{3,2},{4,5},{5,4},{6,7},{7,6},{8,9},{9,8},{10,11... | collective-permute-start | bytes 1572872 | tf_op jit(solution)/shard_map/ppermute | solution.py:38
  5.6 12.0 %copy-start = (bf16[2,2,256,256]{3,2,1,0:T(8,128)(2,1)S(1)}, bf16[2,2,256,256]{3,2,1,0:T(8,128)(2,1)}, u32[]{:S(2)}) copy-start(bf16[2,2,256,256]{3,2,1,0:T(8,128)(2,1)} %shard_map.59.refs_4_) | copy-start | bytes 1572868
  5.7 13.7 %collective-permute-start.4 = (bf16[2,2,256,256]{3,2,1,0:T(8,128)(2,1)}, bf16[2,2,256,256]{3,2,1,0:T(8,128)(2,1)}, u32[]{:S(2)}, u32[]{:S(2)}) collective-permute-start(bf16[2,2,256,256]{3,2,1,0:T(8,128)(2,1)} %shard_map.59.refs_4_), channel_id=1, source_target_pairs={{0,8},{4,12},{8,0},{12,4},{1,9},{5,13},{9,1},{13,5},{2,10},{6,14},... | collective-permute-start | bytes 1572872 | tf_op jit(solution)/shard_map/ppermute | solution.py:38
  7.1 12.4 %collective-permute-start.6 = (bf16[2,2,256,256]{3,2,1,0:T(8,128)(2,1)}, bf16[2,2,256,256]{3,2,1,0:T(8,128)(2,1)}, u32[]{:S(2)}, u32[]{:S(2)}) collective-permute-start(bf16[2,2,256,256]{3,2,1,0:T(8,128)(2,1)} %refs_0_.2), channel_id=1, source_target_pairs={{1,2},{2,1},{5,6},{6,5},{9,10},{10,9},{13,14},{14,13},{17,18},{18,... | collective-permute-start | bytes 1572872 | tf_op jit(solution)/shard_map/ppermute | solution.py:38
  8.6 12.2 %collective-permute-start.3 = (bf16[2,2,256,256]{3,2,1,0:T(8,128)(2,1)}, bf16[2,2,256,256]{3,2,1,0:T(8,128)(2,1)}, u32[]{:S(2)}, u32[]{:S(2)}) collective-permute-start(bf16[2,2,256,256]{3,2,1,0:T(8,128)(2,1)} %shard_map.59.refs_4_), channel_id=1, source_target_pairs={{0,4},{4,0},{8,12},{12,8},{1,5},{5,1},{9,13},{13,9},{2,6},{6,2},{1... | collective-permute-start | bytes 1572872 | tf_op jit(solution)/shard_map/ppermute | solution.py:140
  16.0 6.0 %collective-permute-start.1 = (bf16[2,2,256,256]{3,2,1,0:T(8,128)(2,1)}, bf16[2,2,256,256]{3,2,1,0:T(8,128)(2,1)}, u32[]{:S(2)}, u32[]{:S(2)}) collective-permute-start(bf16[2,2,256,256]{3,2,1,0:T(8,128)(2,1)} %collective-permute-done.refs_1_), channel_id=1, source_target_pairs={{1,2},{2,1},{5,6},{6,5},{9,10},{10,9},{13,14},{14,13},{17,18},{18,... | collective-permute-start | bytes 1572872 | tf_op jit(solution)/shard_map/ppermute | solution.py:38
  17.6 18.4 %copy-start.1 = (bf16[2,2,256,256]{3,2,1,0:T(8,128)(2,1)S(1)}, bf16[2,2,256,256]{3,2,1,0:T(8,128)(2,1)}, u32[]{:S(2)}) copy-start(bf16[2,2,256,256]{3,2,1,0:T(8,128)(2,1)} %refs_0_.2) | copy-start | bytes 1572868
  19.4 5.0 %collective-permute-start.5 = (bf16[2,2,256,256]{3,2,1,0:T(8,128)(2,1)}, bf16[2,2,256,256]{3,2,1,0:T(8,128)(2,1)}, u32[]{:S(2)}, u32[]{:S(2)}) collective-permute-start(bf16[2,2,256,256]{3,2,1,0:T(8,128)(2,1)} %collective-permute-done.4), channel_id=1, source_target_pairs={{0,4},{4,0},{8,12},{12,8},{1,5},{5,1},{9,13},{13,9},{2,6},{6,2},{1... | collective-permute-start | bytes 1572872 | tf_op jit(solution)/shard_map/ppermute | solution.py:140
  19.5 16.5 %collective-permute-start.7 = (bf16[2,2,256,256]{3,2,1,0:T(8,128)(2,1)}, bf16[2,2,256,256]{3,2,1,0:T(8,128)(2,1)S(1)}, u32[]{:S(2)}, u32[]{:S(2)}) collective-permute-start(bf16[2,2,256,256]{3,2,1,0:T(8,128)(2,1)} %collective-permute-done.6.refs_2_), channel_id=1, source_target_pairs={{1,0},{2,3},{5,4},{6,7},{9,8},{10,11},{13,12},{14,15},{17,16},{18,... | collective-permute-start | bytes 1572872 | tf_op jit(solution)/shard_map/ppermute | solution.py:38
  21.9 25.4 %collective-permute-start.2 = (bf16[2,2,256,256]{3,2,1,0:T(8,128)(2,1)}, bf16[2,2,256,256]{3,2,1,0:T(8,128)(2,1)S(1)}, u32[]{:S(2)}, u32[]{:S(2)}) collective-permute-start(bf16[2,2,256,256]{3,2,1,0:T(8,128)(2,1)} %collective-permute-done.1.refs_4_), channel_id=1, source_target_pairs={{1,0},{2,3},{5,4},{6,7},{9,8},{10,11},{13,12},{14,15},{17,16},{18,... | collective-permute-start | bytes 1572872 | tf_op jit(solution)/shard_map/ppermute | solution.py:38
  25.4 21.9 %copy-start.3 = (s32[2,2]{1,0:T(2,128)S(1)}, s32[2,2]{1,0:T(2,128)}, u32[]{:S(2)}) copy-start(s32[2,2]{1,0:T(2,128)} %refs_3_.1) | copy-start | bytes 52
  49.3 0.7 %copy-start.2 = (f32[2,64,256]{2,1,0:T(8,128)}, f32[2,64,256]{2,1,0:T(8,128)S(1)}, u32[]{:S(2)}) copy-start(f32[2,64,256]{2,1,0:T(8,128)S(1)} %get-tuple-element.8.refs_1_) | copy-start | bytes 393220
  50.0 4.3 %collective-permute-start.10 = (bf16[2,64,256]{2,1,0:T(8,128)(2,1)S(1)}, bf16[2,64,256]{2,1,0:T(8,128)(2,1)S(1)}, u32[]{:S(2)}, u32[]{:S(2)}) collective-permute-start(bf16[2,64,256]{2,1,0:T(8,128)(2,1)S(1)} %get-tuple-element.11), channel_id=1, source_target_pairs={{0,12},{4,8},{8,4},{12,0},{1,13},{5,9},{9,5},{13,1},{2,14},{6,10},... | collective-permute-start | bytes 196616 | tf_op jit(solution)/shard_map/ppermute | solution.py:171
  50.0 4.3 %collective-permute-start.8 = (bf16[2,64,256]{2,1,0:T(8,128)(2,1)S(1)}, bf16[2,64,256]{2,1,0:T(8,128)(2,1)S(1)}, u32[]{:S(2)}, u32[]{:S(2)}) collective-permute-start(bf16[2,64,256]{2,1,0:T(8,128)(2,1)S(1)} %get-tuple-element.9), channel_id=1, source_target_pairs={{0,4},{4,0},{8,12},{12,8},{1,5},{5,1},{9,13},{13,9},{2,6},{6,2},{1... | collective-permute-start | bytes 196616 | tf_op jit(solution)/shard_map/ppermute | solution.py:171
  51.5 4.3 %collective-permute-start.9 = (bf16[2,64,256]{2,1,0:T(8,128)(2,1)S(1)}, bf16[2,64,256]{2,1,0:T(8,128)(2,1)S(1)}, u32[]{:S(2)}, u32[]{:S(2)}) collective-permute-start(bf16[2,64,256]{2,1,0:T(8,128)(2,1)S(1)} %get-tuple-element.10), channel_id=1, source_target_pairs={{0,8},{4,12},{8,0},{12,4},{1,9},{5,13},{9,1},{13,5},{2,10},{6,14},... | collective-permute-start | bytes 196616 | tf_op jit(solution)/shard_map/ppermute | solution.py:171
  54.3 1.4 %copy-start.4 = (bf16[2,64,256]{2,1,0:T(8,128)(2,1)}, bf16[2,64,256]{2,1,0:T(8,128)(2,1)S(1)}, u32[]{:S(2)}) copy-start(bf16[2,64,256]{2,1,0:T(8,128)(2,1)S(1)} %collective-permute-done.10.refs_4_) | copy-start | bytes 196612
  54.3 1.4 %copy-start.5 = (bf16[2,64,256]{2,1,0:T(8,128)(2,1)}, bf16[2,64,256]{2,1,0:T(8,128)(2,1)S(1)}, u32[]{:S(2)}) copy-start(bf16[2,64,256]{2,1,0:T(8,128)(2,1)S(1)} %collective-permute-done.8.refs_2_) | copy-start | bytes 196612
  55.7 0.6 %copy-start.6 = (bf16[2,64,256]{2,1,0:T(8,128)(2,1)}, bf16[2,64,256]{2,1,0:T(8,128)(2,1)S(1)}, u32[]{:S(2)}) copy-start(bf16[2,64,256]{2,1,0:T(8,128)(2,1)S(1)} %collective-permute-done.9.refs_3_) | copy-start | bytes 196612

commit v2 on v0

v2 whole, which is shorter than its diff:
```python
import functools

import jax
import jax.numpy as jnp
from jax import lax
from jax.experimental import pallas as pl
from jax.experimental.pallas import tpu as pltpu
from jax.sharding import PartitionSpec as P

F32, BF16 = jnp.float32, jnp.bfloat16
VMEM = pl.BlockSpec(memory_space=pltpu.VMEM)
SMEM = pl.BlockSpec(memory_space=pltpu.SMEM)


def exchange(array, axis, n, distance):
    return lax.ppermute(array, axis, [(i, i ^ distance) for i in range(n)])


def gather(own, axis, n, distances):
    held = [(own, 0)]
    for distance in distances:
        held += [(exchange(a, axis, n, distance), d ^ distance) for a, d in held]
    return held


def column_gather(own, n):
    beside = exchange(own, "col", n, 1)
    held = gather(own, "col", n, [1 << p for p in reversed(range(1, n.bit_length() - 1))])
    beside, *afar = lax.optimization_barrier((beside, *[a for a, _ in held[1:]]))
    afar = [(a, d) for a, (_, d) in zip(afar, held[1:])]
    return [(own, 0), (beside, 1)] + afar + [(exchange(a, "col", n, 1), d ^ 1) for a, d in afar]


def mask_kernel(pattern, token, lower, masked, turned):
    rows, cols = lower.shape[:2]
    for j in range(rows):
        for k in range(cols):
            keep = pattern[j, k].astype(F32)
            value = lower[j, k].astype(F32) * keep
            masked[j, k] = value.astype(BF16)
            turned[j, k] = value.T.astype(BF16)


def add_products(place, block, factor, total):
    rows, inner = block.shape[:2]
    for i in range(rows):
        for k in range(total.shape[1]):
            partial = total[i, k]
            for j in range(inner):
                partial += jnp.dot(block[i, j], factor[place, j, k], preferred_element_type=F32)
            total[i, k] = partial


def early_kernel(n_pieces, n_blocks, owners, places, *refs):
    pieces, blocks, (factor, total) = refs[:n_pieces], refs[n_pieces:n_pieces + n_blocks], refs[n_pieces + n_blocks:]
    for n, piece in enumerate(pieces):
        factor[owners[n]] = piece[...]

    total[...] = jnp.zeros_like(total)
    for n, block in enumerate(blocks):
        add_products(places[n], block, factor, total)


def finish_kernel(n_blocks, n_row, places, *refs):
    blocks = refs[:n_blocks]
    factor, total_in, pattern, turned, lower_out = refs[n_blocks:n_blocks + 5]
    sends, total = refs[n_blocks + 5:-1], refs[-1]
    total[...] = total_in[...]
    for n, block in enumerate(blocks):
        add_products(places[n], block, factor, total)
    row = places[n_blocks]
    rows, cols, b = total.shape[:3]
    piece = b // n_row
    for k in range(cols):
        update = jnp.zeros((b, b), F32)
        for i in range(rows):
            keep = pattern[i, k].astype(F32)
            value = (-(keep * total[i, k])).astype(BF16)
            lower_out[i, k] = value
            update += jnp.dot(turned[i, k], value, preferred_element_type=F32)
        total[0, k] = update
        for d in range(n_row):
            there = pl.multiple_of(jnp.bitwise_xor(row, d) * piece, 16)
            sends[d][k] = total[0, k, pl.ds(there, piece), :].astype(sends[d].dtype)


def last_kernel(*refs):
    diag, own, got, out = refs[0], refs[1], refs[2:-1], refs[-1]
    update = own[...]
    for part in got:
        update += part[...].astype(F32)
    out[...] = diag[...] - update


def call(kernel, out_shape, in_specs, mib, flops=0, scratch=()):
    return pl.pallas_call(
        kernel,
        out_shape=out_shape,
        in_specs=in_specs,
        out_specs=jax.tree.map(lambda _: VMEM, out_shape),
        scratch_shapes=scratch,
        compiler_params=pltpu.CompilerParams(vmem_limit_bytes=mib << 20),
        cost_estimate=pl.CostEstimate(flops=0, bytes_accessed=0, transcendentals=0),
    )


def solution(mesh):
    n_row, n_col = mesh.shape["row"], mesh.shape["col"]

    def on_device(inverse_block, lower_block, pattern, diag_inverse):
        row, col = lax.axis_index("row"), lax.axis_index("col")
        rows, cols, b = lower_block.shape[:3]
        shape = jax.ShapeDtypeStruct

        far = [1 << p for p in range(1, n_row.bit_length() - 1)]
        blocks = column_gather(inverse_block, n_col)
        early, late = blocks[:-1], blocks[-1:]
        token = exchange(pattern, "row", n_row, 1)

        kept = shape(lower_block.shape, BF16)
        masked, turned = call(mask_kernel, [kept, kept], [SMEM, SMEM, VMEM], 60)(pattern, token, lower_block)
        pieces = gather(masked, "row", n_row, far + [1])
        arrays = len(pieces) + len(early)
        factor, total = call(
            functools.partial(early_kernel, len(pieces), len(early)),
            [shape((n_row,) + kept.shape, BF16), shape((rows, cols, b, b), F32)],
            [SMEM, SMEM] + [VMEM] * arrays,
            8 + arrays + n_row,
            48 * b**3,
        )(jnp.stack([row ^ d for _, d in pieces]).astype(jnp.int32), jnp.stack([col ^ d for _, d in early]).astype(jnp.int32),
          *[x for x, _ in pieces], *[x for x, _ in early])
        part = shape((cols, b // n_row, b), BF16)
        lower_out, own, *sends = call(
            functools.partial(finish_kernel, len(late), n_row),
            [shape((rows, cols, b, b), BF16), shape(part.shape, F32)] + [part] * (n_row - 1),
            [SMEM] + [VMEM] * (len(late) + 2) + [SMEM, VMEM],
            12 + n_row,
            24 * b**3,
            [pltpu.VMEM((rows, cols, b, b), F32)],
        )(jnp.stack([col ^ d for _, d in late] + [row]).astype(jnp.int32), *[x for x, _ in late],
          factor, total, pattern, turned)
        got = [exchange(s, "row", n_row, d) for d, s in enumerate(sends, 1)]
        diag_out = call(last_kernel, shape(diag_inverse.shape, F32), [VMEM] * (2 + len(got)), 4)(diag_inverse, own, *got)
        return lower_out, diag_out

    spec, diag = P(("pole", "row"), "col", None, None), P(("pole", "col"), "row", None)
    return jax.shard_map(
        on_device,
        mesh=mesh,
        in_specs=(spec, spec, P("row", "col"), diag),
        out_specs=(spec, diag),
        check_vma=False,
    )
```

time: 115 us -> 52.4 us (0.46)
  waiting for transfers between devices: 90.6 us -> 32.1 us
  between operations: 13.8 us -> 0.66 us
  starting transfers between devices: 0.12 us -> 9.47 us
  Pallas kernels: 0 us -> 6.96 us
  matrix products: 4.53 us -> 0 us
  other arithmetic: 3.09 us -> 0.23 us
    all_gather x2 -> x0, waiting for transfers between devices: 70.6 us -> none  [the longest x1 47.2 us: on_device(): gathered = lax.all_gather(inverse_block, 'col', axis=1, tiled=True)]
    ppermute x0 -> x10, waiting for transfers between devices: none -> 32.1 us  [exchange(): return lax.ppermute(array, axis, [(i, i ^ distance) for i in range(n)])]
    reduce_scatter x1 -> x0, waiting for transfers between devices: 19.2 us -> none  [on_device(): lax.psum_scatter(diag_terms.astype(jnp.bfloat16), 'row', scatter_dimensio...]
    ppermute x0 -> x10, starting transfers between devices: none -> 9.47 us  [exchange(): return lax.ppermute(array, axis, [(i, i ^ distance) for i in range(n)])]
    pallas_call x0 -> x4, Pallas kernels: none -> 6.96 us  [the longest x1 2.17 us: on_device(): call(mask_kernel, [kept, kept], [SMEM, SMEM, VMEM], 60)]
    dot_general x2 -> x0, matrix products: 4.53 us -> none  [the longest x1 3.5 us: on_device(): jnp.einsum('ijab,jkbc->ikac', gathered, factor_cols, preferred_element_ty...]
    sub x1 -> x0, other arithmetic: 1.51 us -> none  [on_device(): inverse_diagonal = diag_inverse - summed]
    unnamed x6 -> x12, local copies, waits for them, and re-layouts: 2.25 us -> 2.66 us
  transfers between devices with their start and end apart: 3 -> 10, of which waited for: 3 -> 7; matrix products, arithmetic and copies ran while one was open for 4% -> 0% of each run, Pallas kernels for 0% -> 8%
where the time goes in v2:
time: 52.4 us; the launch traced here: 52.1 us
  waiting for transfers between devices  32.1 us (61%)
  starting transfers between devices  9.47 us (18%)
  Pallas kernels  6.96 us (13%)
  local copies, waits for them, and re-layouts  2.66 us (5%)
  between operations  0.66 us (1%)
    ppermute x10, waiting for transfers between devices, exchange(): return lax.ppermute(array, axis, [(i, i ^ distance) for i in range(n)])  32.1 us
    ppermute x10, starting transfers between devices, exchange(): return lax.ppermute(array, axis, [(i, i ^ distance) for i in range(n)])  9.47 us
    unnamed x12, local copies, waits for them, and re-layouts  2.66 us
    pallas_call x1, Pallas kernels, on_device(): call(mask_kernel, [kept, kept], [SMEM, SMEM, VMEM], 60)  2.17 us
    pallas_call x1, Pallas kernels, on_device(): call(functools.partial(early_kernel, len(pieces), len(early)), [shape((n_...  2.16 us
    pallas_call x1, Pallas kernels, on_device(): call(functools.partial(finish_kernel, len(late), n_row), [shape((rows, co...  1.93 us
  transfers between devices with their start and end apart: 10, of which 7 were waited for; matrix products, arithmetic and copies ran while one was open for 0% of the time, Pallas kernels for 8%

profile of v2, /device:TPU:0, one launch (start us, length us, event | category | flops | bytes accessed | tf_op | source)
XLA Modules:
  0.0 52.1 jit_solution(7959978548965983262)
XLA Ops:
  0.6 0.0 copy-start.4
  0.6 3.1 %collective-permute-start = (bf16[2,2,256,256]{3,2,1,0:T(8,128)(2,1)}, bf16[2,2,256,256]{3,2,1,0:T(8,128)(2,1)S(1)}, u32[]{:S(2)}, u32[]{:S(2)}) collective-permute-start(bf16[2,2,256,256]{3,2,1,0:T(8,128)(2,1)} %refs_4_.1), channel_id=1, source_target_pairs={{0,1},{1,0},{2,3},{3,2},{4,5},{5,4},{6,7},{7,6},{8,9},{9,8},{10,11... | collective-permute-start | bytes 1572872 | tf_op jit(solution)/shard_map/ppermute | solution.py:16
  3.7 2.6 %collective-permute-start.1 = (bf16[2,2,256,256]{3,2,1,0:T(8,128)(2,1)}, bf16[2,2,256,256]{3,2,1,0:T(8,128)(2,1)S(1)}, u32[]{:S(2)}, u32[]{:S(2)}) collective-permute-start(bf16[2,2,256,256]{3,2,1,0:T(8,128)(2,1)} %refs_4_.1), channel_id=1, source_target_pairs={{0,2},{1,3},{2,0},{3,1},{4,6},{5,7},{6,4},{7,5},{8,10},{9,11},{10,... | collective-permute-start | bytes 1572872 | tf_op jit(solution)/shard_map/ppermute | solution.py:16
  6.3 0.0 collective-permute-start.3
  6.3 1.3 %collective-permute-done.3.token = s32[2,2]{1,0:T(2,128)S(1)} collective-permute-done((s32[2,2]{1,0:T(2,128)}, s32[2,2]{1,0:T(2,128)S(1)}, u32[]{:S(2)}, u32[]{:S(2)}) %collective-permute-start.3) | collective-permute-done | bytes 48 | tf_op jit(solution)/shard_map/ppermute | solution.py:16
  7.7 0.6 %copy-done.5 = s32[2,2]{1,0:T(2,128)} copy-done((s32[2,2]{1,0:T(2,128)}, s32[2,2]{1,0:T(2,128)S(1)}, u32[]{:S(2)}) %copy-start.5) | copy-done | bytes 40
  8.2 2.2 %shard_map.59 = (bf16[2,2,256,256]{3,2,1,0:T(8,128)(2,1)}, bf16[2,2,256,256]{3,2,1,0:T(8,128)(2,1)}) custom-call(s32[2,2]{1,0:T(2,128)} %refs_3_.1, s32[2,2]{1,0:T(2,128)} %copy-done.5, bf16[2,2,256,256]{3,2,1,0:T(8,128)(2,1)} %lower.1), custom_call_target="tpu_custom_call" | custom-call | tf_op jit(solution)/shard_map/pallas_call | solution.py:121
  10.4 1.5 %collective-permute-start.4 = (bf16[2,2,256,256]{3,2,1,0:T(8,128)(2,1)}, bf16[2,2,256,256]{3,2,1,0:T(8,128)(2,1)S(1)}, u32[]{:S(2)}, u32[]{:S(2)}) collective-permute-start(bf16[2,2,256,256]{3,2,1,0:T(8,128)(2,1)} %get-tuple-element.14.refs_0_), channel_id=1, source_target_pairs={{0,8},{4,12},{8,0},{12,4},{1,9},{5,13},{9,1},{13,5},{2,10},{6,14},... | collective-permute-start | bytes 1572872 | tf_op jit(solution)/shard_map/ppermute | solution.py:16
  11.9 0.0 collective-permute-start.5
  11.9 15.1 %collective-permute-done.refs_5_ = bf16[2,2,256,256]{3,2,1,0:T(8,128)(2,1)S(1)} collective-permute-done((bf16[2,2,256,256]{3,2,1,0:T(8,128)(2,1)}, bf16[2,2,256,256]{3,2,1,0:T(8,128)(2,1)S(1)}, u32[]{:S(2)}, u32[]{:S(2)}) %collective-permute-start) | collective-permute-done | bytes 524320 | tf_op jit(solution)/shard_map/ppermute | solution.py:16
  27.0 2.5 %collective-permute-done.1.refs_6_ = bf16[2,2,256,256]{3,2,1,0:T(8,128)(2,1)S(1)} collective-permute-done((bf16[2,2,256,256]{3,2,1,0:T(8,128)(2,1)}, bf16[2,2,256,256]{3,2,1,0:T(8,128)(2,1)S(1)}, u32[]{:S(2)}, u32[]{:S(2)}) %collective-permute-start.1) | collective-permute-done | bytes 524320 | tf_op jit(solution)/shard_map/ppermute | solution.py:16
  29.5 0.0 collective-permute-done.4.refs_1_
  29.5 0.0 collective-permute-start.6
  29.5 0.4 collective-permute-start.2
  30.0 0.1 pad_add_fusion.places
  30.0 0.1 pad_add_fusion.1.owners
  30.1 0.1 pad_add_fusion.2.places
  30.2 0.0 collective-permute-done.5.refs_2_
  30.2 1.4 %collective-permute-done.6.refs_3_ = bf16[2,2,256,256]{3,2,1,0:T(8,128)(2,1)} collective-permute-done((bf16[2,2,256,256]{3,2,1,0:T(8,128)(2,1)S(1)}, bf16[2,2,256,256]{3,2,1,0:T(8,128)(2,1)}, u32[]{:S(2)}, u32[]{:S(2)}) %collective-permute-start.6) | collective-permute-done | bytes 524320 | tf_op jit(solution)/shard_map/ppermute | solution.py:16
  31.6 1.0 %copy-done.1 = bf16[2,2,256,256]{3,2,1,0:T(8,128)(2,1)S(1)} copy-done((bf16[2,2,256,256]{3,2,1,0:T(8,128)(2,1)S(1)}, bf16[2,2,256,256]{3,2,1,0:T(8,128)(2,1)}, u32[]{:S(2)}) %copy-start.1) | copy-done | bytes 524312
  32.6 1.0 %copy-done.2 = bf16[2,2,256,256]{3,2,1,0:T(8,128)(2,1)S(1)} copy-done((bf16[2,2,256,256]{3,2,1,0:T(8,128)(2,1)S(1)}, bf16[2,2,256,256]{3,2,1,0:T(8,128)(2,1)}, u32[]{:S(2)}) %copy-start.2) | copy-done | bytes 524312
  33.7 2.2 %shard_map.60 = (bf16[4,2,2,256,256]{4,3,2,1,0:T(8,128)(2,1)S(1)}, f32[2,2,256,256]{3,2,1,0:T(8,128)S(1)}) custom-call(s32[4]{0:T(128)S(1)} %pad_add_fusion.1.owners, s32[3]{0:T(128)S(1)} %pad_add_fusion.2.places, bf16[2,2,256,256]{3,2,1,0:T(8,128)(2,1)S(1)} %copy-done.2, bf16[2,2,256,256]{3,2,1,0:T(8,128)(2,1)S(1)} %collective-permute-done.4.refs_1_, ...), custom_call_target="tpu_custom_call" | custom-call | tf_op jit(solution)/shard_map/pallas_call | solution.py:124
  35.8 8.0 %collective-permute-done.2.refs_0_ = bf16[2,2,256,256]{3,2,1,0:T(8,128)(2,1)S(1)} collective-permute-done((bf16[2,2,256,256]{3,2,1,0:T(8,128)(2,1)S(1)}, bf16[2,2,256,256]{3,2,1,0:T(8,128)(2,1)S(1)}, u32[]{:S(2)}, u32[]{:S(2)}) %collective-permute-start.2) | collective-permute-done | bytes 524320 | tf_op jit(solution)/shard_map/ppermute | solution.py:16
  43.9 0.0 copy-done.4
  43.9 1.9 %shard_map.61 = (bf16[2,2,256,256]{3,2,1,0:T(8,128)(2,1)}, f32[2,64,256]{2,1,0:T(8,128)S(1)}, bf16[2,64,256]{2,1,0:T(8,128)(2,1)S(1)}, bf16[2,64,256]{2,1,0:T(8,128)(2,1)S(1)}, bf16[2,64,256]{2,1,0:T(8,128)(2,1)S(1)}) custom-call(s32[2]{0:T(128)S(1)} %pad_add_fusion.places, bf16[2,2,256,256]{3,2,1,0:T(8,128)(2,1)S(1)} %collective-permute-done.2.refs_0_, ...), custom_call_target="tpu_custom_call" | custom-call | tf_op jit(solution)/shard_map/pallas_call | solution.py:133
  45.8 0.0 collective-permute-start.7
  45.8 1.5 %collective-permute-start.8 = (bf16[2,64,256]{2,1,0:T(8,128)(2,1)S(1)}, bf16[2,64,256]{2,1,0:T(8,128)(2,1)S(1)}, u32[]{:S(2)}, u32[]{:S(2)}) collective-permute-start(bf16[2,64,256]{2,1,0:T(8,128)(2,1)S(1)} %get-tuple-element.22), channel_id=1, source_target_pairs={{0,8},{4,12},{8,0},{12,4},{1,9},{5,13},{9,1},{13,5},{2,10},{6,14},... | collective-permute-start | bytes 196616 | tf_op jit(solution)/shard_map/ppermute | solution.py:16
  47.3 0.4 collective-permute-start.9
  47.7 0.0 collective-permute-done.7.refs_2_
  47.7 2.7 %collective-permute-done.8.refs_3_ = bf16[2,64,256]{2,1,0:T(8,128)(2,1)S(1)} collective-permute-done((bf16[2,64,256]{2,1,0:T(8,128)(2,1)S(1)}, bf16[2,64,256]{2,1,0:T(8,128)(2,1)S(1)}, u32[]{:S(2)}, u32[]{:S(2)}) %collective-permute-start.8) | collective-permute-done | bytes 65568 | tf_op jit(solution)/shard_map/ppermute | solution.py:16
  50.3 1.1 %collective-permute-done.9.refs_4_ = bf16[2,64,256]{2,1,0:T(8,128)(2,1)S(1)} collective-permute-done((bf16[2,64,256]{2,1,0:T(8,128)(2,1)S(1)}, bf16[2,64,256]{2,1,0:T(8,128)(2,1)S(1)}, u32[]{:S(2)}, u32[]{:S(2)}) %collective-permute-start.9) | collective-permute-done | bytes 65568 | tf_op jit(solution)/shard_map/ppermute | solution.py:16
  51.4 0.7 %shard_map.62 = f32[2,64,256]{2,1,0:T(8,128)} custom-call(f32[2,64,256]{2,1,0:T(8,128)S(1)} %copy-done.3, f32[2,64,256]{2,1,0:T(8,128)S(1)} %get-tuple-element.20.refs_1_, bf16[2,64,256]{2,1,0:T(8,128)(2,1)S(1)} %collective-permute-done.7.refs_2_, bf16[2,64,256]{2,1,0:T(8,128)(2,1)S(1)} %collective-permute-done.8.refs_3_, ...), custom_call_target="tpu_custom_call" | custom-call | tf_op jit(solution)/shard_map/pallas_call | solution.py:143
  (7 shorter events, 0.0 us)
Async XLA Ops:
  0.6 43.2 %copy-start.4 = (s32[2,2]{1,0:T(2,128)S(1)}, s32[2,2]{1,0:T(2,128)}, u32[]{:S(2)}) copy-start(s32[2,2]{1,0:T(2,128)} %refs_3_.1) | copy-start | bytes 52
  0.6 26.3 %collective-permute-start = (bf16[2,2,256,256]{3,2,1,0:T(8,128)(2,1)}, bf16[2,2,256,256]{3,2,1,0:T(8,128)(2,1)S(1)}, u32[]{:S(2)}, u32[]{:S(2)}) collective-permute-start(bf16[2,2,256,256]{3,2,1,0:T(8,128)(2,1)} %refs_4_.1), channel_id=1, source_target_pairs={{0,1},{1,0},{2,3},{3,2},{4,5},{5,4},{6,7},{7,6},{8,9},{9,8},{10,11... | collective-permute-start | bytes 1572872 | tf_op jit(solution)/shard_map/ppermute | solution.py:16
  3.7 25.8 %collective-permute-start.1 = (bf16[2,2,256,256]{3,2,1,0:T(8,128)(2,1)}, bf16[2,2,256,256]{3,2,1,0:T(8,128)(2,1)S(1)}, u32[]{:S(2)}, u32[]{:S(2)}) collective-permute-start(bf16[2,2,256,256]{3,2,1,0:T(8,128)(2,1)} %refs_4_.1), channel_id=1, source_target_pairs={{0,2},{1,3},{2,0},{3,1},{4,6},{5,7},{6,4},{7,5},{8,10},{9,11},{10,... | collective-permute-start | bytes 1572872 | tf_op jit(solution)/shard_map/ppermute | solution.py:16
  6.3 1.4 %collective-permute-start.3 = (s32[2,2]{1,0:T(2,128)}, s32[2,2]{1,0:T(2,128)S(1)}, u32[]{:S(2)}, u32[]{:S(2)}) collective-permute-start(s32[2,2]{1,0:T(2,128)} %refs_3_.1), channel_id=1, source_target_pairs={{0,4},{4,0},{8,12},{12,8},{1,5},{5,1},{9,13},{13,9},{2,6},{6,2},{1... | collective-permute-start | bytes 56 | tf_op jit(solution)/shard_map/ppermute | solution.py:16
  7.7 0.6 %copy-start.5 = (s32[2,2]{1,0:T(2,128)}, s32[2,2]{1,0:T(2,128)S(1)}, u32[]{:S(2)}) copy-start(s32[2,2]{1,0:T(2,128)S(1)} %collective-permute-done.3.token) | copy-start | bytes 52
  10.4 33.5 %copy-start = (bf16[2,2,256,256]{3,2,1,0:T(8,128)(2,1)S(1)}, bf16[2,2,256,256]{3,2,1,0:T(8,128)(2,1)}, u32[]{:S(2)}) copy-start(bf16[2,2,256,256]{3,2,1,0:T(8,128)(2,1)} %get-tuple-element.18.refs_4_) | copy-start | bytes 1572868
  10.4 19.1 %collective-permute-start.4 = (bf16[2,2,256,256]{3,2,1,0:T(8,128)(2,1)}, bf16[2,2,256,256]{3,2,1,0:T(8,128)(2,1)S(1)}, u32[]{:S(2)}, u32[]{:S(2)}) collective-permute-start(bf16[2,2,256,256]{3,2,1,0:T(8,128)(2,1)} %get-tuple-element.14.refs_0_), channel_id=1, source_target_pairs={{0,8},{4,12},{8,0},{12,4},{1,9},{5,13},{9,1},{13,5},{2,10},{6,14},... | collective-permute-start | bytes 1572872 | tf_op jit(solution)/shard_map/ppermute | solution.py:16
  11.9 18.3 %collective-permute-start.5 = (bf16[2,2,256,256]{3,2,1,0:T(8,128)(2,1)}, bf16[2,2,256,256]{3,2,1,0:T(8,128)(2,1)S(1)}, u32[]{:S(2)}, u32[]{:S(2)}) collective-permute-start(bf16[2,2,256,256]{3,2,1,0:T(8,128)(2,1)} %get-tuple-element.14.refs_0_), channel_id=1, source_target_pairs={{0,4},{4,0},{8,12},{12,8},{1,5},{5,1},{9,13},{13,9},{2,6},{6,2},{1... | collective-permute-start | bytes 1572872 | tf_op jit(solution)/shard_map/ppermute | solution.py:16
  29.5 2.0 %collective-permute-start.6 = (bf16[2,2,256,256]{3,2,1,0:T(8,128)(2,1)S(1)}, bf16[2,2,256,256]{3,2,1,0:T(8,128)(2,1)}, u32[]{:S(2)}, u32[]{:S(2)}) collective-permute-start(bf16[2,2,256,256]{3,2,1,0:T(8,128)(2,1)S(1)} %collective-permute-done.4.refs_1_), channel_id=1, source_target_pairs={{0,4},{4,0},{8,12},{12,8},{1,5},{5,1},{9,13},{13,9},{2,6},{6,2},{1... | collective-permute-start | bytes 1572872 | tf_op jit(solution)/shard_map/ppermute | solution.py:16
  29.5 14.3 %collective-permute-start.2 = (bf16[2,2,256,256]{3,2,1,0:T(8,128)(2,1)S(1)}, bf16[2,2,256,256]{3,2,1,0:T(8,128)(2,1)S(1)}, u32[]{:S(2)}, u32[]{:S(2)}) collective-permute-start(bf16[2,2,256,256]{3,2,1,0:T(8,128)(2,1)S(1)} %collective-permute-done.1.refs_6_), channel_id=1, source_target_pairs={{0,1},{1,0},{2,3},{3,2},{4,5},{5,4},{6,7},{7,6},{8,9},{9,8},{10,11... | collective-permute-start | bytes 1572872 | tf_op jit(solution)/shard_map/ppermute | solution.py:16
  31.6 1.0 %copy-start.1 = (bf16[2,2,256,256]{3,2,1,0:T(8,128)(2,1)S(1)}, bf16[2,2,256,256]{3,2,1,0:T(8,128)(2,1)}, u32[]{:S(2)}) copy-start(bf16[2,2,256,256]{3,2,1,0:T(8,128)(2,1)} %refs_4_.1) | copy-start | bytes 1572868
  32.6 1.0 %copy-start.2 = (bf16[2,2,256,256]{3,2,1,0:T(8,128)(2,1)S(1)}, bf16[2,2,256,256]{3,2,1,0:T(8,128)(2,1)}, u32[]{:S(2)}) copy-start(bf16[2,2,256,256]{3,2,1,0:T(8,128)(2,1)} %get-tuple-element.14.refs_0_) | copy-start | bytes 1572868
  43.9 7.5 %copy-start.3 = (f32[2,64,256]{2,1,0:T(8,128)S(1)}, f32[2,64,256]{2,1,0:T(8,128)}, u32[]{:S(2)}) copy-start(f32[2,64,256]{2,1,0:T(8,128)} %refs_0_.1) | copy-start | bytes 393220
  45.8 1.9 %collective-permute-start.7 = (bf16[2,64,256]{2,1,0:T(8,128)(2,1)S(1)}, bf16[2,64,256]{2,1,0:T(8,128)(2,1)S(1)}, u32[]{:S(2)}, u32[]{:S(2)}) collective-permute-start(bf16[2,64,256]{2,1,0:T(8,128)(2,1)S(1)} %get-tuple-element.21), channel_id=1, source_target_pairs={{0,4},{4,0},{8,12},{12,8},{1,5},{5,1},{9,13},{13,9},{2,6},{6,2},{1... | collective-permute-start | bytes 196616 | tf_op jit(solution)/shard_map/ppermute | solution.py:16
  45.8 4.5 %collective-permute-start.8 = (bf16[2,64,256]{2,1,0:T(8,128)(2,1)S(1)}, bf16[2,64,256]{2,1,0:T(8,128)(2,1)S(1)}, u32[]{:S(2)}, u32[]{:S(2)}) collective-permute-start(bf16[2,64,256]{2,1,0:T(8,128)(2,1)S(1)} %get-tuple-element.22), channel_id=1, source_target_pairs={{0,8},{4,12},{8,0},{12,4},{1,9},{5,13},{9,1},{13,5},{2,10},{6,14},... | collective-permute-start | bytes 196616 | tf_op jit(solution)/shard_map/ppermute | solution.py:16
  47.3 4.1 %collective-permute-start.9 = (bf16[2,64,256]{2,1,0:T(8,128)(2,1)S(1)}, bf16[2,64,256]{2,1,0:T(8,128)(2,1)S(1)}, u32[]{:S(2)}, u32[]{:S(2)}) collective-permute-start(bf16[2,64,256]{2,1,0:T(8,128)(2,1)S(1)} %get-tuple-element.23), channel_id=1, source_target_pairs={{0,12},{4,8},{8,4},{12,0},{1,13},{5,9},{9,5},{13,1},{2,14},{6,10},... | collective-permute-start | bytes 196616 | tf_op jit(solution)/shard_map/ppermute | solution.py:16

commit v3 on v2

v3 whole, which is shorter than its diff:
```python
import functools

import jax
import jax.numpy as jnp
from jax import lax
from jax.experimental import pallas as pl
from jax.experimental.pallas import tpu as pltpu
from jax.sharding import PartitionSpec as P

F32, BF16 = jnp.float32, jnp.bfloat16
VMEM = pl.BlockSpec(memory_space=pltpu.VMEM)
SMEM = pl.BlockSpec(memory_space=pltpu.SMEM)
ANY = pl.BlockSpec(memory_space=pl.ANY)


def exchange(array, axis, n, distance):
    return lax.ppermute(array, axis, [(i, i ^ distance) for i in range(n)])


def gather(own, axis, n, distances):
    held = [(own, 0)]
    for distance in distances:
        held += [(exchange(a, axis, n, distance), d ^ distance) for a, d in held]
    return held


def column_gather(own, top, bottom, n):
    far = [1 << p for p in reversed(range(1, n.bit_length() - 1))]
    half = top.shape[0]
    beside = exchange(own, "col", n, 1)
    upper = gather(top, "col", n, far)[1:]
    lower = gather(bottom, "col", n, far)[1:]
    arrays, beside = lax.optimization_barrier(([a for a, _ in lower], beside))
    lower = [(a, d) for a, (_, d) in zip(arrays, lower)]
    got = [(0, top, 0), (half, bottom, 0), (0, beside, 1)]
    for start, part in ((0, upper), (half, lower)):
        got += [(start, a, d) for a, d in part]
    upper = [(exchange(a, "col", n, 1), d ^ 1) for a, d in upper]
    afar, arrays = lax.optimization_barrier(([a for a, _ in lower], [a for a, _ in upper]))
    lower = [(a, d) for a, (_, d) in zip(afar, lower)]
    upper = [(a, d) for a, (_, d) in zip(arrays, upper)]
    lower = [(exchange(a, "col", n, 1), d ^ 1) for a, d in lower]
    for start, part in ((0, upper), (half, lower)):
        got += [(start, a, d) for a, d in part]
    return got


def keep(info, cols, i, k):
    return info[2 + i * cols + k].astype(F32)


def mask_kernel(info, token, lower, *masked):
    cols = lower.shape[1]
    for j, out in enumerate(masked):
        for k in range(cols):
            out[k] = (lower[j, k].astype(F32) * keep(info, cols, j, k)).astype(BF16)


def add_products(place, start, block, factor, total):
    rows, inner = block.shape[:2]
    for i in range(rows):
        for k in range(total.shape[1]):
            partial = total[start + i, k]
            for j in range(inner):
                partial += jnp.dot(block[i, j], factor[place, j, k], preferred_element_type=F32)
            total[start + i, k] = partial


def place_kernel(sources, parts, info, *refs):
    n_pieces = len(sources)
    pieces, blocks, (factor, turned, total) = refs[:n_pieces], refs[n_pieces:-3], refs[-3:]
    for (j, d), piece in zip(sources, pieces):
        factor[jnp.bitwise_xor(info[0], d), j] = piece[...]
    for (j, d), piece in zip(sources, pieces):
        if d == 0:
            for k in range(piece.shape[0]):
                turned[j, k] = piece[k].astype(F32).T.astype(BF16)
    total[...] = jnp.zeros_like(total)
    for (start, d), block in zip(parts, blocks):
        add_products(jnp.bitwise_xor(info[1], d), start, block, factor, total)


def early_kernel(parts, info, *refs):
    blocks, (factor, total_in, turned, value, total, update, both) = refs[:-7], refs[-7:]
    rows, cols = total_in.shape[:2]
    half = rows // 2
    both[...] = total_in[...]
    for (start, d), block in zip(parts, blocks):
        add_products(jnp.bitwise_xor(info[1], d), start, block, factor, both)
    for i in range(half, rows):
        total[i - half] = both[i]
    for k in range(cols):
        share = jnp.zeros(update.shape[1:], F32)
        for i in range(half):
            value[i, k] = (-(keep(info, cols, i, k) * both[i, k])).astype(BF16)
            share += jnp.dot(turned[i, k], value[i, k], preferred_element_type=F32)
        update[k] = share


def finish_kernel(n_row, distance, info, block, factor, total, update, turned, value, *refs):
    sends, whole = refs[:-1], refs[-1]
    half, cols, b = total.shape[:3]
    place = jnp.bitwise_xor(info[1], distance)
    piece = b // n_row
    for k in range(cols):
        share = update[k]
        for i in range(half):
            partial = total[i, k]
            for j in range(block.shape[1]):
                partial += jnp.dot(block[i, j], factor[place, j, k], preferred_element_type=F32)
            value[i, k] = (-(keep(info, cols, half + i, k) * partial)).astype(BF16)
            share += jnp.dot(turned[half + i, k], value[i, k], preferred_element_type=F32)
        whole[k] = share
        for d in range(n_row):
            there = pl.multiple_of(jnp.bitwise_xor(info[0], d) * piece, 16)
            sends[d][k] = whole[k, pl.ds(there, piece), :].astype(sends[d].dtype)


def join_kernel(top, bottom, out, sems):
    half = top.shape[0]
    copies = [
        pltpu.make_async_copy(top, out.at[pl.ds(0, half)], sems.at[0]),
        pltpu.make_async_copy(bottom, out.at[pl.ds(half, half)], sems.at[1]),
    ]
    for copy in copies:
        copy.start()
    for copy in copies:
        copy.wait()


def last_kernel(*refs):
    diag, own, got, out = refs[0], refs[1], refs[2:-1], refs[-1]
    update = own[...]
    for part in got:
        update += part[...].astype(F32)
    out[...] = diag[...] - update


def call(kernel, out_shape, in_specs, mib, scratch=(), out_specs=None, aliases={}):
    return pl.pallas_call(
        kernel,
        out_shape=out_shape,
        in_specs=in_specs,
        out_specs=jax.tree.map(lambda _: VMEM, out_shape) if out_specs is None else out_specs,
        scratch_shapes=scratch,
        input_output_aliases=aliases,
        compiler_params=pltpu.CompilerParams(vmem_limit_bytes=mib << 20),
        cost_estimate=pl.CostEstimate(flops=0, bytes_accessed=0, transcendentals=0),
    )


def solution(mesh):
    n_row, n_col = mesh.shape["row"], mesh.shape["col"]

    def on_device(inverse_block, lower_block, pattern, diag_inverse):
        row, col = lax.axis_index("row"), lax.axis_index("col")
        rows, cols, b = lower_block.shape[:3]
        shape = jax.ShapeDtypeStruct

        half = rows // 2
        info = jnp.concatenate([jnp.stack([row, col]).astype(jnp.int32), pattern.reshape(-1)])
        blocks = column_gather(inverse_block, inverse_block[:half], inverse_block[half:], n_col)
        token = exchange(pattern, "row", n_row, 1)

        masked = call(mask_kernel, [shape((cols, b, b), BF16)] * rows, [SMEM, SMEM, VMEM], 4)(info, token, lower_block)
        far = [1 << p for p in range(1, n_row.bit_length() - 1)]
        pieces = [(m, (j, d)) for j, own in enumerate(masked) for m, d in gather(own, "row", n_row, far + [1])]
        near, others, last = [x for x in blocks if x[2] == 0], [x for x in blocks[:-1] if x[2]], blocks[-1]

        kept, ends = shape(lower_block.shape, BF16), shape((half, cols, b, b), F32)
        sums, value = shape((rows, cols, b, b), F32), shape((half, cols, b, b), BF16)
        factor, turned, total = call(
            functools.partial(place_kernel, [x for _, x in pieces], [(start, d) for start, _, d in near]),
            [shape((n_row,) + kept.shape, BF16), kept, sums],
            [SMEM] + [VMEM] * (len(pieces) + len(near)),
            20,
        )(info, *[m for m, _ in pieces], *[x for _, x, _ in near])
        top, total, update = call(
            functools.partial(early_kernel, [(start, d) for start, _, d in others]),
            [value, ends, shape((cols, b, b), F32)],
            [SMEM] + [VMEM] * (len(others) + 3),
            20,
            [pltpu.VMEM(sums.shape, F32)],
        )(info, *[x for _, x, _ in others], factor, total, turned)
        part = shape((cols, b // n_row, b), BF16)
        bottom, own, *sends = call(
            functools.partial(finish_kernel, n_row, last[2]),
            [value, shape(part.shape, F32)] + [part] * (n_row - 1),
            [SMEM] + [VMEM] * 5,
            8,
            [pltpu.VMEM((cols, b, b), F32)],
        )(info, last[1], factor, total, update, turned)
        got = [exchange(s, "row", n_row, d) for d, s in enumerate(sends, 1)]
        lower_out = call(
            join_kernel,
            shape(inverse_block.shape[:1] + lower_block.shape[1:], BF16),
            [VMEM] * 2,
            2,
            [pltpu.SemaphoreType.DMA((2,))],
            ANY,
        )(top, bottom)
        got, lower_out = lax.optimization_barrier((got, lower_out))
        diag_out = call(last_kernel, shape(diag_inverse.shape, F32), [VMEM] * (2 + len(got)), 4)(diag_inverse, own, *got)
        return lower_out, diag_out

    spec, diag = P(("pole", "row"), "col", None, None), P(("pole", "col"), "row", None)
    return jax.shard_map(
        on_device,
        mesh=mesh,
        in_specs=(spec, spec, P("row", "col"), diag),
        out_specs=(spec, diag),
        check_vma=False,
    )
```

time: 52.4 us -> 48 us (0.916)
  waiting for transfers between devices: 32.1 us -> 21.5 us
  starting transfers between devices: 9.47 us -> 16.5 us
  Pallas kernels: 6.96 us -> 6.21 us
    ppermute x10 -> x15, waiting for transfers between devices: 32.1 us -> 21.5 us  [exchange(): return lax.ppermute(array, axis, [(i, i ^ distance) for i in range(n)])]
    ppermute x10 -> x15, starting transfers between devices: 9.47 us -> 16.5 us  [exchange(): return lax.ppermute(array, axis, [(i, i ^ distance) for i in range(n)])]
    unnamed x12 -> x4, local copies, waits for them, and re-layouts: 2.66 us -> 1.05 us
    slice x0 -> x1, local copies, waits for them, and re-layouts: none -> 1.06 us  [on_device(): inverse_block[:half]]
    reshape x0 -> x1, local copies, waits for them, and re-layouts: none -> 0.76 us  [on_device(): pattern.reshape(-1)]
    pallas_call x3 -> x5, Pallas kernels: 6.26 us -> 5.51 us  [the longest x1 1.59 us: on_device(): call(functools.partial(early_kernel, [(start, d) for start, _, d in other...]
  transfers between devices with their start and end apart: 10 -> 15, of which waited for: 7 -> 7; matrix products, arithmetic and copies ran while one was open for 0% -> 4% of each run, Pallas kernels for 8% -> 9%
where the time goes in v3:
time: 48 us; the launch traced here: 47.8 us
  waiting for transfers between devices  21.5 us (45%)
  starting transfers between devices  16.5 us (34%)
  Pallas kernels  6.21 us (13%)
  local copies, waits for them, and re-layouts  2.87 us (6%)
  between operations  0.71 us (1%)
    ppermute x15, waiting for transfers between devices, exchange(): return lax.ppermute(array, axis, [(i, i ^ distance) for i in range(n)])  21.5 us
    ppermute x15, starting transfers between devices, exchange(): return lax.ppermute(array, axis, [(i, i ^ distance) for i in range(n)])  16.5 us
    pallas_call x1, Pallas kernels, on_device(): call(functools.partial(early_kernel, [(start, d) for start, _, d in other...  1.59 us
    pallas_call x1, Pallas kernels, on_device(): call(functools.partial(finish_kernel, n_row, last[2]), [value, shape(part...  1.35 us
    pallas_call x1, Pallas kernels, on_device(): call(functools.partial(place_kernel, [x for _, x in pieces], [(start, d)...  1.13 us
    slice x1, local copies, waits for them, and re-layouts, on_device(): inverse_block[:half]  1.06 us
    unnamed x4, local copies, waits for them, and re-layouts  1.05 us
  transfers between devices with their start and end apart: 15, of which 7 were waited for; matrix products, arithmetic and copies ran while one was open for 4% of the time, Pallas kernels for 9%

profile of v3, /device:TPU:0, one launch (start us, length us, event | category | flops | bytes accessed | tf_op | source)
XLA Modules:
  0.0 47.8 jit_solution(6325591410789003776)
XLA Ops:
  0.6 3.1 %collective-permute-start.1 = (bf16[2,2,256,256]{3,2,1,0:T(8,128)(2,1)}, bf16[2,2,256,256]{3,2,1,0:T(8,128)(2,1)S(1)}, u32[]{:S(2)}, u32[]{:S(2)}) collective-permute-start(bf16[2,2,256,256]{3,2,1,0:T(8,128)(2,1)} %param.4), channel_id=1, source_target_pairs={{0,1},{1,0},{2,3},{3,2},{4,5},{5,4},{6,7},{7,6},{8,9},{9,8},{10,11... | collective-permute-start | bytes 1572872 | tf_op jit(solution)/shard_map/ppermute | solution.py:17
  3.7 1.1 %fusion = (bf16[1,2,256,256]{3,2,1,0:T(8,128)(2,1)S(1)}, bf16[1,2,256,256]{3,2,1,0:T(8,128)(2,1)S(1)}) fusion(bf16[2,2,256,256]{3,2,1,0:T(8,128)(2,1)} %param.4), kind=kLoop, calls=%fused_computation.1 | loop fusion | bytes 1048576 | tf_op jit(solution)/shard_map/slice | solution.py:162
  4.8 2.7 %collective-permute-start.2 = (bf16[1,2,256,256]{3,2,1,0:T(8,128)(2,1)S(1)}, bf16[1,2,256,256]{3,2,1,0:T(8,128)(2,1)S(1)}, u32[]{:S(2)}, u32[]{:S(2)}) collective-permute-start(bf16[1,2,256,256]{3,2,1,0:T(8,128)(2,1)S(1)} %get-tuple-element.44.refs_8_), channel_id=1, source_target_pairs={{0,2},{1,3},{2,0},{3,1},{4,6},{5,7},{6,4},{7,5},{8,10},{9,11},{10,... | collective-permute-start | bytes 786440 | tf_op jit(solution)/shard_map/ppermute | solution.py:17
  7.4 0.3 collective-permute-start
  7.8 0.8 %reshape.7 = s32[4]{0:T(128)S(1)} reshape(s32[2,2]{1,0:T(2,128)} %param.6) | data formatting | bytes 32 | tf_op jit(solution)/shard_map/reshape | solution.py:161
  8.5 0.1 pad_add_fusion.info
  8.6 0.2 collective-permute-done.5.token
  8.8 1.0 %copy-done = bf16[2,2,256,256]{3,2,1,0:T(8,128)(2,1)S(1)} copy-done((bf16[2,2,256,256]{3,2,1,0:T(8,128)(2,1)S(1)}, bf16[2,2,256,256]{3,2,1,0:T(8,128)(2,1)}, u32[]{:S(2)}) %copy-start) | copy-done | bytes 524312
  9.8 0.6 %shard_map.59 = (bf16[2,256,256]{2,1,0:T(8,128)(2,1)S(1)}, bf16[2,256,256]{2,1,0:T(8,128)(2,1)S(1)}) custom-call(s32[6]{0:T(128)S(1)} %pad_add_fusion.info, s32[2,2]{1,0:T(2,128)S(1)} %collective-permute-done.5.token, bf16[2,2,256,256]{3,2,1,0:T(8,128)(2,1)S(1)} %copy-done), custom_call_target="tpu_custom_call" | custom-call | tf_op jit(solution)/shard_map/pallas_call | solution.py:165
  10.5 1.6 %collective-permute-start.9 = (bf16[2,256,256]{2,1,0:T(8,128)(2,1)S(1)}, bf16[2,256,256]{2,1,0:T(8,128)(2,1)S(1)}, u32[]{:S(2)}, u32[]{:S(2)}) collective-permute-start(bf16[2,256,256]{2,1,0:T(8,128)(2,1)S(1)} %get-tuple-element.26.refs_4_), channel_id=1, source_target_pairs={{0,8},{4,12},{8,0},{12,4},{1,9},{5,13},{9,1},{13,5},{2,10},{6,14},... | collective-permute-start | bytes 786440 | tf_op jit(solution)/shard_map/ppermute | solution.py:17
  12.0 0.5 %collective-permute-start.6 = (bf16[2,256,256]{2,1,0:T(8,128)(2,1)S(1)}, bf16[2,256,256]{2,1,0:T(8,128)(2,1)S(1)}, u32[]{:S(2)}, u32[]{:S(2)}) collective-permute-start(bf16[2,256,256]{2,1,0:T(8,128)(2,1)S(1)} %get-tuple-element.25.refs_0_), channel_id=1, source_target_pairs={{0,8},{4,12},{8,0},{12,4},{1,9},{5,13},{9,1},{13,5},{2,10},{6,14},... | collective-permute-start | bytes 786440 | tf_op jit(solution)/shard_map/ppermute | solution.py:17
  12.6 9.3 %collective-permute-done.2.refs_1_ = bf16[1,2,256,256]{3,2,1,0:T(8,128)(2,1)S(1)} collective-permute-done((bf16[1,2,256,256]{3,2,1,0:T(8,128)(2,1)S(1)}, bf16[1,2,256,256]{3,2,1,0:T(8,128)(2,1)S(1)}, u32[]{:S(2)}, u32[]{:S(2)}) %collective-permute-start.2) | collective-permute-done | bytes 262176 | tf_op jit(solution)/shard_map/ppermute | solution.py:17
  21.9 3.6 %collective-permute-start.3 = (bf16[1,2,256,256]{3,2,1,0:T(8,128)(2,1)S(1)}, bf16[1,2,256,256]{3,2,1,0:T(8,128)(2,1)S(1)}, u32[]{:S(2)}, u32[]{:S(2)}) collective-permute-start(bf16[1,2,256,256]{3,2,1,0:T(8,128)(2,1)S(1)} %collective-permute-done.2.refs_1_), channel_id=1, source_target_pairs={{0,1},{1,0},{2,3},{3,2},{4,5},{5,4},{6,7},{7,6},{8,9},{9,8},{10,11... | collective-permute-start | bytes 786440 | tf_op jit(solution)/shard_map/ppermute | solution.py:17
  25.5 4.9 %collective-permute-done.refs_2_ = bf16[1,2,256,256]{3,2,1,0:T(8,128)(2,1)S(1)} collective-permute-done((bf16[1,2,256,256]{3,2,1,0:T(8,128)(2,1)S(1)}, bf16[1,2,256,256]{3,2,1,0:T(8,128)(2,1)S(1)}, u32[]{:S(2)}, u32[]{:S(2)}) %collective-permute-start) | collective-permute-done | bytes 262176 | tf_op jit(solution)/shard_map/ppermute | solution.py:17
  30.4 0.0 collective-permute-start.10
  30.4 0.0 collective-permute-done.9.refs_5_
  30.4 0.5 %collective-permute-start.7 = (bf16[2,256,256]{2,1,0:T(8,128)(2,1)S(1)}, bf16[2,256,256]{2,1,0:T(8,128)(2,1)S(1)}, u32[]{:S(2)}, u32[]{:S(2)}) collective-permute-start(bf16[2,256,256]{2,1,0:T(8,128)(2,1)S(1)} %get-tuple-element.25.refs_0_), channel_id=1, source_target_pairs={{0,4},{4,0},{8,12},{12,8},{1,5},{5,1},{9,13},{13,9},{2,6},{6,2},{1... | collective-permute-start | bytes 786440 | tf_op jit(solution)/shard_map/ppermute | solution.py:17
  30.9 0.1 collective-permute-start.11
  30.9 0.4 collective-permute-start.8
  31.4 1.3 %collective-permute-done.3.refs_3_ = bf16[1,2,256,256]{3,2,1,0:T(8,128)(2,1)S(1)} collective-permute-done((bf16[1,2,256,256]{3,2,1,0:T(8,128)(2,1)S(1)}, bf16[1,2,256,256]{3,2,1,0:T(8,128)(2,1)S(1)}, u32[]{:S(2)}, u32[]{:S(2)}) %collective-permute-start.3) | collective-permute-done | bytes 262176 | tf_op jit(solution)/shard_map/ppermute | solution.py:17
  32.7 1.8 %collective-permute-start.4 = (bf16[1,2,256,256]{3,2,1,0:T(8,128)(2,1)S(1)}, bf16[1,2,256,256]{3,2,1,0:T(8,128)(2,1)S(1)}, u32[]{:S(2)}, u32[]{:S(2)}) collective-permute-start(bf16[1,2,256,256]{3,2,1,0:T(8,128)(2,1)S(1)} %collective-permute-done.refs_2_), channel_id=1, source_target_pairs={{0,1},{1,0},{2,3},{3,2},{4,5},{5,4},{6,7},{7,6},{8,9},{9,8},{10,11... | collective-permute-start | bytes 786440 | tf_op jit(solution)/shard_map/ppermute | solution.py:17
  34.5 1.1 %shard_map.60 = (bf16[4,2,2,256,256]{4,3,2,1,0:T(8,128)(2,1)S(1)}, bf16[2,2,256,256]{3,2,1,0:T(8,128)(2,1)S(1)}, f32[2,2,256,256]{3,2,1,0:T(8,128)S(1)}) custom-call(s32[6]{0:T(128)S(1)} %pad_add_fusion.info, bf16[2,256,256]{2,1,0:T(8,128)(2,1)S(1)} %get-tuple-element.25.refs_0_, bf16[2,256,256]{2,1,0:T(8,128)(2,1)S(1)} %collective-permute-done.6.refs_1_, ...), custom_call_target="tpu_custom_call" | custom-call | tf_op jit(solution)/shard_map/pallas_call | solution.py:172
  35.6 1.6 %shard_map.61 = (bf16[1,2,256,256]{3,2,1,0:T(8,128)(2,1)S(1)}, f32[1,2,256,256]{3,2,1,0:T(8,128)S(1)}, f32[2,256,256]{2,1,0:T(8,128)S(1)}) custom-call(s32[6]{0:T(128)S(1)} %pad_add_fusion.info, bf16[2,2,256,256]{3,2,1,0:T(8,128)(2,1)S(1)} %collective-permute-done.1.refs_0_, bf16[1,2,256,256]{3,2,1,0:T(8,128)(2,1)S(1)} %collective-permute-done.2.refs_1_, ...), custom_call_target="tpu_custom_call" | custom-call | tf_op jit(solution)/shard_map/pallas_call | solution.py:178
  37.2 2.8 %collective-permute-done.4.block = bf16[1,2,256,256]{3,2,1,0:T(8,128)(2,1)S(1)} collective-permute-done((bf16[1,2,256,256]{3,2,1,0:T(8,128)(2,1)S(1)}, bf16[1,2,256,256]{3,2,1,0:T(8,128)(2,1)S(1)}, u32[]{:S(2)}, u32[]{:S(2)}) %collective-permute-start.4) | collective-permute-done | bytes 262176 | tf_op jit(solution)/shard_map/ppermute | solution.py:17
  40.0 1.4 %shard_map.62 = (bf16[1,2,256,256]{3,2,1,0:T(8,128)(2,1)S(1)}, f32[2,64,256]{2,1,0:T(8,128)S(1)}, bf16[2,64,256]{2,1,0:T(8,128)(2,1)S(1)}, bf16[2,64,256]{2,1,0:T(8,128)(2,1)S(1)}, bf16[2,64,256]{2,1,0:T(8,128)(2,1)S(1)}) custom-call(s32[6]{0:T(128)S(1)} %pad_add_fusion.info, bf16[1,2,256,256]{3,2,1,0:T(8,128)(2,1)S(1)} %collective-permute-done.4.block, ...), custom_call_target="tpu_custom_call" | custom-call | tf_op jit(solution)/shard_map/pallas_call | solution.py:186
  41.4 0.1 collective-permute-start.12
  41.4 1.6 %collective-permute-start.13 = (bf16[2,64,256]{2,1,0:T(8,128)(2,1)S(1)}, bf16[2,64,256]{2,1,0:T(8,128)(2,1)S(1)}, u32[]{:S(2)}, u32[]{:S(2)}) collective-permute-start(bf16[2,64,256]{2,1,0:T(8,128)(2,1)S(1)} %get-tuple-element.35), channel_id=1, source_target_pairs={{0,8},{4,12},{8,0},{12,4},{1,9},{5,13},{9,1},{13,5},{2,10},{6,14},... | collective-permute-start | bytes 196616 | tf_op jit(solution)/shard_map/ppermute | solution.py:17
  43.0 0.3 collective-permute-start.14
  43.3 0.8 %shard_map.63 = bf16[2,2,256,256]{3,2,1,0:T(8,128)(2,1)} custom-call(bf16[1,2,256,256]{3,2,1,0:T(8,128)(2,1)S(1)} %get-tuple-element.37.top, bf16[1,2,256,256]{3,2,1,0:T(8,128)(2,1)S(1)} %get-tuple-element.38.bottom), custom_call_target="tpu_custom_call" | custom-call | tf_op jit(solution)/shard_map/pallas_call | solution.py:194
  44.1 1.8 %collective-permute-done.13.refs_3_ = bf16[2,64,256]{2,1,0:T(8,128)(2,1)S(1)} collective-permute-done((bf16[2,64,256]{2,1,0:T(8,128)(2,1)S(1)}, bf16[2,64,256]{2,1,0:T(8,128)(2,1)S(1)}, u32[]{:S(2)}, u32[]{:S(2)}) %collective-permute-start.13) | collective-permute-done | bytes 65568 | tf_op jit(solution)/shard_map/ppermute | solution.py:17
  46.0 1.1 %collective-permute-done.14.refs_4_ = bf16[2,64,256]{2,1,0:T(8,128)(2,1)S(1)} collective-permute-done((bf16[2,64,256]{2,1,0:T(8,128)(2,1)S(1)}, bf16[2,64,256]{2,1,0:T(8,128)(2,1)S(1)}, u32[]{:S(2)}, u32[]{:S(2)}) %collective-permute-start.14) | collective-permute-done | bytes 65568 | tf_op jit(solution)/shard_map/ppermute | solution.py:17
  47.1 0.7 %shard_map.64 = f32[2,64,256]{2,1,0:T(8,128)} custom-call(f32[2,64,256]{2,1,0:T(8,128)S(1)} %copy-done.1, f32[2,64,256]{2,1,0:T(8,128)S(1)} %get-tuple-element.40.refs_1_, bf16[2,64,256]{2,1,0:T(8,128)(2,1)S(1)} %collective-permute-done.12.refs_2_, bf16[2,64,256]{2,1,0:T(8,128)(2,1)S(1)} %collective-permute-done.13.refs_3_, ...), custom_call_target="tpu_custom_call" | custom-call | tf_op jit(solution)/shard_map/pallas_call | solution.py:203
  (11 shorter events, 0.0 us)
Async XLA Ops:
  0.6 30.3 %collective-permute-start.1 = (bf16[2,2,256,256]{3,2,1,0:T(8,128)(2,1)}, bf16[2,2,256,256]{3,2,1,0:T(8,128)(2,1)S(1)}, u32[]{:S(2)}, u32[]{:S(2)}) collective-permute-start(bf16[2,2,256,256]{3,2,1,0:T(8,128)(2,1)} %param.4), channel_id=1, source_target_pairs={{0,1},{1,0},{2,3},{3,2},{4,5},{5,4},{6,7},{7,6},{8,9},{9,8},{10,11... | collective-permute-start | bytes 1572872 | tf_op jit(solution)/shard_map/ppermute | solution.py:17
  4.8 17.1 %collective-permute-start.2 = (bf16[1,2,256,256]{3,2,1,0:T(8,128)(2,1)S(1)}, bf16[1,2,256,256]{3,2,1,0:T(8,128)(2,1)S(1)}, u32[]{:S(2)}, u32[]{:S(2)}) collective-permute-start(bf16[1,2,256,256]{3,2,1,0:T(8,128)(2,1)S(1)} %get-tuple-element.44.refs_8_), channel_id=1, source_target_pairs={{0,2},{1,3},{2,0},{3,1},{4,6},{5,7},{6,4},{7,5},{8,10},{9,11},{10,... | collective-permute-start | bytes 786440 | tf_op jit(solution)/shard_map/ppermute | solution.py:17
  7.4 1.4 %collective-permute-start.5 = (s32[2,2]{1,0:T(2,128)}, s32[2,2]{1,0:T(2,128)S(1)}, u32[]{:S(2)}, u32[]{:S(2)}) collective-permute-start(s32[2,2]{1,0:T(2,128)} %param.6), channel_id=1, source_target_pairs={{0,4},{4,0},{8,12},{12,8},{1,5},{5,1},{9,13},{13,9},{2,6},{6,2},{1... | collective-permute-start | bytes 56 | tf_op jit(solution)/shard_map/ppermute | solution.py:17
  7.4 22.9 %collective-permute-start = (bf16[1,2,256,256]{3,2,1,0:T(8,128)(2,1)S(1)}, bf16[1,2,256,256]{3,2,1,0:T(8,128)(2,1)S(1)}, u32[]{:S(2)}, u32[]{:S(2)}) collective-permute-start(bf16[1,2,256,256]{3,2,1,0:T(8,128)(2,1)S(1)} %get-tuple-element.45.refs_9_), channel_id=1, source_target_pairs={{0,2},{1,3},{2,0},{3,1},{4,6},{5,7},{6,4},{7,5},{8,10},{9,11},{10,... | collective-permute-start | bytes 786440 | tf_op jit(solution)/shard_map/ppermute | solution.py:17
  8.8 1.0 %copy-start = (bf16[2,2,256,256]{3,2,1,0:T(8,128)(2,1)S(1)}, bf16[2,2,256,256]{3,2,1,0:T(8,128)(2,1)}, u32[]{:S(2)}) copy-start(bf16[2,2,256,256]{3,2,1,0:T(8,128)(2,1)} %lower.1) | copy-start | bytes 1572868
  10.5 19.9 %collective-permute-start.9 = (bf16[2,256,256]{2,1,0:T(8,128)(2,1)S(1)}, bf16[2,256,256]{2,1,0:T(8,128)(2,1)S(1)}, u32[]{:S(2)}, u32[]{:S(2)}) collective-permute-start(bf16[2,256,256]{2,1,0:T(8,128)(2,1)S(1)} %get-tuple-element.26.refs_4_), channel_id=1, source_target_pairs={{0,8},{4,12},{8,0},{12,4},{1,9},{5,13},{9,1},{13,5},{2,10},{6,14},... | collective-permute-start | bytes 786440 | tf_op jit(solution)/shard_map/ppermute | solution.py:17
  12.0 18.8 %collective-permute-start.6 = (bf16[2,256,256]{2,1,0:T(8,128)(2,1)S(1)}, bf16[2,256,256]{2,1,0:T(8,128)(2,1)S(1)}, u32[]{:S(2)}, u32[]{:S(2)}) collective-permute-start(bf16[2,256,256]{2,1,0:T(8,128)(2,1)S(1)} %get-tuple-element.25.refs_0_), channel_id=1, source_target_pairs={{0,8},{4,12},{8,0},{12,4},{1,9},{5,13},{9,1},{13,5},{2,10},{6,14},... | collective-permute-start | bytes 786440 | tf_op jit(solution)/shard_map/ppermute | solution.py:17
  21.9 10.8 %collective-permute-start.3 = (bf16[1,2,256,256]{3,2,1,0:T(8,128)(2,1)S(1)}, bf16[1,2,256,256]{3,2,1,0:T(8,128)(2,1)S(1)}, u32[]{:S(2)}, u32[]{:S(2)}) collective-permute-start(bf16[1,2,256,256]{3,2,1,0:T(8,128)(2,1)S(1)} %collective-permute-done.2.refs_1_), channel_id=1, source_target_pairs={{0,1},{1,0},{2,3},{3,2},{4,5},{5,4},{6,7},{7,6},{8,9},{9,8},{10,11... | collective-permute-start | bytes 786440 | tf_op jit(solution)/shard_map/ppermute | solution.py:17
  30.4 4.1 %collective-permute-start.10 = (bf16[2,256,256]{2,1,0:T(8,128)(2,1)S(1)}, bf16[2,256,256]{2,1,0:T(8,128)(2,1)S(1)}, u32[]{:S(2)}, u32[]{:S(2)}) collective-permute-start(bf16[2,256,256]{2,1,0:T(8,128)(2,1)S(1)} %get-tuple-element.26.refs_4_), channel_id=1, source_target_pairs={{0,4},{4,0},{8,12},{12,8},{1,5},{5,1},{9,13},{13,9},{2,6},{6,2},{1... | collective-permute-start | bytes 786440 | tf_op jit(solution)/shard_map/ppermute | solution.py:17
  30.4 4.1 %collective-permute-start.7 = (bf16[2,256,256]{2,1,0:T(8,128)(2,1)S(1)}, bf16[2,256,256]{2,1,0:T(8,128)(2,1)S(1)}, u32[]{:S(2)}, u32[]{:S(2)}) collective-permute-start(bf16[2,256,256]{2,1,0:T(8,128)(2,1)S(1)} %get-tuple-element.25.refs_0_), channel_id=1, source_target_pairs={{0,4},{4,0},{8,12},{12,8},{1,5},{5,1},{9,13},{13,9},{2,6},{6,2},{1... | collective-permute-start | bytes 786440 | tf_op jit(solution)/shard_map/ppermute | solution.py:17
  30.9 3.6 %collective-permute-start.11 = (bf16[2,256,256]{2,1,0:T(8,128)(2,1)S(1)}, bf16[2,256,256]{2,1,0:T(8,128)(2,1)S(1)}, u32[]{:S(2)}, u32[]{:S(2)}) collective-permute-start(bf16[2,256,256]{2,1,0:T(8,128)(2,1)S(1)} %collective-permute-done.9.refs_5_), channel_id=1, source_target_pairs={{0,4},{4,0},{8,12},{12,8},{1,5},{5,1},{9,13},{13,9},{2,6},{6,2},{1... | collective-permute-start | bytes 786440 | tf_op jit(solution)/shard_map/ppermute | solution.py:17
  30.9 3.6 %collective-permute-start.8 = (bf16[2,256,256]{2,1,0:T(8,128)(2,1)S(1)}, bf16[2,256,256]{2,1,0:T(8,128)(2,1)S(1)}, u32[]{:S(2)}, u32[]{:S(2)}) collective-permute-start(bf16[2,256,256]{2,1,0:T(8,128)(2,1)S(1)} %collective-permute-done.6.refs_1_), channel_id=1, source_target_pairs={{0,4},{4,0},{8,12},{12,8},{1,5},{5,1},{9,13},{13,9},{2,6},{6,2},{1... | collective-permute-start | bytes 786440 | tf_op jit(solution)/shard_map/ppermute | solution.py:17
  32.7 7.3 %collective-permute-start.4 = (bf16[1,2,256,256]{3,2,1,0:T(8,128)(2,1)S(1)}, bf16[1,2,256,256]{3,2,1,0:T(8,128)(2,1)S(1)}, u32[]{:S(2)}, u32[]{:S(2)}) collective-permute-start(bf16[1,2,256,256]{3,2,1,0:T(8,128)(2,1)S(1)} %collective-permute-done.refs_2_), channel_id=1, source_target_pairs={{0,1},{1,0},{2,3},{3,2},{4,5},{5,4},{6,7},{7,6},{8,9},{9,8},{10,11... | collective-permute-start | bytes 786440 | tf_op jit(solution)/shard_map/ppermute | solution.py:17
  40.0 7.1 %copy-start.1 = (f32[2,64,256]{2,1,0:T(8,128)S(1)}, f32[2,64,256]{2,1,0:T(8,128)}, u32[]{:S(2)}) copy-start(f32[2,64,256]{2,1,0:T(8,128)} %refs_0_.1) | copy-start | bytes 393220
  41.4 2.8 %collective-permute-start.12 = (bf16[2,64,256]{2,1,0:T(8,128)(2,1)S(1)}, bf16[2,64,256]{2,1,0:T(8,128)(2,1)S(1)}, u32[]{:S(2)}, u32[]{:S(2)}) collective-permute-start(bf16[2,64,256]{2,1,0:T(8,128)(2,1)S(1)} %get-tuple-element.34), channel_id=1, source_target_pairs={{0,4},{4,0},{8,12},{12,8},{1,5},{5,1},{9,13},{13,9},{2,6},{6,2},{1... | collective-permute-start | bytes 196616 | tf_op jit(solution)/shard_map/ppermute | solution.py:17
  41.4 4.5 %collective-permute-start.13 = (bf16[2,64,256]{2,1,0:T(8,128)(2,1)S(1)}, bf16[2,64,256]{2,1,0:T(8,128)(2,1)S(1)}, u32[]{:S(2)}, u32[]{:S(2)}) collective-permute-start(bf16[2,64,256]{2,1,0:T(8,128)(2,1)S(1)} %get-tuple-element.35), channel_id=1, source_target_pairs={{0,8},{4,12},{8,0},{12,4},{1,9},{5,13},{9,1},{13,5},{2,10},{6,14},... | collective-permute-start | bytes 196616 | tf_op jit(solution)/shard_map/ppermute | solution.py:17
  43.0 4.0 %collective-permute-start.14 = (bf16[2,64,256]{2,1,0:T(8,128)(2,1)S(1)}, bf16[2,64,256]{2,1,0:T(8,128)(2,1)S(1)}, u32[]{:S(2)}, u32[]{:S(2)}) collective-permute-start(bf16[2,64,256]{2,1,0:T(8,128)(2,1)S(1)} %get-tuple-element.36), channel_id=1, source_target_pairs={{0,12},{4,8},{8,4},{12,0},{1,13},{5,9},{9,5},{13,1},{2,14},{6,10},... | collective-permute-start | bytes 196616 | tf_op jit(solution)/shard_map/ppermute | solution.py:17

commit v4 on v3

--- a/solution.py
+++ b/solution.py
@@ -66,15 +66,25 @@
             total[start + i, k] = partial
 
 
-def place_kernel(sources, parts, info, *refs):
+def place_kernel(sources, parts, n_row, distance, info, *refs):
     n_pieces = len(sources)
-    pieces, blocks, (factor, turned, total) = refs[:n_pieces], refs[n_pieces:-3], refs[-3:]
+    pieces, blocks, (factor, final, turned, total, whole) = refs[:n_pieces], refs[n_pieces:-5], refs[-5:]
+    half, inner, cols, b = final.shape[:4]
+    step = b // n_row
     for (j, d), piece in zip(sources, pieces):
         factor[jnp.bitwise_xor(info[0], d), j] = piece[...]
+    for i in range(half):
+        for j in range(inner):
+            for k in range(cols):
+                block = factor[jnp.bitwise_xor(info[1], distance), j, k].astype(F32)
+                final[i, j, k] = (-keep(info, cols, half + i, k) * block).astype(BF16)
     for (j, d), piece in zip(sources, pieces):
         if d == 0:
-            for k in range(piece.shape[0]):
-                turned[j, k] = piece[k].astype(F32).T.astype(BF16)
+            for k in range(cols):
+                whole[...] = piece[k].astype(F32).T
+                for e in range(n_row):
+                    there = pl.multiple_of(jnp.bitwise_xor(info[0], e) * step, 16)
+                    turned[j, k, e * step:(e + 1) * step, :] = whole[pl.ds(there, step), :].astype(BF16)
     total[...] = jnp.zeros_like(total)
     for (start, d), block in zip(parts, blocks):
         add_products(jnp.bitwise_xor(info[1], d), start, block, factor, total)
@@ -87,33 +97,28 @@
     both[...] = total_in[...]
     for (start, d), block in zip(parts, blocks):
         add_products(jnp.bitwise_xor(info[1], d), start, block, factor, both)
-    for i in range(half, rows):
-        total[i - half] = both[i]
     for k in range(cols):
         share = jnp.zeros(update.shape[1:], F32)
         for i in range(half):
+            total[i, k] = -(keep(info, cols, half + i, k) * both[half + i, k])
             value[i, k] = (-(keep(info, cols, i, k) * both[i, k])).astype(BF16)
             share += jnp.dot(turned[i, k], value[i, k], preferred_element_type=F32)
         update[k] = share
 
 
-def finish_kernel(n_row, distance, info, block, factor, total, update, turned, value, *refs):
-    sends, whole = refs[:-1], refs[-1]
+def finish_kernel(block, final, total, update, turned, value, *sends):
     half, cols, b = total.shape[:3]
-    place = jnp.bitwise_xor(info[1], distance)
-    piece = b // n_row
+    step = b // len(sends)
     for k in range(cols):
         share = update[k]
         for i in range(half):
             partial = total[i, k]
             for j in range(block.shape[1]):
-                partial += jnp.dot(block[i, j], factor[place, j, k], preferred_element_type=F32)
-            value[i, k] = (-(keep(info, cols, half + i, k) * partial)).astype(BF16)
+                partial += jnp.dot(block[i, j], final[i, j, k], preferred_element_type=F32)
+            value[i, k] = partial.astype(BF16)
             share += jnp.dot(turned[half + i, k], value[i, k], preferred_element_type=F32)
-        whole[k] = share
-        for d in range(n_row):
-            there = pl.multiple_of(jnp.bitwise_xor(info[0], d) * piece, 16)
-            sends[d][k] = whole[k, pl.ds(there, piece), :].astype(sends[d].dtype)
+        for d, send in enumerate(sends):
+            send[k] = share[d * step:(d + 1) * step].astype(send.dtype)
 
 
 def join_kernel(top, bottom, out, sems):
@@ -169,11 +174,13 @@
 
         kept, ends = shape(lower_block.shape, BF16), shape((half, cols, b, b), F32)
         sums, value = shape((rows, cols, b, b), F32), shape((half, cols, b, b), BF16)
-        factor, turned, total = call(
-            functools.partial(place_kernel, [x for _, x in pieces], [(start, d) for start, _, d in near]),
-            [shape((n_row,) + kept.shape, BF16), kept, sums],
+        final = shape((half,) + last[1].shape[1:2] + (cols, b, b), BF16)
+        factor, final, turned, total = call(
+            functools.partial(place_kernel, [x for _, x in pieces], [(start, d) for start, _, d in near], n_row, last[2]),
+            [shape((n_row,) + kept.shape, BF16), final, kept, sums],
             [SMEM] + [VMEM] * (len(pieces) + len(near)),
             20,
+            [pltpu.VMEM((b, b), F32)],
         )(info, *[m for m, _ in pieces], *[x for _, x, _ in near])
         top, total, update = call(
             functools.partial(early_kernel, [(start, d) for start, _, d in others]),
@@ -184,13 +191,11 @@
         )(info, *[x for _, x, _ in others], factor, total, turned)
         part = shape((cols, b // n_row, b), BF16)
         bottom, own, *sends = call(
-            functools.partial(finish_kernel, n_row, last[2]),
+            finish_kernel,
             [value, shape(part.shape, F32)] + [part] * (n_row - 1),
-            [SMEM] + [VMEM] * 5,
+            [VMEM] * 5,
             8,
-            [pltpu.VMEM((cols, b, b), F32)],
-        )(info, last[1], factor, total, update, turned)
-        got = [exchange(s, "row", n_row, d) for d, s in enumerate(sends, 1)]
+        )(last[1], final, total, update, turned)
         lower_out = call(
             join_kernel,
             shape(inverse_block.shape[:1] + lower_block.shape[1:], BF16),
@@ -199,6 +204,7 @@
             [pltpu.SemaphoreType.DMA((2,))],
             ANY,
         )(top, bottom)
+        got = [exchange(s, "row", n_row, d) for d, s in enumerate(sends, 1)]
         got, lower_out = lax.optimization_barrier((got, lower_out))
         diag_out = call(last_kernel, shape(diag_inverse.shape, F32), [VMEM] * (2 + len(got)), 4)(diag_inverse, own, *got)
         return lower_out, diag_out

time: 48 us -> 47.4 us (0.987)
  Pallas kernels: 6.21 us -> 5.7 us
    pallas_call x1, Pallas kernels: 1.35 us -> 0.79 us  [on_device(): call(finish_kernel, [value, shape(part.shape, F32)] + [part] * (n_row - 1...]
where the time goes in v4:
time: 47.4 us; the launch traced here: 47.2 us
  waiting for transfers between devices  21.4 us (45%)
  starting transfers between devices  16.5 us (35%)
  Pallas kernels  5.7 us (12%)
  local copies, waits for them, and re-layouts  2.87 us (6%)
  between operations  0.72 us (2%)
    ppermute x15, waiting for transfers between devices, exchange(): return lax.ppermute(array, axis, [(i, i ^ distance) for i in range(n)])  21.4 us
    ppermute x15, starting transfers between devices, exchange(): return lax.ppermute(array, axis, [(i, i ^ distance) for i in range(n)])  16.5 us
    pallas_call x1, Pallas kernels, on_device(): call(functools.partial(early_kernel, [(start, d) for start, _, d in other...  1.59 us
    pallas_call x1, Pallas kernels, on_device(): call(functools.partial(place_kernel, [x for _, x in pieces], [(start, d)...  1.17 us
    slice x1, local copies, waits for them, and re-layouts, on_device(): inverse_block[:half]  1.06 us
    unnamed x4, local copies, waits for them, and re-layouts  1.05 us
  transfers between devices with their start and end apart: 15, of which 7 were waited for; matrix products, arithmetic and copies ran while one was open for 4% of the time, Pallas kernels for 9%

profile of v4, /device:TPU:0, one launch (start us, length us, event | category | flops | bytes accessed | tf_op | source)
XLA Modules:
  0.0 47.2 jit_solution(4875546289640506727)
XLA Ops:
  0.6 3.1 %collective-permute-start.1 = (bf16[2,2,256,256]{3,2,1,0:T(8,128)(2,1)}, bf16[2,2,256,256]{3,2,1,0:T(8,128)(2,1)S(1)}, u32[]{:S(2)}, u32[]{:S(2)}) collective-permute-start(bf16[2,2,256,256]{3,2,1,0:T(8,128)(2,1)} %param.4), channel_id=1, source_target_pairs={{0,1},{1,0},{2,3},{3,2},{4,5},{5,4},{6,7},{7,6},{8,9},{9,8},{10,11... | collective-permute-start | bytes 1572872 | tf_op jit(solution)/shard_map/ppermute | solution.py:17
  3.7 1.1 %fusion = (bf16[1,2,256,256]{3,2,1,0:T(8,128)(2,1)S(1)}, bf16[1,2,256,256]{3,2,1,0:T(8,128)(2,1)S(1)}) fusion(bf16[2,2,256,256]{3,2,1,0:T(8,128)(2,1)} %param.4), kind=kLoop, calls=%fused_computation.1 | loop fusion | bytes 1048576 | tf_op jit(solution)/shard_map/slice | solution.py:167
  4.8 2.7 %collective-permute-start.2 = (bf16[1,2,256,256]{3,2,1,0:T(8,128)(2,1)S(1)}, bf16[1,2,256,256]{3,2,1,0:T(8,128)(2,1)S(1)}, u32[]{:S(2)}, u32[]{:S(2)}) collective-permute-start(bf16[1,2,256,256]{3,2,1,0:T(8,128)(2,1)S(1)} %get-tuple-element.46.refs_8_), channel_id=1, source_target_pairs={{0,2},{1,3},{2,0},{3,1},{4,6},{5,7},{6,4},{7,5},{8,10},{9,11},{10,... | collective-permute-start | bytes 786440 | tf_op jit(solution)/shard_map/ppermute | solution.py:17
  7.4 0.3 collective-permute-start
  7.8 0.8 %reshape.7 = s32[4]{0:T(128)S(1)} reshape(s32[2,2]{1,0:T(2,128)} %param.6) | data formatting | bytes 32 | tf_op jit(solution)/shard_map/reshape | solution.py:166
  8.5 0.1 pad_add_fusion.info
  8.6 0.2 collective-permute-done.5.token
  8.8 1.0 %copy-done = bf16[2,2,256,256]{3,2,1,0:T(8,128)(2,1)S(1)} copy-done((bf16[2,2,256,256]{3,2,1,0:T(8,128)(2,1)S(1)}, bf16[2,2,256,256]{3,2,1,0:T(8,128)(2,1)}, u32[]{:S(2)}) %copy-start) | copy-done | bytes 524312
  9.8 0.6 %shard_map.59 = (bf16[2,256,256]{2,1,0:T(8,128)(2,1)S(1)}, bf16[2,256,256]{2,1,0:T(8,128)(2,1)S(1)}) custom-call(s32[6]{0:T(128)S(1)} %pad_add_fusion.info, s32[2,2]{1,0:T(2,128)S(1)} %collective-permute-done.5.token, bf16[2,2,256,256]{3,2,1,0:T(8,128)(2,1)S(1)} %copy-done), custom_call_target="tpu_custom_call" | custom-call | tf_op jit(solution)/shard_map/pallas_call | solution.py:170
  10.5 1.6 %collective-permute-start.9 = (bf16[2,256,256]{2,1,0:T(8,128)(2,1)S(1)}, bf16[2,256,256]{2,1,0:T(8,128)(2,1)S(1)}, u32[]{:S(2)}, u32[]{:S(2)}) collective-permute-start(bf16[2,256,256]{2,1,0:T(8,128)(2,1)S(1)} %get-tuple-element.27.refs_4_), channel_id=1, source_target_pairs={{0,8},{4,12},{8,0},{12,4},{1,9},{5,13},{9,1},{13,5},{2,10},{6,14},... | collective-permute-start | bytes 786440 | tf_op jit(solution)/shard_map/ppermute | solution.py:17
  12.0 0.5 %collective-permute-start.6 = (bf16[2,256,256]{2,1,0:T(8,128)(2,1)S(1)}, bf16[2,256,256]{2,1,0:T(8,128)(2,1)S(1)}, u32[]{:S(2)}, u32[]{:S(2)}) collective-permute-start(bf16[2,256,256]{2,1,0:T(8,128)(2,1)S(1)} %get-tuple-element.26.refs_0_), channel_id=1, source_target_pairs={{0,8},{4,12},{8,0},{12,4},{1,9},{5,13},{9,1},{13,5},{2,10},{6,14},... | collective-permute-start | bytes 786440 | tf_op jit(solution)/shard_map/ppermute | solution.py:17
  12.6 9.3 %collective-permute-done.2.refs_1_ = bf16[1,2,256,256]{3,2,1,0:T(8,128)(2,1)S(1)} collective-permute-done((bf16[1,2,256,256]{3,2,1,0:T(8,128)(2,1)S(1)}, bf16[1,2,256,256]{3,2,1,0:T(8,128)(2,1)S(1)}, u32[]{:S(2)}, u32[]{:S(2)}) %collective-permute-start.2) | collective-permute-done | bytes 262176 | tf_op jit(solution)/shard_map/ppermute | solution.py:17
  21.9 3.6 %collective-permute-start.3 = (bf16[1,2,256,256]{3,2,1,0:T(8,128)(2,1)S(1)}, bf16[1,2,256,256]{3,2,1,0:T(8,128)(2,1)S(1)}, u32[]{:S(2)}, u32[]{:S(2)}) collective-permute-start(bf16[1,2,256,256]{3,2,1,0:T(8,128)(2,1)S(1)} %collective-permute-done.2.refs_1_), channel_id=1, source_target_pairs={{0,1},{1,0},{2,3},{3,2},{4,5},{5,4},{6,7},{7,6},{8,9},{9,8},{10,11... | collective-permute-start | bytes 786440 | tf_op jit(solution)/shard_map/ppermute | solution.py:17
  25.5 4.9 %collective-permute-done.refs_2_ = bf16[1,2,256,256]{3,2,1,0:T(8,128)(2,1)S(1)} collective-permute-done((bf16[1,2,256,256]{3,2,1,0:T(8,128)(2,1)S(1)}, bf16[1,2,256,256]{3,2,1,0:T(8,128)(2,1)S(1)}, u32[]{:S(2)}, u32[]{:S(2)}) %collective-permute-start) | collective-permute-done | bytes 262176 | tf_op jit(solution)/shard_map/ppermute | solution.py:17
  30.4 0.0 collective-permute-start.10
  30.4 0.5 %collective-permute-start.7 = (bf16[2,256,256]{2,1,0:T(8,128)(2,1)S(1)}, bf16[2,256,256]{2,1,0:T(8,128)(2,1)S(1)}, u32[]{:S(2)}, u32[]{:S(2)}) collective-permute-start(bf16[2,256,256]{2,1,0:T(8,128)(2,1)S(1)} %get-tuple-element.26.refs_0_), channel_id=1, source_target_pairs={{0,4},{4,0},{8,12},{12,8},{1,5},{5,1},{9,13},{13,9},{2,6},{6,2},{1... | collective-permute-start | bytes 786440 | tf_op jit(solution)/shard_map/ppermute | solution.py:17
  30.9 0.1 collective-permute-start.11
  30.9 0.4 collective-permute-start.8
  31.4 1.3 %collective-permute-done.3.refs_3_ = bf16[1,2,256,256]{3,2,1,0:T(8,128)(2,1)S(1)} collective-permute-done((bf16[1,2,256,256]{3,2,1,0:T(8,128)(2,1)S(1)}, bf16[1,2,256,256]{3,2,1,0:T(8,128)(2,1)S(1)}, u32[]{:S(2)}, u32[]{:S(2)}) %collective-permute-start.3) | collective-permute-done | bytes 262176 | tf_op jit(solution)/shard_map/ppermute | solution.py:17
  32.7 1.8 %collective-permute-start.4 = (bf16[1,2,256,256]{3,2,1,0:T(8,128)(2,1)S(1)}, bf16[1,2,256,256]{3,2,1,0:T(8,128)(2,1)S(1)}, u32[]{:S(2)}, u32[]{:S(2)}) collective-permute-start(bf16[1,2,256,256]{3,2,1,0:T(8,128)(2,1)S(1)} %collective-permute-done.refs_2_), channel_id=1, source_target_pairs={{0,1},{1,0},{2,3},{3,2},{4,5},{5,4},{6,7},{7,6},{8,9},{9,8},{10,11... | collective-permute-start | bytes 786440 | tf_op jit(solution)/shard_map/ppermute | solution.py:17
  34.5 1.2 %shard_map.60 = (bf16[4,2,2,256,256]{4,3,2,1,0:T(8,128)(2,1)S(1)}, bf16[1,2,2,256,256]{4,3,2,1,0:T(8,128)(2,1)S(1)}, bf16[2,2,256,256]{3,2,1,0:T(8,128)(2,1)S(1)}, f32[2,2,256,256]{3,2,1,0:T(8,128)S(1)}) custom-call(s32[6]{0:T(128)S(1)} %pad_add_fusion.info, bf16[2,256,256]{2,1,0:T(8,128)(2,1)S(1)} %get-tuple-element.26.refs_0_, ...), custom_call_target="tpu_custom_call" | custom-call | tf_op jit(solution)/shard_map/pallas_call | solution.py:178
  35.7 1.6 %shard_map.61 = (bf16[1,2,256,256]{3,2,1,0:T(8,128)(2,1)S(1)}, f32[1,2,256,256]{3,2,1,0:T(8,128)S(1)}, f32[2,256,256]{2,1,0:T(8,128)S(1)}) custom-call(s32[6]{0:T(128)S(1)} %pad_add_fusion.info, bf16[2,2,256,256]{3,2,1,0:T(8,128)(2,1)S(1)} %collective-permute-done.1.refs_0_, bf16[1,2,256,256]{3,2,1,0:T(8,128)(2,1)S(1)} %collective-permute-done.2.refs_1_, ...), custom_call_target="tpu_custom_call" | custom-call | tf_op jit(solution)/shard_map/pallas_call | solution.py:185
  37.3 0.0 copy-start.1
  37.3 2.7 %collective-permute-done.4.block = bf16[1,2,256,256]{3,2,1,0:T(8,128)(2,1)S(1)} collective-permute-done((bf16[1,2,256,256]{3,2,1,0:T(8,128)(2,1)S(1)}, bf16[1,2,256,256]{3,2,1,0:T(8,128)(2,1)S(1)}, u32[]{:S(2)}, u32[]{:S(2)}) %collective-permute-start.4) | collective-permute-done | bytes 262176 | tf_op jit(solution)/shard_map/ppermute | solution.py:17
  40.0 0.8 %shard_map.62 = (bf16[1,2,256,256]{3,2,1,0:T(8,128)(2,1)S(1)}, f32[2,64,256]{2,1,0:T(8,128)S(1)}, bf16[2,64,256]{2,1,0:T(8,128)(2,1)S(1)}, bf16[2,64,256]{2,1,0:T(8,128)(2,1)S(1)}, bf16[2,64,256]{2,1,0:T(8,128)(2,1)S(1)}) custom-call(bf16[1,2,256,256]{3,2,1,0:T(8,128)(2,1)S(1)} %collective-permute-done.4.block, ...), custom_call_target="tpu_custom_call" | custom-call | tf_op jit(solution)/shard_map/pallas_call | solution.py:193
  40.8 0.1 collective-permute-start.12
  40.9 1.6 %collective-permute-start.13 = (bf16[2,64,256]{2,1,0:T(8,128)(2,1)S(1)}, bf16[2,64,256]{2,1,0:T(8,128)(2,1)S(1)}, u32[]{:S(2)}, u32[]{:S(2)}) collective-permute-start(bf16[2,64,256]{2,1,0:T(8,128)(2,1)S(1)} %get-tuple-element.37), channel_id=1, source_target_pairs={{0,8},{4,12},{8,0},{12,4},{1,9},{5,13},{9,1},{13,5},{2,10},{6,14},... | collective-permute-start | bytes 196616 | tf_op jit(solution)/shard_map/ppermute | solution.py:17
  42.5 0.3 collective-permute-start.14
  42.7 0.8 %shard_map.63 = bf16[2,2,256,256]{3,2,1,0:T(8,128)(2,1)} custom-call(bf16[1,2,256,256]{3,2,1,0:T(8,128)(2,1)S(1)} %get-tuple-element.39.top, bf16[1,2,256,256]{3,2,1,0:T(8,128)(2,1)S(1)} %get-tuple-element.40.bottom), custom_call_target="tpu_custom_call" | custom-call | tf_op jit(solution)/shard_map/pallas_call | solution.py:199
  43.6 1.8 %collective-permute-done.13.refs_3_ = bf16[2,64,256]{2,1,0:T(8,128)(2,1)S(1)} collective-permute-done((bf16[2,64,256]{2,1,0:T(8,128)(2,1)S(1)}, bf16[2,64,256]{2,1,0:T(8,128)(2,1)S(1)}, u32[]{:S(2)}, u32[]{:S(2)}) %collective-permute-start.13) | collective-permute-done | bytes 65568 | tf_op jit(solution)/shard_map/ppermute | solution.py:17
  45.4 1.1 %collective-permute-done.14.refs_4_ = bf16[2,64,256]{2,1,0:T(8,128)(2,1)S(1)} collective-permute-done((bf16[2,64,256]{2,1,0:T(8,128)(2,1)S(1)}, bf16[2,64,256]{2,1,0:T(8,128)(2,1)S(1)}, u32[]{:S(2)}, u32[]{:S(2)}) %collective-permute-start.14) | collective-permute-done | bytes 65568 | tf_op jit(solution)/shard_map/ppermute | solution.py:17
  46.5 0.7 %shard_map.64 = f32[2,64,256]{2,1,0:T(8,128)} custom-call(f32[2,64,256]{2,1,0:T(8,128)S(1)} %copy-done.1, f32[2,64,256]{2,1,0:T(8,128)S(1)} %get-tuple-element.42.refs_1_, bf16[2,64,256]{2,1,0:T(8,128)(2,1)S(1)} %collective-permute-done.12.refs_2_, bf16[2,64,256]{2,1,0:T(8,128)(2,1)S(1)} %collective-permute-done.13.refs_3_, ...), custom_call_target="tpu_custom_call" | custom-call | tf_op jit(solution)/shard_map/pallas_call | solution.py:209
  (11 shorter events, 0.0 us)
Async XLA Ops:
  0.6 30.3 %collective-permute-start.1 = (bf16[2,2,256,256]{3,2,1,0:T(8,128)(2,1)}, bf16[2,2,256,256]{3,2,1,0:T(8,128)(2,1)S(1)}, u32[]{:S(2)}, u32[]{:S(2)}) collective-permute-start(bf16[2,2,256,256]{3,2,1,0:T(8,128)(2,1)} %param.4), channel_id=1, source_target_pairs={{0,1},{1,0},{2,3},{3,2},{4,5},{5,4},{6,7},{7,6},{8,9},{9,8},{10,11... | collective-permute-start | bytes 1572872 | tf_op jit(solution)/shard_map/ppermute | solution.py:17
  4.8 17.1 %collective-permute-start.2 = (bf16[1,2,256,256]{3,2,1,0:T(8,128)(2,1)S(1)}, bf16[1,2,256,256]{3,2,1,0:T(8,128)(2,1)S(1)}, u32[]{:S(2)}, u32[]{:S(2)}) collective-permute-start(bf16[1,2,256,256]{3,2,1,0:T(8,128)(2,1)S(1)} %get-tuple-element.46.refs_8_), channel_id=1, source_target_pairs={{0,2},{1,3},{2,0},{3,1},{4,6},{5,7},{6,4},{7,5},{8,10},{9,11},{10,... | collective-permute-start | bytes 786440 | tf_op jit(solution)/shard_map/ppermute | solution.py:17
  7.4 1.4 %collective-permute-start.5 = (s32[2,2]{1,0:T(2,128)}, s32[2,2]{1,0:T(2,128)S(1)}, u32[]{:S(2)}, u32[]{:S(2)}) collective-permute-start(s32[2,2]{1,0:T(2,128)} %param.6), channel_id=1, source_target_pairs={{0,4},{4,0},{8,12},{12,8},{1,5},{5,1},{9,13},{13,9},{2,6},{6,2},{1... | collective-permute-start | bytes 56 | tf_op jit(solution)/shard_map/ppermute | solution.py:17
  7.4 22.9 %collective-permute-start = (bf16[1,2,256,256]{3,2,1,0:T(8,128)(2,1)S(1)}, bf16[1,2,256,256]{3,2,1,0:T(8,128)(2,1)S(1)}, u32[]{:S(2)}, u32[]{:S(2)}) collective-permute-start(bf16[1,2,256,256]{3,2,1,0:T(8,128)(2,1)S(1)} %get-tuple-element.47.refs_9_), channel_id=1, source_target_pairs={{0,2},{1,3},{2,0},{3,1},{4,6},{5,7},{6,4},{7,5},{8,10},{9,11},{10,... | collective-permute-start | bytes 786440 | tf_op jit(solution)/shard_map/ppermute | solution.py:17
  8.8 1.0 %copy-start = (bf16[2,2,256,256]{3,2,1,0:T(8,128)(2,1)S(1)}, bf16[2,2,256,256]{3,2,1,0:T(8,128)(2,1)}, u32[]{:S(2)}) copy-start(bf16[2,2,256,256]{3,2,1,0:T(8,128)(2,1)} %lower.1) | copy-start | bytes 1572868
  10.5 19.9 %collective-permute-start.9 = (bf16[2,256,256]{2,1,0:T(8,128)(2,1)S(1)}, bf16[2,256,256]{2,1,0:T(8,128)(2,1)S(1)}, u32[]{:S(2)}, u32[]{:S(2)}) collective-permute-start(bf16[2,256,256]{2,1,0:T(8,128)(2,1)S(1)} %get-tuple-element.27.refs_4_), channel_id=1, source_target_pairs={{0,8},{4,12},{8,0},{12,4},{1,9},{5,13},{9,1},{13,5},{2,10},{6,14},... | collective-permute-start | bytes 786440 | tf_op jit(solution)/shard_map/ppermute | solution.py:17
  12.0 18.8 %collective-permute-start.6 = (bf16[2,256,256]{2,1,0:T(8,128)(2,1)S(1)}, bf16[2,256,256]{2,1,0:T(8,128)(2,1)S(1)}, u32[]{:S(2)}, u32[]{:S(2)}) collective-permute-start(bf16[2,256,256]{2,1,0:T(8,128)(2,1)S(1)} %get-tuple-element.26.refs_0_), channel_id=1, source_target_pairs={{0,8},{4,12},{8,0},{12,4},{1,9},{5,13},{9,1},{13,5},{2,10},{6,14},... | collective-permute-start | bytes 786440 | tf_op jit(solution)/shard_map/ppermute | solution.py:17
  21.9 10.8 %collective-permute-start.3 = (bf16[1,2,256,256]{3,2,1,0:T(8,128)(2,1)S(1)}, bf16[1,2,256,256]{3,2,1,0:T(8,128)(2,1)S(1)}, u32[]{:S(2)}, u32[]{:S(2)}) collective-permute-start(bf16[1,2,256,256]{3,2,1,0:T(8,128)(2,1)S(1)} %collective-permute-done.2.refs_1_), channel_id=1, source_target_pairs={{0,1},{1,0},{2,3},{3,2},{4,5},{5,4},{6,7},{7,6},{8,9},{9,8},{10,11... | collective-permute-start | bytes 786440 | tf_op jit(solution)/shard_map/ppermute | solution.py:17
  30.4 4.1 %collective-permute-start.10 = (bf16[2,256,256]{2,1,0:T(8,128)(2,1)S(1)}, bf16[2,256,256]{2,1,0:T(8,128)(2,1)S(1)}, u32[]{:S(2)}, u32[]{:S(2)}) collective-permute-start(bf16[2,256,256]{2,1,0:T(8,128)(2,1)S(1)} %get-tuple-element.27.refs_4_), channel_id=1, source_target_pairs={{0,4},{4,0},{8,12},{12,8},{1,5},{5,1},{9,13},{13,9},{2,6},{6,2},{1... | collective-permute-start | bytes 786440 | tf_op jit(solution)/shard_map/ppermute | solution.py:17
  30.4 4.1 %collective-permute-start.7 = (bf16[2,256,256]{2,1,0:T(8,128)(2,1)S(1)}, bf16[2,256,256]{2,1,0:T(8,128)(2,1)S(1)}, u32[]{:S(2)}, u32[]{:S(2)}) collective-permute-start(bf16[2,256,256]{2,1,0:T(8,128)(2,1)S(1)} %get-tuple-element.26.refs_0_), channel_id=1, source_target_pairs={{0,4},{4,0},{8,12},{12,8},{1,5},{5,1},{9,13},{13,9},{2,6},{6,2},{1... | collective-permute-start | bytes 786440 | tf_op jit(solution)/shard_map/ppermute | solution.py:17
  30.9 3.6 %collective-permute-start.11 = (bf16[2,256,256]{2,1,0:T(8,128)(2,1)S(1)}, bf16[2,256,256]{2,1,0:T(8,128)(2,1)S(1)}, u32[]{:S(2)}, u32[]{:S(2)}) collective-permute-start(bf16[2,256,256]{2,1,0:T(8,128)(2,1)S(1)} %collective-permute-done.9.refs_5_), channel_id=1, source_target_pairs={{0,4},{4,0},{8,12},{12,8},{1,5},{5,1},{9,13},{13,9},{2,6},{6,2},{1... | collective-permute-start | bytes 786440 | tf_op jit(solution)/shard_map/ppermute | solution.py:17
  30.9 3.6 %collective-permute-start.8 = (bf16[2,256,256]{2,1,0:T(8,128)(2,1)S(1)}, bf16[2,256,256]{2,1,0:T(8,128)(2,1)S(1)}, u32[]{:S(2)}, u32[]{:S(2)}) collective-permute-start(bf16[2,256,256]{2,1,0:T(8,128)(2,1)S(1)} %collective-permute-done.6.refs_1_), channel_id=1, source_target_pairs={{0,4},{4,0},{8,12},{12,8},{1,5},{5,1},{9,13},{13,9},{2,6},{6,2},{1... | collective-permute-start | bytes 786440 | tf_op jit(solution)/shard_map/ppermute | solution.py:17
  32.7 7.3 %collective-permute-start.4 = (bf16[1,2,256,256]{3,2,1,0:T(8,128)(2,1)S(1)}, bf16[1,2,256,256]{3,2,1,0:T(8,128)(2,1)S(1)}, u32[]{:S(2)}, u32[]{:S(2)}) collective-permute-start(bf16[1,2,256,256]{3,2,1,0:T(8,128)(2,1)S(1)} %collective-permute-done.refs_2_), channel_id=1, source_target_pairs={{0,1},{1,0},{2,3},{3,2},{4,5},{5,4},{6,7},{7,6},{8,9},{9,8},{10,11... | collective-permute-start | bytes 786440 | tf_op jit(solution)/shard_map/ppermute | solution.py:17
  37.3 9.2 %copy-start.1 = (f32[2,64,256]{2,1,0:T(8,128)S(1)}, f32[2,64,256]{2,1,0:T(8,128)}, u32[]{:S(2)}) copy-start(f32[2,64,256]{2,1,0:T(8,128)} %refs_0_.1) | copy-start | bytes 393220
  40.8 2.8 %collective-permute-start.12 = (bf16[2,64,256]{2,1,0:T(8,128)(2,1)S(1)}, bf16[2,64,256]{2,1,0:T(8,128)(2,1)S(1)}, u32[]{:S(2)}, u32[]{:S(2)}) collective-permute-start(bf16[2,64,256]{2,1,0:T(8,128)(2,1)S(1)} %get-tuple-element.36), channel_id=1, source_target_pairs={{0,4},{4,0},{8,12},{12,8},{1,5},{5,1},{9,13},{13,9},{2,6},{6,2},{1... | collective-permute-start | bytes 196616 | tf_op jit(solution)/shard_map/ppermute | solution.py:17
  40.9 4.5 %collective-permute-start.13 = (bf16[2,64,256]{2,1,0:T(8,128)(2,1)S(1)}, bf16[2,64,256]{2,1,0:T(8,128)(2,1)S(1)}, u32[]{:S(2)}, u32[]{:S(2)}) collective-permute-start(bf16[2,64,256]{2,1,0:T(8,128)(2,1)S(1)} %get-tuple-element.37), channel_id=1, source_target_pairs={{0,8},{4,12},{8,0},{12,4},{1,9},{5,13},{9,1},{13,5},{2,10},{6,14},... | collective-permute-start | bytes 196616 | tf_op jit(solution)/shard_map/ppermute | solution.py:17
  42.5 4.0 %collective-permute-start.14 = (bf16[2,64,256]{2,1,0:T(8,128)(2,1)S(1)}, bf16[2,64,256]{2,1,0:T(8,128)(2,1)S(1)}, u32[]{:S(2)}, u32[]{:S(2)}) collective-permute-start(bf16[2,64,256]{2,1,0:T(8,128)(2,1)S(1)} %get-tuple-element.38), channel_id=1, source_target_pairs={{0,12},{4,8},{8,4},{12,0},{1,13},{5,9},{9,5},{13,1},{2,14},{6,10},... | collective-permute-start | bytes 196616 | tf_op jit(solution)/shard_map/ppermute | solution.py:17

commit v5 on v0

v5 whole, which is shorter than its diff:
```python
import functools

import jax
import jax.numpy as jnp
from jax import lax
from jax.experimental import pallas as pl
from jax.experimental.pallas import tpu as pltpu
from jax.sharding import PartitionSpec as P

F32, BF16 = jnp.float32, jnp.bfloat16
VMEM = pl.BlockSpec(memory_space=pltpu.VMEM)
SMEM = pl.BlockSpec(memory_space=pltpu.SMEM)
ANY = pl.BlockSpec(memory_space=pl.ANY)


def exchange(array, axis, n, distance):
    return lax.ppermute(array, axis, [(i, i ^ distance) for i in range(n)])


def gather(own, axis, n, distances):
    held = [(own, 0)]
    for distance in distances:
        held += [(exchange(a, axis, n, distance), d ^ distance) for a, d in held]
    return held


def column_gather(own, n, cut):
    far = [1 << p for p in reversed(range(1, n.bit_length() - 1))]
    whole, first, rest = slice(0, own.shape[2]), slice(0, cut), slice(cut, own.shape[2])
    beside = exchange(own, "col", n, 1)
    upper = gather(own[:, :, first], "col", n, far)[1:]
    lower = gather(own[:, :, rest], "col", n, far)[1:]
    arrays, beside = lax.optimization_barrier(([a for a, _ in lower], beside))
    lower = [(a, d) for a, (_, d) in zip(arrays, lower)]
    top = [(exchange(a, "col", n, 1), d ^ 1) for a, d in upper]
    arrays, before = lax.optimization_barrier(([a for a, _ in lower], [a for a, _ in top]))
    lower = [(a, d) for a, (_, d) in zip(arrays, lower)]
    top = [(a, d) for a, (_, d) in zip(before, top)]
    late = [(rest, exchange(a, "col", n, 1), d ^ 1) for a, d in lower]
    early = [(whole, own, 0), (whole, beside, 1)] + [(first, a, d) for a, d in upper] + [(rest, a, d) for a, d in lower]
    return early + [(first, a, d) for a, d in top], late


def keep(info, cols, i, k):
    return info[2 + i * cols + k].astype(F32)


def mask_kernel(info, token, lower, *masked):
    cols = lower.shape[1]
    for j, out in enumerate(masked):
        for k in range(cols):
            out[k] = (lower[j, k].astype(F32) * keep(info, cols, j, k)).astype(BF16)


def early_kernel(sources, parts, n_row, distance, info, *refs):
    n_pieces = len(sources)
    pieces, blocks, (final, turned, total, factor, whole) = refs[:n_pieces], refs[n_pieces:-5], refs[-5:]
    rows, inner, cols, b = final.shape[:4]
    step = b // n_row
    for (j, d), piece in zip(sources, pieces):
        factor[jnp.bitwise_xor(info[0], d), j] = piece[...]
    for i in range(rows):
        for k in range(cols):
            sign = -keep(info, cols, i, k)
            for j in range(inner):
                final[i, j, k] = (sign * factor[jnp.bitwise_xor(info[1], distance), j, k].astype(F32)).astype(BF16)
            whole[...] = pieces[sources.index((i, 0))][k].astype(F32).T
            for d in range(n_row):
                there = pl.multiple_of(jnp.bitwise_xor(info[0], d) * step, 16)
                turned[i, k, d * step:(d + 1) * step, :] = whole[pl.ds(there, step), :].astype(BF16)
            total[i, k] = jnp.zeros((b, b), F32)
            for (at, d), block in zip(parts, blocks):
                partial = total[i, k, at, :]
                for j in range(inner):
                    partial += jnp.dot(
                        block[i, j], factor[jnp.bitwise_xor(info[1], d), j, k], preferred_element_type=F32
                    )
                total[i, k, at, :] = partial
            total[i, k] = sign * total[i, k]


def finish_kernel(parts, *refs):
    blocks, (final, total, turned, value, kept, sent) = refs[:len(parts)], refs[len(parts):]
    rows, cols, b = total.shape[:3]
    step = kept.shape[2]
    start = parts[0].start
    for k in range(cols):
        share = jnp.zeros((b, b), F32)
        for i in range(rows):
            value[i, k, :start, :] = total[i, k, :start, :].astype(BF16)
            for at, block in zip(parts, blocks):
                partial = total[i, k, at, :]
                for j in range(block.shape[1]):
                    partial += jnp.dot(block[i, j], final[i, j, k], preferred_element_type=F32)
                value[i, k, at, :] = partial.astype(BF16)
            share += jnp.dot(turned[i, k], value[i, k], preferred_element_type=F32)
        for m in range(kept.shape[0]):
            at = 2 * m * step
            kept[m, k] = share[at:at + step]
            sent[m, k] = share[at + step:at + 2 * step].astype(BF16)


def chip_kernel(kept, got, own, *sends):
    own[...] = kept[0] + got[0].astype(F32)
    for m, send in enumerate(sends, 1):
        send[...] = (kept[m] + got[m].astype(F32)).astype(BF16)


def join_kernel(value, out, sem):
    copy = pltpu.make_async_copy(value, out, sem)
    copy.start()
    copy.wait()


def last_kernel(*refs):
    diag, own, got, out = refs[0], refs[1], refs[2:-1], refs[-1]
    update = own[...]
    for part in got:
        update += part[...].astype(F32)
    out[...] = diag[...] - update


def call(kernel, out_shape, in_specs, mib, scratch=(), out_specs=None, aliases={}):
    return pl.pallas_call(
        kernel,
        out_shape=out_shape,
        in_specs=in_specs,
        out_specs=jax.tree.map(lambda _: VMEM, out_shape) if out_specs is None else out_specs,
        scratch_shapes=scratch,
        input_output_aliases=aliases,
        compiler_params=pltpu.CompilerParams(vmem_limit_bytes=mib << 20),
        cost_estimate=pl.CostEstimate(flops=0, bytes_accessed=0, transcendentals=0),
    )


def solution(mesh):
    n_row, n_col = mesh.shape["row"], mesh.shape["col"]

    def on_device(inverse_block, lower_block, pattern, diag_inverse):
        row, col = lax.axis_index("row"), lax.axis_index("col")
        rows, cols, b = lower_block.shape[:3]
        shape = jax.ShapeDtypeStruct

        info = jnp.concatenate([jnp.stack([row, col]).astype(jnp.int32), pattern.reshape(-1)])
        early, late = column_gather(inverse_block, n_col, inverse_block.shape[2] * 7 // 16)
        token = exchange(pattern, "row", n_row, 1)

        kept = shape(lower_block.shape, BF16)
        masked = call(mask_kernel, [shape((cols, b, b), BF16)] * rows, [SMEM, SMEM, VMEM], 4)(info, token, lower_block)
        order = [1 << p for p in range(1, n_row.bit_length() - 1)] + [1]
        pieces = [(m, (j, d)) for j, own in enumerate(masked) for m, d in gather(own, "row", n_row, order)]
        last, early = late[-1:], early + late[:-1]

        sums = shape((rows, cols, b, b), F32)
        final, turned, total = call(
            functools.partial(
                early_kernel, [d for _, d in pieces], [(at, d) for at, _, d in early], n_row, last[0][2]
            ),
            [shape((rows,) + inverse_block.shape[1:2] + kept.shape[1:], BF16), kept, sums],
            [SMEM] + [VMEM] * (len(pieces) + len(early)),
            16 + n_row,
            [pltpu.VMEM((n_row,) + kept.shape, BF16), pltpu.VMEM((b, b), F32)],
        )(info, *[m for m, _ in pieces], *[x for _, x, _ in early])
        part = shape((cols, b // n_row, b), BF16)
        pairs = (n_row // 2,) + part.shape
        value, mine, theirs = call(
            functools.partial(finish_kernel, [at for at, _, _ in last]),
            [shape(sums.shape, BF16), shape(pairs, F32), shape(pairs, BF16)],
            [VMEM] * (len(last) + 3),
            8,
        )(*[x for _, x, _ in last], final, total, turned)
        own, *sends = call(chip_kernel, [shape(part.shape, F32)] + [part] * (n_row // 2 - 1), [VMEM] * 2, 2)(
            mine, exchange(theirs, "row", n_row, 1)
        )
        lower_out = call(
            join_kernel,
            shape(sums.shape, BF16),
            [VMEM],
            2,
            [pltpu.SemaphoreType.DMA(())],
            ANY,
        )(value)
        got = [exchange(s, "row", n_row, 2 * m) for m, s in enumerate(sends, 1)]
        got, lower_out = lax.optimization_barrier((got, lower_out))
        diag_out = call(last_kernel, shape(diag_inverse.shape, F32), [VMEM] * (2 + len(got)), 4)(diag_inverse, own, *got)
        return lower_out, diag_out

    spec, diag = P(("pole", "row"), "col", None, None), P(("pole", "col"), "row", None)
    return jax.shard_map(
        on_device,
        mesh=mesh,
        in_specs=(spec, spec, P("row", "col"), diag),
        out_specs=(spec, diag),
        check_vma=False,
    )
```

time: 115 us -> 47.4 us (0.41)
  waiting for transfers between devices: 90.6 us -> 23.6 us
  starting transfers between devices: 0.12 us -> 16.1 us
  between operations: 13.8 us -> 0.72 us
  Pallas kernels: 0 us -> 4.7 us
  matrix products: 4.53 us -> 0 us
  other arithmetic: 3.09 us -> 0.08 us
    all_gather x2 -> x0, waiting for transfers between devices: 70.6 us -> none  [the longest x1 47.2 us: on_device(): gathered = lax.all_gather(inverse_block, 'col', axis=1, tiled=True)]
    ppermute x0 -> x14, waiting for transfers between devices: none -> 23.6 us  [exchange(): return lax.ppermute(array, axis, [(i, i ^ distance) for i in range(n)])]
    reduce_scatter x1 -> x0, waiting for transfers between devices: 19.2 us -> none  [on_device(): lax.psum_scatter(diag_terms.astype(jnp.bfloat16), 'row', scatter_dimensio...]
    ppermute x0 -> x14, starting transfers between devices: none -> 16.1 us  [exchange(): return lax.ppermute(array, axis, [(i, i ^ distance) for i in range(n)])]
    pallas_call x0 -> x6, Pallas kernels: none -> 4.7 us  [the longest x1 1.97 us: on_device(): call(functools.partial(early_kernel, [d for _, d in pieces], [(at, d) for...]
    dot_general x2 -> x0, matrix products: 4.53 us -> none  [the longest x1 3.5 us: on_device(): jnp.einsum('ijab,jkbc->ikac', gathered, factor_cols, preferred_element_ty...]
    unnamed x6 -> x8, local copies, waits for them, and re-layouts: 2.25 us -> 0.02 us
    slice x0 -> x2, local copies, waits for them, and re-layouts: none -> 1.97 us  [the longest x1 0.99 us: column_gather(): upper = gather(own[:, :, first], 'col', n, far)[1:]]
  transfers between devices with their start and end apart: 3 -> 14, of which waited for: 3 -> 10; matrix products, arithmetic and copies ran while one was open for 4% -> 5% of each run, Pallas kernels for 0% -> 7%
where the time goes in v5:
time: 47.4 us; the launch traced here: 47.3 us
  waiting for transfers between devices  23.6 us (50%)
  starting transfers between devices  16.1 us (34%)
  Pallas kernels  4.7 us (10%)
  local copies, waits for them, and re-layouts  2.07 us (4%)
  between operations  0.72 us (2%)
    ppermute x14, waiting for transfers between devices, exchange(): return lax.ppermute(array, axis, [(i, i ^ distance) for i in range(n)])  23.6 us
    ppermute x14, starting transfers between devices, exchange(): return lax.ppermute(array, axis, [(i, i ^ distance) for i in range(n)])  16.1 us
    pallas_call x1, Pallas kernels, on_device(): call(functools.partial(early_kernel, [d for _, d in pieces], [(at, d) for...  1.97 us
    slice x1, local copies, waits for them, and re-layouts, column_gather(): upper = gather(own[:, :, first], 'col', n, far)[1:]  0.99 us
    slice x1, local copies, waits for them, and re-layouts, column_gather(): lower = gather(own[:, :, rest], 'col', n, far)[1:]  0.98 us
  transfers between devices with their start and end apart: 14, of which 10 were waited for; matrix products, arithmetic and copies ran while one was open for 5% of the time, Pallas kernels for 7%

profile of v5, /device:TPU:0, one launch (start us, length us, event | category | flops | bytes accessed | tf_op | source)
XLA Modules:
  0.0 47.3 jit_solution(3769681401855296139)
XLA Ops:
  0.6 3.1 %collective-permute-start.1 = (bf16[2,2,256,256]{3,2,1,0:T(8,128)(2,1)}, bf16[2,2,256,256]{3,2,1,0:T(8,128)(2,1)S(1)}, u32[]{:S(2)}, u32[]{:S(2)}) collective-permute-start(bf16[2,2,256,256]{3,2,1,0:T(8,128)(2,1)} %refs_8_.1), channel_id=1, source_target_pairs={{0,1},{1,0},{2,3},{3,2},{4,5},{5,4},{6,7},{7,6},{8,9},{9,8},{10,11... | collective-permute-start | bytes 1572872 | tf_op jit(solution)/shard_map/ppermute | solution.py:17
  3.7 1.0 %slice.7 = bf16[2,2,112,256]{3,2,1,0:T(8,128)(2,1)S(1)} slice(bf16[2,2,256,256]{3,2,1,0:T(8,128)(2,1)} %refs_8_.1), slice={[0:2], [0:2], [0:112], [0:256]} | slice | bytes 458752 | tf_op jit(solution)/shard_map/slice | solution.py:31
  4.7 0.0 copy-start
  4.7 2.7 %collective-permute-start.2 = (bf16[2,2,112,256]{3,2,1,0:T(8,128)(2,1)S(1)}, bf16[2,2,112,256]{3,2,1,0:T(8,128)(2,1)S(1)}, u32[]{:S(2)}, u32[]{:S(2)}) collective-permute-start(bf16[2,2,112,256]{3,2,1,0:T(8,128)(2,1)S(1)} %slice.7), channel_id=1, source_target_pairs={{0,2},{1,3},{2,0},{3,1},{4,6},{5,7},{6,4},{7,5},{8,10},{9,11},{10,... | collective-permute-start | bytes 688136 | tf_op jit(solution)/shard_map/ppermute | solution.py:17
  7.4 1.0 %slice.6 = bf16[2,2,144,256]{3,2,1,0:T(8,128)(2,1)S(1)} slice(bf16[2,2,256,256]{3,2,1,0:T(8,128)(2,1)} %refs_8_.1), slice={[0:2], [0:2], [112:256], [0:256]} | slice | bytes 589824 | tf_op jit(solution)/shard_map/slice | solution.py:32
  8.4 0.4 collective-permute-start
  8.8 0.1 reshape.7
  8.9 0.1 pad_add_fusion.info
  9.0 0.6 %shard_map.59 = (bf16[2,256,256]{2,1,0:T(8,128)(2,1)S(1)}, bf16[2,256,256]{2,1,0:T(8,128)(2,1)S(1)}) custom-call(s32[6]{0:T(128)S(1)} %pad_add_fusion.info, s32[2,2]{1,0:T(2,128)S(1)} %collective-permute-done.5.token, bf16[2,2,256,256]{3,2,1,0:T(8,128)(2,1)S(1)} %copy-done.1), custom_call_target="tpu_custom_call" | custom-call | tf_op jit(solution)/shard_map/pallas_call | solution.py:149
  9.6 1.6 %collective-permute-start.6 = (bf16[2,256,256]{2,1,0:T(8,128)(2,1)S(1)}, bf16[2,256,256]{2,1,0:T(8,128)(2,1)S(1)}, u32[]{:S(2)}, u32[]{:S(2)}) collective-permute-start(bf16[2,256,256]{2,1,0:T(8,128)(2,1)S(1)} %get-tuple-element.20.refs_0_), channel_id=1, source_target_pairs={{0,8},{4,12},{8,0},{12,4},{1,9},{5,13},{9,1},{13,5},{2,10},{6,14},... | collective-permute-start | bytes 786440 | tf_op jit(solution)/shard_map/ppermute | solution.py:17
  11.2 0.5 %collective-permute-start.9 = (bf16[2,256,256]{2,1,0:T(8,128)(2,1)S(1)}, bf16[2,256,256]{2,1,0:T(8,128)(2,1)S(1)}, u32[]{:S(2)}, u32[]{:S(2)}) collective-permute-start(bf16[2,256,256]{2,1,0:T(8,128)(2,1)S(1)} %get-tuple-element.21.refs_4_), channel_id=1, source_target_pairs={{0,8},{4,12},{8,0},{12,4},{1,9},{5,13},{9,1},{13,5},{2,10},{6,14},... | collective-permute-start | bytes 786440 | tf_op jit(solution)/shard_map/ppermute | solution.py:17
  11.7 9.5 %collective-permute-done.2.refs_10_ = bf16[2,2,112,256]{3,2,1,0:T(8,128)(2,1)S(1)} collective-permute-done((bf16[2,2,112,256]{3,2,1,0:T(8,128)(2,1)S(1)}, bf16[2,2,112,256]{3,2,1,0:T(8,128)(2,1)S(1)}, u32[]{:S(2)}, u32[]{:S(2)}) %collective-permute-start.2) | collective-permute-done | bytes 229408 | tf_op jit(solution)/shard_map/ppermute | solution.py:17
  21.2 3.5 %collective-permute-start.3 = (bf16[2,2,112,256]{3,2,1,0:T(8,128)(2,1)S(1)}, bf16[2,2,112,256]{3,2,1,0:T(8,128)(2,1)S(1)}, u32[]{:S(2)}, u32[]{:S(2)}) collective-permute-start(bf16[2,2,112,256]{3,2,1,0:T(8,128)(2,1)S(1)} %collective-permute-done.2.refs_10_), channel_id=1, source_target_pairs={{0,1},{1,0},{2,3},{3,2},{4,5},{5,4},{6,7},{7,6},{8,9},{9,8},{10,11... | collective-permute-start | bytes 688136 | tf_op jit(solution)/shard_map/ppermute | solution.py:17
  24.8 5.5 %collective-permute-done.refs_11_ = bf16[2,2,144,256]{3,2,1,0:T(8,128)(2,1)S(1)} collective-permute-done((bf16[2,2,144,256]{3,2,1,0:T(8,128)(2,1)S(1)}, bf16[2,2,144,256]{3,2,1,0:T(8,128)(2,1)S(1)}, u32[]{:S(2)}, u32[]{:S(2)}) %collective-permute-start) | collective-permute-done | bytes 294944 | tf_op jit(solution)/shard_map/ppermute | solution.py:17
  30.2 1.8 %collective-permute-done.3.refs_12_ = bf16[2,2,112,256]{3,2,1,0:T(8,128)(2,1)S(1)} collective-permute-done((bf16[2,2,112,256]{3,2,1,0:T(8,128)(2,1)S(1)}, bf16[2,2,112,256]{3,2,1,0:T(8,128)(2,1)S(1)}, u32[]{:S(2)}, u32[]{:S(2)}) %collective-permute-start.3) | collective-permute-done | bytes 229408 | tf_op jit(solution)/shard_map/ppermute | solution.py:17
  32.0 1.8 %collective-permute-start.4 = (bf16[2,2,144,256]{3,2,1,0:T(8,128)(2,1)S(1)}, bf16[2,2,144,256]{3,2,1,0:T(8,128)(2,1)S(1)}, u32[]{:S(2)}, u32[]{:S(2)}) collective-permute-start(bf16[2,2,144,256]{3,2,1,0:T(8,128)(2,1)S(1)} %collective-permute-done.refs_11_), channel_id=1, source_target_pairs={{0,1},{1,0},{2,3},{3,2},{4,5},{5,4},{6,7},{7,6},{8,9},{9,8},{10,11... | collective-permute-start | bytes 884744 | tf_op jit(solution)/shard_map/ppermute | solution.py:17
  33.8 0.5 %collective-permute-start.10 = (bf16[2,256,256]{2,1,0:T(8,128)(2,1)S(1)}, bf16[2,256,256]{2,1,0:T(8,128)(2,1)S(1)}, u32[]{:S(2)}, u32[]{:S(2)}) collective-permute-start(bf16[2,256,256]{2,1,0:T(8,128)(2,1)S(1)} %get-tuple-element.21.refs_4_), channel_id=1, source_target_pairs={{0,4},{4,0},{8,12},{12,8},{1,5},{5,1},{9,13},{13,9},{2,6},{6,2},{1... | collective-permute-start | bytes 786440 | tf_op jit(solution)/shard_map/ppermute | solution.py:17
  34.3 0.0 collective-permute-start.8
  34.3 0.5 %collective-permute-start.11 = (bf16[2,256,256]{2,1,0:T(8,128)(2,1)S(1)}, bf16[2,256,256]{2,1,0:T(8,128)(2,1)S(1)}, u32[]{:S(2)}, u32[]{:S(2)}) collective-permute-start(bf16[2,256,256]{2,1,0:T(8,128)(2,1)S(1)} %collective-permute-done.9.refs_5_), channel_id=1, source_target_pairs={{0,4},{4,0},{8,12},{12,8},{1,5},{5,1},{9,13},{13,9},{2,6},{6,2},{1... | collective-permute-start | bytes 786440 | tf_op jit(solution)/shard_map/ppermute | solution.py:17
  34.8 0.5 %collective-permute-done.7.refs_2_ = bf16[2,256,256]{2,1,0:T(8,128)(2,1)S(1)} collective-permute-done((bf16[2,256,256]{2,1,0:T(8,128)(2,1)S(1)}, bf16[2,256,256]{2,1,0:T(8,128)(2,1)S(1)}, u32[]{:S(2)}, u32[]{:S(2)}) %collective-permute-start.7) | collective-permute-done | bytes 262176 | tf_op jit(solution)/shard_map/ppermute | solution.py:17
  35.3 0.4 collective-permute-done.10.refs_6_
  35.7 0.4 collective-permute-done.8.refs_3_
  36.1 0.4 collective-permute-done.11.refs_7_
  36.5 2.0 %shard_map.60 = (bf16[2,2,2,256,256]{4,3,2,1,0:T(8,128)(2,1)S(1)}, bf16[2,2,256,256]{3,2,1,0:T(8,128)(2,1)S(1)}, f32[2,2,256,256]{3,2,1,0:T(8,128)S(1)}) custom-call(s32[6]{0:T(128)S(1)} %pad_add_fusion.info, bf16[2,256,256]{2,1,0:T(8,128)(2,1)S(1)} %get-tuple-element.20.refs_0_, bf16[2,256,256]{2,1,0:T(8,128)(2,1)S(1)} %collective-permute-done.6.refs_1_, ...), custom_call_target="tpu_custom_call" | custom-call | tf_op jit(solution)/shard_map/pallas_call | solution.py:155
  38.5 1.8 %collective-permute-done.4.refs_0_ = bf16[2,2,144,256]{3,2,1,0:T(8,128)(2,1)S(1)} collective-permute-done((bf16[2,2,144,256]{3,2,1,0:T(8,128)(2,1)S(1)}, bf16[2,2,144,256]{3,2,1,0:T(8,128)(2,1)S(1)}, u32[]{:S(2)}, u32[]{:S(2)}) %collective-permute-start.4) | collective-permute-done | bytes 294944 | tf_op jit(solution)/shard_map/ppermute | solution.py:17
  40.2 0.6 %shard_map.61 = (bf16[2,2,256,256]{3,2,1,0:T(8,128)(2,1)S(1)}, f32[2,2,64,256]{3,2,1,0:T(8,128)S(1)}, bf16[2,2,64,256]{3,2,1,0:T(8,128)(2,1)S(1)}) custom-call(bf16[2,2,144,256]{3,2,1,0:T(8,128)(2,1)S(1)} %collective-permute-done.4.refs_0_, bf16[2,2,2,256,256]{4,3,2,1,0:T(8,128)(2,1)S(1)} %get-tuple-element.24.refs_1_, ...), custom_call_target="tpu_custom_call" | custom-call | tf_op jit(solution)/shard_map/pallas_call | solution.py:166
  40.8 0.1 collective-permute-start.12
  40.9 1.3 %collective-permute-done.12.got = bf16[2,2,64,256]{3,2,1,0:T(8,128)(2,1)S(1)} collective-permute-done((bf16[2,2,64,256]{3,2,1,0:T(8,128)(2,1)S(1)}, bf16[2,2,64,256]{3,2,1,0:T(8,128)(2,1)S(1)}, u32[]{:S(2)}, u32[]{:S(2)}) %collective-permute-start.12) | collective-permute-done | bytes 131104 | tf_op jit(solution)/shard_map/ppermute | solution.py:17
  42.3 1.4 %collective-permute-start.13 = (bf16[2,64,256]{2,1,0:T(8,128)(2,1)S(1)}, bf16[2,64,256]{2,1,0:T(8,128)(2,1)S(1)}, u32[]{:S(2)}, u32[]{:S(2)}) collective-permute-start(bf16[2,64,256]{2,1,0:T(8,128)(2,1)S(1)} %get-tuple-element.29), channel_id=1, source_target_pairs={{0,8},{4,12},{8,0},{12,4},{1,9},{5,13},{9,1},{13,5},{2,10},{6,14},... | collective-permute-start | bytes 196616 | tf_op jit(solution)/shard_map/ppermute | solution.py:17
  43.7 0.8 %shard_map.63 = bf16[2,2,256,256]{3,2,1,0:T(8,128)(2,1)} custom-call(bf16[2,2,256,256]{3,2,1,0:T(8,128)(2,1)S(1)} %get-tuple-element.30.value), custom_call_target="tpu_custom_call" | custom-call | tf_op jit(solution)/shard_map/pallas_call | solution.py:175
  44.5 2.1 %collective-permute-done.13.refs_2_ = bf16[2,64,256]{2,1,0:T(8,128)(2,1)S(1)} collective-permute-done((bf16[2,64,256]{2,1,0:T(8,128)(2,1)S(1)}, bf16[2,64,256]{2,1,0:T(8,128)(2,1)S(1)}, u32[]{:S(2)}, u32[]{:S(2)}) %collective-permute-start.13) | collective-permute-done | bytes 65568 | tf_op jit(solution)/shard_map/ppermute | solution.py:17
  46.6 0.7 %shard_map.64 = f32[2,64,256]{2,1,0:T(8,128)} custom-call(f32[2,64,256]{2,1,0:T(8,128)S(1)} %copy-done.2, f32[2,64,256]{2,1,0:T(8,128)S(1)} %get-tuple-element.32.refs_1_, bf16[2,64,256]{2,1,0:T(8,128)(2,1)S(1)} %collective-permute-done.13.refs_2_), custom_call_target="tpu_custom_call" | custom-call | tf_op jit(solution)/shard_map/pallas_call | solution.py:185
  (14 shorter events, 0.1 us)
Async XLA Ops:
  0.6 6.8 %copy-start.3 = (s32[2,2]{1,0:T(2,128)S(1)}, s32[2,2]{1,0:T(2,128)}, u32[]{:S(2)}) copy-start(s32[2,2]{1,0:T(2,128)} %param.6) | copy-start | bytes 52
  0.6 8.3 %copy-start.1 = (bf16[2,2,256,256]{3,2,1,0:T(8,128)(2,1)S(1)}, bf16[2,2,256,256]{3,2,1,0:T(8,128)(2,1)}, u32[]{:S(2)}) copy-start(bf16[2,2,256,256]{3,2,1,0:T(8,128)(2,1)} %lower.1) | copy-start | bytes 1572868
  0.6 29.6 %collective-permute-start.1 = (bf16[2,2,256,256]{3,2,1,0:T(8,128)(2,1)}, bf16[2,2,256,256]{3,2,1,0:T(8,128)(2,1)S(1)}, u32[]{:S(2)}, u32[]{:S(2)}) collective-permute-start(bf16[2,2,256,256]{3,2,1,0:T(8,128)(2,1)} %refs_8_.1), channel_id=1, source_target_pairs={{0,1},{1,0},{2,3},{3,2},{4,5},{5,4},{6,7},{7,6},{8,9},{9,8},{10,11... | collective-permute-start | bytes 1572872 | tf_op jit(solution)/shard_map/ppermute | solution.py:17
  4.7 31.7 %copy-start = (bf16[2,2,256,256]{3,2,1,0:T(8,128)(2,1)S(1)}, bf16[2,2,256,256]{3,2,1,0:T(8,128)(2,1)}, u32[]{:S(2)}) copy-start(bf16[2,2,256,256]{3,2,1,0:T(8,128)(2,1)} %refs_8_.1) | copy-start | bytes 1572868
  4.7 16.5 %collective-permute-start.2 = (bf16[2,2,112,256]{3,2,1,0:T(8,128)(2,1)S(1)}, bf16[2,2,112,256]{3,2,1,0:T(8,128)(2,1)S(1)}, u32[]{:S(2)}, u32[]{:S(2)}) collective-permute-start(bf16[2,2,112,256]{3,2,1,0:T(8,128)(2,1)S(1)} %slice.7), channel_id=1, source_target_pairs={{0,2},{1,3},{2,0},{3,1},{4,6},{5,7},{6,4},{7,5},{8,10},{9,11},{10,... | collective-permute-start | bytes 688136 | tf_op jit(solution)/shard_map/ppermute | solution.py:17
  7.4 1.6 %collective-permute-start.5 = (s32[2,2]{1,0:T(2,128)S(1)}, s32[2,2]{1,0:T(2,128)S(1)}, u32[]{:S(2)}, u32[]{:S(2)}) collective-permute-start(s32[2,2]{1,0:T(2,128)S(1)} %copy-done.3), channel_id=1, source_target_pairs={{0,4},{4,0},{8,12},{12,8},{1,5},{5,1},{9,13},{13,9},{2,6},{6,2},{1... | collective-permute-start | bytes 56 | tf_op jit(solution)/shard_map/ppermute | solution.py:17
  8.4 21.9 %collective-permute-start = (bf16[2,2,144,256]{3,2,1,0:T(8,128)(2,1)S(1)}, bf16[2,2,144,256]{3,2,1,0:T(8,128)(2,1)S(1)}, u32[]{:S(2)}, u32[]{:S(2)}) collective-permute-start(bf16[2,2,144,256]{3,2,1,0:T(8,128)(2,1)S(1)} %slice.6), channel_id=1, source_target_pairs={{0,2},{1,3},{2,0},{3,1},{4,6},{5,7},{6,4},{7,5},{8,10},{9,11},{10,... | collective-permute-start | bytes 884744 | tf_op jit(solution)/shard_map/ppermute | solution.py:17
  9.6 24.7 %collective-permute-start.6 = (bf16[2,256,256]{2,1,0:T(8,128)(2,1)S(1)}, bf16[2,256,256]{2,1,0:T(8,128)(2,1)S(1)}, u32[]{:S(2)}, u32[]{:S(2)}) collective-permute-start(bf16[2,256,256]{2,1,0:T(8,128)(2,1)S(1)} %get-tuple-element.20.refs_0_), channel_id=1, source_target_pairs={{0,8},{4,12},{8,0},{12,4},{1,9},{5,13},{9,1},{13,5},{2,10},{6,14},... | collective-permute-start | bytes 786440 | tf_op jit(solution)/shard_map/ppermute | solution.py:17
  11.2 23.2 %collective-permute-start.9 = (bf16[2,256,256]{2,1,0:T(8,128)(2,1)S(1)}, bf16[2,256,256]{2,1,0:T(8,128)(2,1)S(1)}, u32[]{:S(2)}, u32[]{:S(2)}) collective-permute-start(bf16[2,256,256]{2,1,0:T(8,128)(2,1)S(1)} %get-tuple-element.21.refs_4_), channel_id=1, source_target_pairs={{0,8},{4,12},{8,0},{12,4},{1,9},{5,13},{9,1},{13,5},{2,10},{6,14},... | collective-permute-start | bytes 786440 | tf_op jit(solution)/shard_map/ppermute | solution.py:17
  21.2 10.8 %collective-permute-start.3 = (bf16[2,2,112,256]{3,2,1,0:T(8,128)(2,1)S(1)}, bf16[2,2,112,256]{3,2,1,0:T(8,128)(2,1)S(1)}, u32[]{:S(2)}, u32[]{:S(2)}) collective-permute-start(bf16[2,2,112,256]{3,2,1,0:T(8,128)(2,1)S(1)} %collective-permute-done.2.refs_10_), channel_id=1, source_target_pairs={{0,1},{1,0},{2,3},{3,2},{4,5},{5,4},{6,7},{7,6},{8,9},{9,8},{10,11... | collective-permute-start | bytes 688136 | tf_op jit(solution)/shard_map/ppermute | solution.py:17
  32.0 8.2 %collective-permute-start.4 = (bf16[2,2,144,256]{3,2,1,0:T(8,128)(2,1)S(1)}, bf16[2,2,144,256]{3,2,1,0:T(8,128)(2,1)S(1)}, u32[]{:S(2)}, u32[]{:S(2)}) collective-permute-start(bf16[2,2,144,256]{3,2,1,0:T(8,128)(2,1)S(1)} %collective-permute-done.refs_11_), channel_id=1, source_target_pairs={{0,1},{1,0},{2,3},{3,2},{4,5},{5,4},{6,7},{7,6},{8,9},{9,8},{10,11... | collective-permute-start | bytes 884744 | tf_op jit(solution)/shard_map/ppermute | solution.py:17
  33.8 1.5 %collective-permute-start.7 = (bf16[2,256,256]{2,1,0:T(8,128)(2,1)S(1)}, bf16[2,256,256]{2,1,0:T(8,128)(2,1)S(1)}, u32[]{:S(2)}, u32[]{:S(2)}) collective-permute-start(bf16[2,256,256]{2,1,0:T(8,128)(2,1)S(1)} %get-tuple-element.20.refs_0_), channel_id=1, source_target_pairs={{0,4},{4,0},{8,12},{12,8},{1,5},{5,1},{9,13},{13,9},{2,6},{6,2},{1... | collective-permute-start | bytes 786440 | tf_op jit(solution)/shard_map/ppermute | solution.py:17
  33.8 1.9 %collective-permute-start.10 = (bf16[2,256,256]{2,1,0:T(8,128)(2,1)S(1)}, bf16[2,256,256]{2,1,0:T(8,128)(2,1)S(1)}, u32[]{:S(2)}, u32[]{:S(2)}) collective-permute-start(bf16[2,256,256]{2,1,0:T(8,128)(2,1)S(1)} %get-tuple-element.21.refs_4_), channel_id=1, source_target_pairs={{0,4},{4,0},{8,12},{12,8},{1,5},{5,1},{9,13},{13,9},{2,6},{6,2},{1... | collective-permute-start | bytes 786440 | tf_op jit(solution)/shard_map/ppermute | solution.py:17
  34.3 1.8 %collective-permute-start.8 = (bf16[2,256,256]{2,1,0:T(8,128)(2,1)S(1)}, bf16[2,256,256]{2,1,0:T(8,128)(2,1)S(1)}, u32[]{:S(2)}, u32[]{:S(2)}) collective-permute-start(bf16[2,256,256]{2,1,0:T(8,128)(2,1)S(1)} %collective-permute-done.6.refs_1_), channel_id=1, source_target_pairs={{0,4},{4,0},{8,12},{12,8},{1,5},{5,1},{9,13},{13,9},{2,6},{6,2},{1... | collective-permute-start | bytes 786440 | tf_op jit(solution)/shard_map/ppermute | solution.py:17
  34.3 2.1 %collective-permute-start.11 = (bf16[2,256,256]{2,1,0:T(8,128)(2,1)S(1)}, bf16[2,256,256]{2,1,0:T(8,128)(2,1)S(1)}, u32[]{:S(2)}, u32[]{:S(2)}) collective-permute-start(bf16[2,256,256]{2,1,0:T(8,128)(2,1)S(1)} %collective-permute-done.9.refs_5_), channel_id=1, source_target_pairs={{0,4},{4,0},{8,12},{12,8},{1,5},{5,1},{9,13},{13,9},{2,6},{6,2},{1... | collective-permute-start | bytes 786440 | tf_op jit(solution)/shard_map/ppermute | solution.py:17
  40.8 1.4 %collective-permute-start.12 = (bf16[2,2,64,256]{3,2,1,0:T(8,128)(2,1)S(1)}, bf16[2,2,64,256]{3,2,1,0:T(8,128)(2,1)S(1)}, u32[]{:S(2)}, u32[]{:S(2)}) collective-permute-start(bf16[2,2,64,256]{3,2,1,0:T(8,128)(2,1)S(1)} %get-tuple-element.28), channel_id=1, source_target_pairs={{0,4},{4,0},{8,12},{12,8},{1,5},{5,1},{9,13},{13,9},{2,6},{6,2},{1... | collective-permute-start | bytes 393224 | tf_op jit(solution)/shard_map/ppermute | solution.py:17
  42.3 4.3 %collective-permute-start.13 = (bf16[2,64,256]{2,1,0:T(8,128)(2,1)S(1)}, bf16[2,64,256]{2,1,0:T(8,128)(2,1)S(1)}, u32[]{:S(2)}, u32[]{:S(2)}) collective-permute-start(bf16[2,64,256]{2,1,0:T(8,128)(2,1)S(1)} %get-tuple-element.29), channel_id=1, source_target_pairs={{0,8},{4,12},{8,0},{12,4},{1,9},{5,13},{9,1},{13,5},{2,10},{6,14},... | collective-permute-start | bytes 196616 | tf_op jit(solution)/shard_map/ppermute | solution.py:17
  43.7 2.9 %copy-start.2 = (f32[2,64,256]{2,1,0:T(8,128)S(1)}, f32[2,64,256]{2,1,0:T(8,128)}, u32[]{:S(2)}) copy-start(f32[2,64,256]{2,1,0:T(8,128)} %refs_0_.1) | copy-start | bytes 393220

commit v6 on v5

--- a/solution.py
+++ b/solution.py
@@ -24,12 +24,28 @@
     return held
 
 
+def cut_kernel(whole, first, rest):
+    first[...] = whole[:, :, :first.shape[2], :]
+    rest[...] = whole[:, :, first.shape[2]:, :]
+
+
+def cut_rows(whole, cut):
+    i, j, a, b = whole.shape
+    return call(
+        cut_kernel,
+        [jax.ShapeDtypeStruct((i, j, cut, b), BF16), jax.ShapeDtypeStruct((i, j, a - cut, b), BF16)],
+        [VMEM],
+        4,
+    )(whole)
+
+
 def column_gather(own, n, cut):
     far = [1 << p for p in reversed(range(1, n.bit_length() - 1))]
     whole, first, rest = slice(0, own.shape[2]), slice(0, cut), slice(cut, own.shape[2])
+    head, tail = cut_rows(own, cut)
     beside = exchange(own, "col", n, 1)
-    upper = gather(own[:, :, first], "col", n, far)[1:]
-    lower = gather(own[:, :, rest], "col", n, far)[1:]
+    upper = gather(head, "col", n, far)[1:]
+    lower = gather(tail, "col", n, far)[1:]
     arrays, beside = lax.optimization_barrier(([a for a, _ in lower], beside))
     lower = [(a, d) for a, (_, d) in zip(arrays, lower)]
     top = [(exchange(a, "col", n, 1), d ^ 1) for a, d in upper]

time: 47.4 us -> 47.5 us (level)
    unnamed x8 -> x10, local copies, waits for them, and re-layouts: 0.02 us -> 2.13 us
    slice x2 -> x0, local copies, waits for them, and re-layouts: 1.97 us -> none  [the longest x1 0.99 us: column_gather(): upper = gather(own[:, :, first], 'col', n, far)[1:]]
  transfers between devices with their start and end apart: 14 -> 14, of which waited for: 10 -> 11; matrix products, arithmetic and copies ran while one was open for 5% -> 0% of each run, Pallas kernels for 7% -> 7%
where the time goes in v6:
time: 47.5 us; the launch traced here: 47.2 us
  waiting for transfers between devices  23.2 us (49%)
  starting transfers between devices  16.3 us (34%)
  Pallas kernels  4.75 us (10%)
  local copies, waits for them, and re-layouts  2.21 us (5%)
  between operations  0.7 us (1%)
    ppermute x14, waiting for transfers between devices, exchange(): return lax.ppermute(array, axis, [(i, i ^ distance) for i in range(n)])  23.2 us
    ppermute x14, starting transfers between devices, exchange(): return lax.ppermute(array, axis, [(i, i ^ distance) for i in range(n)])  16.3 us
    unnamed x10, local copies, waits for them, and re-layouts  2.13 us
    pallas_call x1, Pallas kernels, on_device(): call(functools.partial(early_kernel, [d for _, d in pieces], [(at, d) for...  1.98 us
  transfers between devices with their start and end apart: 14, of which 11 were waited for; matrix products, arithmetic and copies ran while one was open for 0% of the time, Pallas kernels for 7%

profile of v6, /device:TPU:0, one launch (start us, length us, event | category | flops | bytes accessed | tf_op | source)
XLA Modules:
  0.0 47.2 jit_solution(7911222441840661379)
XLA Ops:
  0.6 3.1 %collective-permute-start.1 = (bf16[2,2,256,256]{3,2,1,0:T(8,128)(2,1)}, bf16[2,2,256,256]{3,2,1,0:T(8,128)(2,1)S(1)}, u32[]{:S(2)}, u32[]{:S(2)}) collective-permute-start(bf16[2,2,256,256]{3,2,1,0:T(8,128)(2,1)} %refs_8_.1), channel_id=1, source_target_pairs={{0,1},{1,0},{2,3},{3,2},{4,5},{5,4},{6,7},{7,6},{8,9},{9,8},{10,11... | collective-permute-start | bytes 1572872 | tf_op jit(solution)/shard_map/ppermute | solution.py:17
  3.7 1.1 %copy-done = bf16[2,2,256,256]{3,2,1,0:T(8,128)(2,1)S(1)} copy-done((bf16[2,2,256,256]{3,2,1,0:T(8,128)(2,1)S(1)}, bf16[2,2,256,256]{3,2,1,0:T(8,128)(2,1)}, u32[]{:S(2)}) %copy-start) | copy-done | bytes 524312
  4.8 0.0 copy-start.4
  4.8 2.7 %collective-permute-start.2 = (bf16[2,2,112,256]{3,2,1,0:T(8,128)(2,1)S(1)}, bf16[2,2,112,256]{3,2,1,0:T(8,128)(2,1)S(1)}, u32[]{:S(2)}, u32[]{:S(2)}) collective-permute-start(bf16[2,2,112,256]{3,2,1,0:T(8,128)(2,1)S(1)} %get-tuple-element.22), channel_id=1, source_target_pairs={{0,2},{1,3},{2,0},{3,1},{4,6},{5,7},{6,4},{7,5},{8,10},{9,11},{10,... | collective-permute-start | bytes 688136 | tf_op jit(solution)/shard_map/ppermute | solution.py:17
  7.5 0.7 %collective-permute-start = (bf16[2,2,144,256]{3,2,1,0:T(8,128)(2,1)S(1)}, bf16[2,2,144,256]{3,2,1,0:T(8,128)(2,1)S(1)}, u32[]{:S(2)}, u32[]{:S(2)}) collective-permute-start(bf16[2,2,144,256]{3,2,1,0:T(8,128)(2,1)S(1)} %get-tuple-element.20), channel_id=1, source_target_pairs={{0,2},{1,3},{2,0},{3,1},{4,6},{5,7},{6,4},{7,5},{8,10},{9,11},{10,... | collective-permute-start | bytes 884744 | tf_op jit(solution)/shard_map/ppermute | solution.py:17
  8.2 0.1 reshape.7
  8.2 0.1 pad_add_fusion.info
  8.3 0.3 collective-permute-done.5.token
  8.6 1.0 %copy-done.2 = bf16[2,2,256,256]{3,2,1,0:T(8,128)(2,1)S(1)} copy-done((bf16[2,2,256,256]{3,2,1,0:T(8,128)(2,1)S(1)}, bf16[2,2,256,256]{3,2,1,0:T(8,128)(2,1)}, u32[]{:S(2)}) %copy-start.2) | copy-done | bytes 524312
  9.7 0.6 %shard_map.60 = (bf16[2,256,256]{2,1,0:T(8,128)(2,1)S(1)}, bf16[2,256,256]{2,1,0:T(8,128)(2,1)S(1)}) custom-call(s32[6]{0:T(128)S(1)} %pad_add_fusion.info, s32[2,2]{1,0:T(2,128)S(1)} %collective-permute-done.5.token, bf16[2,2,256,256]{3,2,1,0:T(8,128)(2,1)S(1)} %copy-done.2), custom_call_target="tpu_custom_call" | custom-call | tf_op jit(solution)/shard_map/pallas_call | solution.py:165
  10.3 1.6 %collective-permute-start.6 = (bf16[2,256,256]{2,1,0:T(8,128)(2,1)S(1)}, bf16[2,256,256]{2,1,0:T(8,128)(2,1)S(1)}, u32[]{:S(2)}, u32[]{:S(2)}) collective-permute-start(bf16[2,256,256]{2,1,0:T(8,128)(2,1)S(1)} %get-tuple-element.24.refs_0_), channel_id=1, source_target_pairs={{0,8},{4,12},{8,0},{12,4},{1,9},{5,13},{9,1},{13,5},{2,10},{6,14},... | collective-permute-start | bytes 786440 | tf_op jit(solution)/shard_map/ppermute | solution.py:17
  11.9 0.5 %collective-permute-start.9 = (bf16[2,256,256]{2,1,0:T(8,128)(2,1)S(1)}, bf16[2,256,256]{2,1,0:T(8,128)(2,1)S(1)}, u32[]{:S(2)}, u32[]{:S(2)}) collective-permute-start(bf16[2,256,256]{2,1,0:T(8,128)(2,1)S(1)} %get-tuple-element.25.refs_4_), channel_id=1, source_target_pairs={{0,8},{4,12},{8,0},{12,4},{1,9},{5,13},{9,1},{13,5},{2,10},{6,14},... | collective-permute-start | bytes 786440 | tf_op jit(solution)/shard_map/ppermute | solution.py:17
  12.4 8.8 %collective-permute-done.2.refs_10_ = bf16[2,2,112,256]{3,2,1,0:T(8,128)(2,1)S(1)} collective-permute-done((bf16[2,2,112,256]{3,2,1,0:T(8,128)(2,1)S(1)}, bf16[2,2,112,256]{3,2,1,0:T(8,128)(2,1)S(1)}, u32[]{:S(2)}, u32[]{:S(2)}) %collective-permute-start.2) | collective-permute-done | bytes 229408 | tf_op jit(solution)/shard_map/ppermute | solution.py:17
  21.2 3.6 %collective-permute-start.3 = (bf16[2,2,112,256]{3,2,1,0:T(8,128)(2,1)S(1)}, bf16[2,2,112,256]{3,2,1,0:T(8,128)(2,1)S(1)}, u32[]{:S(2)}, u32[]{:S(2)}) collective-permute-start(bf16[2,2,112,256]{3,2,1,0:T(8,128)(2,1)S(1)} %collective-permute-done.2.refs_10_), channel_id=1, source_target_pairs={{0,1},{1,0},{2,3},{3,2},{4,5},{5,4},{6,7},{7,6},{8,9},{9,8},{10,11... | collective-permute-start | bytes 688136 | tf_op jit(solution)/shard_map/ppermute | solution.py:17
  24.8 5.7 %collective-permute-done.refs_11_ = bf16[2,2,144,256]{3,2,1,0:T(8,128)(2,1)S(1)} collective-permute-done((bf16[2,2,144,256]{3,2,1,0:T(8,128)(2,1)S(1)}, bf16[2,2,144,256]{3,2,1,0:T(8,128)(2,1)S(1)}, u32[]{:S(2)}, u32[]{:S(2)}) %collective-permute-start) | collective-permute-done | bytes 294944 | tf_op jit(solution)/shard_map/ppermute | solution.py:17
  30.5 1.5 %collective-permute-done.3.refs_12_ = bf16[2,2,112,256]{3,2,1,0:T(8,128)(2,1)S(1)} collective-permute-done((bf16[2,2,112,256]{3,2,1,0:T(8,128)(2,1)S(1)}, bf16[2,2,112,256]{3,2,1,0:T(8,128)(2,1)S(1)}, u32[]{:S(2)}, u32[]{:S(2)}) %collective-permute-start.3) | collective-permute-done | bytes 229408 | tf_op jit(solution)/shard_map/ppermute | solution.py:17
  32.0 1.8 %collective-permute-start.4 = (bf16[2,2,144,256]{3,2,1,0:T(8,128)(2,1)S(1)}, bf16[2,2,144,256]{3,2,1,0:T(8,128)(2,1)S(1)}, u32[]{:S(2)}, u32[]{:S(2)}) collective-permute-start(bf16[2,2,144,256]{3,2,1,0:T(8,128)(2,1)S(1)} %collective-permute-done.refs_11_), channel_id=1, source_target_pairs={{0,1},{1,0},{2,3},{3,2},{4,5},{5,4},{6,7},{7,6},{8,9},{9,8},{10,11... | collective-permute-start | bytes 884744 | tf_op jit(solution)/shard_map/ppermute | solution.py:17
  33.8 0.5 %collective-permute-start.10 = (bf16[2,256,256]{2,1,0:T(8,128)(2,1)S(1)}, bf16[2,256,256]{2,1,0:T(8,128)(2,1)S(1)}, u32[]{:S(2)}, u32[]{:S(2)}) collective-permute-start(bf16[2,256,256]{2,1,0:T(8,128)(2,1)S(1)} %get-tuple-element.25.refs_4_), channel_id=1, source_target_pairs={{0,4},{4,0},{8,12},{12,8},{1,5},{5,1},{9,13},{13,9},{2,6},{6,2},{1... | collective-permute-start | bytes 786440 | tf_op jit(solution)/shard_map/ppermute | solution.py:17
  34.3 0.5 %collective-permute-start.11 = (bf16[2,256,256]{2,1,0:T(8,128)(2,1)S(1)}, bf16[2,256,256]{2,1,0:T(8,128)(2,1)S(1)}, u32[]{:S(2)}, u32[]{:S(2)}) collective-permute-start(bf16[2,256,256]{2,1,0:T(8,128)(2,1)S(1)} %collective-permute-done.9.refs_5_), channel_id=1, source_target_pairs={{0,4},{4,0},{8,12},{12,8},{1,5},{5,1},{9,13},{13,9},{2,6},{6,2},{1... | collective-permute-start | bytes 786440 | tf_op jit(solution)/shard_map/ppermute | solution.py:17
  34.8 0.5 %collective-permute-done.7.refs_2_ = bf16[2,256,256]{2,1,0:T(8,128)(2,1)S(1)} collective-permute-done((bf16[2,256,256]{2,1,0:T(8,128)(2,1)S(1)}, bf16[2,256,256]{2,1,0:T(8,128)(2,1)S(1)}, u32[]{:S(2)}, u32[]{:S(2)}) %collective-permute-start.7) | collective-permute-done | bytes 262176 | tf_op jit(solution)/shard_map/ppermute | solution.py:17
  35.3 0.4 collective-permute-done.10.refs_6_
  35.7 0.4 collective-permute-done.8.refs_3_
  36.1 0.4 collective-permute-done.11.refs_7_
  36.5 2.0 %shard_map.61 = (bf16[2,2,2,256,256]{4,3,2,1,0:T(8,128)(2,1)S(1)}, bf16[2,2,256,256]{3,2,1,0:T(8,128)(2,1)S(1)}, f32[2,2,256,256]{3,2,1,0:T(8,128)S(1)}) custom-call(s32[6]{0:T(128)S(1)} %pad_add_fusion.info, bf16[2,256,256]{2,1,0:T(8,128)(2,1)S(1)} %get-tuple-element.24.refs_0_, bf16[2,256,256]{2,1,0:T(8,128)(2,1)S(1)} %collective-permute-done.6.refs_1_, ...), custom_call_target="tpu_custom_call" | custom-call | tf_op jit(solution)/shard_map/pallas_call | solution.py:171
  38.4 1.8 %collective-permute-done.4.refs_0_ = bf16[2,2,144,256]{3,2,1,0:T(8,128)(2,1)S(1)} collective-permute-done((bf16[2,2,144,256]{3,2,1,0:T(8,128)(2,1)S(1)}, bf16[2,2,144,256]{3,2,1,0:T(8,128)(2,1)S(1)}, u32[]{:S(2)}, u32[]{:S(2)}) %collective-permute-start.4) | collective-permute-done | bytes 294944 | tf_op jit(solution)/shard_map/ppermute | solution.py:17
  40.2 0.6 %shard_map.62 = (bf16[2,2,256,256]{3,2,1,0:T(8,128)(2,1)S(1)}, f32[2,2,64,256]{3,2,1,0:T(8,128)S(1)}, bf16[2,2,64,256]{3,2,1,0:T(8,128)(2,1)S(1)}) custom-call(bf16[2,2,144,256]{3,2,1,0:T(8,128)(2,1)S(1)} %collective-permute-done.4.refs_0_, bf16[2,2,2,256,256]{4,3,2,1,0:T(8,128)(2,1)S(1)} %get-tuple-element.28.refs_1_, ...), custom_call_target="tpu_custom_call" | custom-call | tf_op jit(solution)/shard_map/pallas_call | solution.py:182
  40.8 0.1 collective-permute-start.12
  40.9 1.3 %collective-permute-done.12.got = bf16[2,2,64,256]{3,2,1,0:T(8,128)(2,1)S(1)} collective-permute-done((bf16[2,2,64,256]{3,2,1,0:T(8,128)(2,1)S(1)}, bf16[2,2,64,256]{3,2,1,0:T(8,128)(2,1)S(1)}, u32[]{:S(2)}, u32[]{:S(2)}) %collective-permute-start.12) | collective-permute-done | bytes 131104 | tf_op jit(solution)/shard_map/ppermute | solution.py:17
  42.2 1.4 %collective-permute-start.13 = (bf16[2,64,256]{2,1,0:T(8,128)(2,1)S(1)}, bf16[2,64,256]{2,1,0:T(8,128)(2,1)S(1)}, u32[]{:S(2)}, u32[]{:S(2)}) collective-permute-start(bf16[2,64,256]{2,1,0:T(8,128)(2,1)S(1)} %get-tuple-element.33), channel_id=1, source_target_pairs={{0,8},{4,12},{8,0},{12,4},{1,9},{5,13},{9,1},{13,5},{2,10},{6,14},... | collective-permute-start | bytes 196616 | tf_op jit(solution)/shard_map/ppermute | solution.py:17
  43.6 0.8 %shard_map.64 = bf16[2,2,256,256]{3,2,1,0:T(8,128)(2,1)} custom-call(bf16[2,2,256,256]{3,2,1,0:T(8,128)(2,1)S(1)} %get-tuple-element.34.value), custom_call_target="tpu_custom_call" | custom-call | tf_op jit(solution)/shard_map/pallas_call | solution.py:191
  44.4 2.1 %collective-permute-done.13.refs_2_ = bf16[2,64,256]{2,1,0:T(8,128)(2,1)S(1)} collective-permute-done((bf16[2,64,256]{2,1,0:T(8,128)(2,1)S(1)}, bf16[2,64,256]{2,1,0:T(8,128)(2,1)S(1)}, u32[]{:S(2)}, u32[]{:S(2)}) %collective-permute-start.13) | collective-permute-done | bytes 65568 | tf_op jit(solution)/shard_map/ppermute | solution.py:17
  46.6 0.7 %shard_map.65 = f32[2,64,256]{2,1,0:T(8,128)} custom-call(f32[2,64,256]{2,1,0:T(8,128)S(1)} %copy-done.3, f32[2,64,256]{2,1,0:T(8,128)S(1)} %get-tuple-element.36.refs_1_, bf16[2,64,256]{2,1,0:T(8,128)(2,1)S(1)} %collective-permute-done.13.refs_2_), custom_call_target="tpu_custom_call" | custom-call | tf_op jit(solution)/shard_map/pallas_call | solution.py:201
  (15 shorter events, 0.1 us)
Async XLA Ops:
  0.6 29.9 %collective-permute-start.1 = (bf16[2,2,256,256]{3,2,1,0:T(8,128)(2,1)}, bf16[2,2,256,256]{3,2,1,0:T(8,128)(2,1)S(1)}, u32[]{:S(2)}, u32[]{:S(2)}) collective-permute-start(bf16[2,2,256,256]{3,2,1,0:T(8,128)(2,1)} %refs_8_.1), channel_id=1, source_target_pairs={{0,1},{1,0},{2,3},{3,2},{4,5},{5,4},{6,7},{7,6},{8,9},{9,8},{10,11... | collective-permute-start | bytes 1572872 | tf_op jit(solution)/shard_map/ppermute | solution.py:17
  3.7 1.1 %copy-start = (bf16[2,2,256,256]{3,2,1,0:T(8,128)(2,1)S(1)}, bf16[2,2,256,256]{3,2,1,0:T(8,128)(2,1)}, u32[]{:S(2)}) copy-start(bf16[2,2,256,256]{3,2,1,0:T(8,128)(2,1)} %refs_8_.1) | copy-start | bytes 1572868
  4.8 31.7 %copy-start.1 = (bf16[2,2,256,256]{3,2,1,0:T(8,128)(2,1)S(1)}, bf16[2,2,256,256]{3,2,1,0:T(8,128)(2,1)}, u32[]{:S(2)}) copy-start(bf16[2,2,256,256]{3,2,1,0:T(8,128)(2,1)} %refs_8_.1) | copy-start | bytes 1572868
  4.8 2.7 %copy-start.4 = (s32[2,2]{1,0:T(2,128)S(1)}, s32[2,2]{1,0:T(2,128)}, u32[]{:S(2)}) copy-start(s32[2,2]{1,0:T(2,128)} %param.6) | copy-start | bytes 52
  4.8 16.4 %collective-permute-start.2 = (bf16[2,2,112,256]{3,2,1,0:T(8,128)(2,1)S(1)}, bf16[2,2,112,256]{3,2,1,0:T(8,128)(2,1)S(1)}, u32[]{:S(2)}, u32[]{:S(2)}) collective-permute-start(bf16[2,2,112,256]{3,2,1,0:T(8,128)(2,1)S(1)} %get-tuple-element.22), channel_id=1, source_target_pairs={{0,2},{1,3},{2,0},{3,1},{4,6},{5,7},{6,4},{7,5},{8,10},{9,11},{10,... | collective-permute-start | bytes 688136 | tf_op jit(solution)/shard_map/ppermute | solution.py:17
  7.5 1.1 %collective-permute-start.5 = (s32[2,2]{1,0:T(2,128)S(1)}, s32[2,2]{1,0:T(2,128)S(1)}, u32[]{:S(2)}, u32[]{:S(2)}) collective-permute-start(s32[2,2]{1,0:T(2,128)S(1)} %copy-done.4), channel_id=1, source_target_pairs={{0,4},{4,0},{8,12},{12,8},{1,5},{5,1},{9,13},{13,9},{2,6},{6,2},{1... | collective-permute-start | bytes 56 | tf_op jit(solution)/shard_map/ppermute | solution.py:17
  7.5 23.0 %collective-permute-start = (bf16[2,2,144,256]{3,2,1,0:T(8,128)(2,1)S(1)}, bf16[2,2,144,256]{3,2,1,0:T(8,128)(2,1)S(1)}, u32[]{:S(2)}, u32[]{:S(2)}) collective-permute-start(bf16[2,2,144,256]{3,2,1,0:T(8,128)(2,1)S(1)} %get-tuple-element.20), channel_id=1, source_target_pairs={{0,2},{1,3},{2,0},{3,1},{4,6},{5,7},{6,4},{7,5},{8,10},{9,11},{10,... | collective-permute-start | bytes 884744 | tf_op jit(solution)/shard_map/ppermute | solution.py:17
  8.6 1.0 %copy-start.2 = (bf16[2,2,256,256]{3,2,1,0:T(8,128)(2,1)S(1)}, bf16[2,2,256,256]{3,2,1,0:T(8,128)(2,1)}, u32[]{:S(2)}) copy-start(bf16[2,2,256,256]{3,2,1,0:T(8,128)(2,1)} %lower.1) | copy-start | bytes 1572868
  10.3 24.0 %collective-permute-start.6 = (bf16[2,256,256]{2,1,0:T(8,128)(2,1)S(1)}, bf16[2,256,256]{2,1,0:T(8,128)(2,1)S(1)}, u32[]{:S(2)}, u32[]{:S(2)}) collective-permute-start(bf16[2,256,256]{2,1,0:T(8,128)(2,1)S(1)} %get-tuple-element.24.refs_0_), channel_id=1, source_target_pairs={{0,8},{4,12},{8,0},{12,4},{1,9},{5,13},{9,1},{13,5},{2,10},{6,14},... | collective-permute-start | bytes 786440 | tf_op jit(solution)/shard_map/ppermute | solution.py:17
  11.9 22.4 %collective-permute-start.9 = (bf16[2,256,256]{2,1,0:T(8,128)(2,1)S(1)}, bf16[2,256,256]{2,1,0:T(8,128)(2,1)S(1)}, u32[]{:S(2)}, u32[]{:S(2)}) collective-permute-start(bf16[2,256,256]{2,1,0:T(8,128)(2,1)S(1)} %get-tuple-element.25.refs_4_), channel_id=1, source_target_pairs={{0,8},{4,12},{8,0},{12,4},{1,9},{5,13},{9,1},{13,5},{2,10},{6,14},... | collective-permute-start | bytes 786440 | tf_op jit(solution)/shard_map/ppermute | solution.py:17
  21.2 10.8 %collective-permute-start.3 = (bf16[2,2,112,256]{3,2,1,0:T(8,128)(2,1)S(1)}, bf16[2,2,112,256]{3,2,1,0:T(8,128)(2,1)S(1)}, u32[]{:S(2)}, u32[]{:S(2)}) collective-permute-start(bf16[2,2,112,256]{3,2,1,0:T(8,128)(2,1)S(1)} %collective-permute-done.2.refs_10_), channel_id=1, source_target_pairs={{0,1},{1,0},{2,3},{3,2},{4,5},{5,4},{6,7},{7,6},{8,9},{9,8},{10,11... | collective-permute-start | bytes 688136 | tf_op jit(solution)/shard_map/ppermute | solution.py:17
  32.0 8.2 %collective-permute-start.4 = (bf16[2,2,144,256]{3,2,1,0:T(8,128)(2,1)S(1)}, bf16[2,2,144,256]{3,2,1,0:T(8,128)(2,1)S(1)}, u32[]{:S(2)}, u32[]{:S(2)}) collective-permute-start(bf16[2,2,144,256]{3,2,1,0:T(8,128)(2,1)S(1)} %collective-permute-done.refs_11_), channel_id=1, source_target_pairs={{0,1},{1,0},{2,3},{3,2},{4,5},{5,4},{6,7},{7,6},{8,9},{9,8},{10,11... | collective-permute-start | bytes 884744 | tf_op jit(solution)/shard_map/ppermute | solution.py:17
  33.8 1.5 %collective-permute-start.7 = (bf16[2,256,256]{2,1,0:T(8,128)(2,1)S(1)}, bf16[2,256,256]{2,1,0:T(8,128)(2,1)S(1)}, u32[]{:S(2)}, u32[]{:S(2)}) collective-permute-start(bf16[2,256,256]{2,1,0:T(8,128)(2,1)S(1)} %get-tuple-element.24.refs_0_), channel_id=1, source_target_pairs={{0,4},{4,0},{8,12},{12,8},{1,5},{5,1},{9,13},{13,9},{2,6},{6,2},{1... | collective-permute-start | bytes 786440 | tf_op jit(solution)/shard_map/ppermute | solution.py:17
  33.8 1.9 %collective-permute-start.10 = (bf16[2,256,256]{2,1,0:T(8,128)(2,1)S(1)}, bf16[2,256,256]{2,1,0:T(8,128)(2,1)S(1)}, u32[]{:S(2)}, u32[]{:S(2)}) collective-permute-start(bf16[2,256,256]{2,1,0:T(8,128)(2,1)S(1)} %get-tuple-element.25.refs_4_), channel_id=1, source_target_pairs={{0,4},{4,0},{8,12},{12,8},{1,5},{5,1},{9,13},{13,9},{2,6},{6,2},{1... | collective-permute-start | bytes 786440 | tf_op jit(solution)/shard_map/ppermute | solution.py:17
  34.3 1.8 %collective-permute-start.8 = (bf16[2,256,256]{2,1,0:T(8,128)(2,1)S(1)}, bf16[2,256,256]{2,1,0:T(8,128)(2,1)S(1)}, u32[]{:S(2)}, u32[]{:S(2)}) collective-permute-start(bf16[2,256,256]{2,1,0:T(8,128)(2,1)S(1)} %collective-permute-done.6.refs_1_), channel_id=1, source_target_pairs={{0,4},{4,0},{8,12},{12,8},{1,5},{5,1},{9,13},{13,9},{2,6},{6,2},{1... | collective-permute-start | bytes 786440 | tf_op jit(solution)/shard_map/ppermute | solution.py:17
  34.3 2.1 %collective-permute-start.11 = (bf16[2,256,256]{2,1,0:T(8,128)(2,1)S(1)}, bf16[2,256,256]{2,1,0:T(8,128)(2,1)S(1)}, u32[]{:S(2)}, u32[]{:S(2)}) collective-permute-start(bf16[2,256,256]{2,1,0:T(8,128)(2,1)S(1)} %collective-permute-done.9.refs_5_), channel_id=1, source_target_pairs={{0,4},{4,0},{8,12},{12,8},{1,5},{5,1},{9,13},{13,9},{2,6},{6,2},{1... | collective-permute-start | bytes 786440 | tf_op jit(solution)/shard_map/ppermute | solution.py:17
  40.8 1.4 %collective-permute-start.12 = (bf16[2,2,64,256]{3,2,1,0:T(8,128)(2,1)S(1)}, bf16[2,2,64,256]{3,2,1,0:T(8,128)(2,1)S(1)}, u32[]{:S(2)}, u32[]{:S(2)}) collective-permute-start(bf16[2,2,64,256]{3,2,1,0:T(8,128)(2,1)S(1)} %get-tuple-element.32), channel_id=1, source_target_pairs={{0,4},{4,0},{8,12},{12,8},{1,5},{5,1},{9,13},{13,9},{2,6},{6,2},{1... | collective-permute-start | bytes 393224 | tf_op jit(solution)/shard_map/ppermute | solution.py:17
  42.2 4.3 %collective-permute-start.13 = (bf16[2,64,256]{2,1,0:T(8,128)(2,1)S(1)}, bf16[2,64,256]{2,1,0:T(8,128)(2,1)S(1)}, u32[]{:S(2)}, u32[]{:S(2)}) collective-permute-start(bf16[2,64,256]{2,1,0:T(8,128)(2,1)S(1)} %get-tuple-element.33), channel_id=1, source_target_pairs={{0,8},{4,12},{8,0},{12,4},{1,9},{5,13},{9,1},{13,5},{2,10},{6,14},... | collective-permute-start | bytes 196616 | tf_op jit(solution)/shard_map/ppermute | solution.py:17
  43.6 2.9 %copy-start.3 = (f32[2,64,256]{2,1,0:T(8,128)S(1)}, f32[2,64,256]{2,1,0:T(8,128)}, u32[]{:S(2)}) copy-start(f32[2,64,256]{2,1,0:T(8,128)} %refs_0_.1) | copy-start | bytes 393220

commit v7 on v4

--- a/solution.py
+++ b/solution.py
@@ -106,9 +106,9 @@
         update[k] = share
 
 
-def finish_kernel(block, final, total, update, turned, value, *sends):
+def finish_kernel(block, final, total, update, turned, value, kept, sent):
     half, cols, b = total.shape[:3]
-    step = b // len(sends)
+    step = kept.shape[2]
     for k in range(cols):
         share = update[k]
         for i in range(half):
@@ -117,8 +117,16 @@
                 partial += jnp.dot(block[i, j], final[i, j, k], preferred_element_type=F32)
             value[i, k] = partial.astype(BF16)
             share += jnp.dot(turned[half + i, k], value[i, k], preferred_element_type=F32)
-        for d, send in enumerate(sends):
-            send[k] = share[d * step:(d + 1) * step].astype(send.dtype)
+        for m in range(kept.shape[0]):
+            at = 2 * m * step
+            kept[m, k] = share[at:at + step]
+            sent[m, k] = share[at + step:at + 2 * step].astype(BF16)
+
+
+def chip_kernel(kept, got, own, *sends):
+    own[...] = kept[0] + got[0].astype(F32)
+    for m, send in enumerate(sends, 1):
+        send[...] = (kept[m] + got[m].astype(F32)).astype(BF16)
 
 
 def join_kernel(top, bottom, out, sems):
@@ -190,12 +198,16 @@
             [pltpu.VMEM(sums.shape, F32)],
         )(info, *[x for _, x, _ in others], factor, total, turned)
         part = shape((cols, b // n_row, b), BF16)
-        bottom, own, *sends = call(
+        pairs = (n_row // 2,) + part.shape
+        bottom, mine, theirs = call(
             finish_kernel,
-            [value, shape(part.shape, F32)] + [part] * (n_row - 1),
+            [value, shape(pairs, F32), shape(pairs, BF16)],
             [VMEM] * 5,
             8,
         )(last[1], final, total, update, turned)
+        own, *sends = call(chip_kernel, [shape(part.shape, F32)] + [part] * (n_row // 2 - 1), [VMEM] * 2, 2)(
+            mine, exchange(theirs, "row", n_row, 1)
+        )
         lower_out = call(
             join_kernel,
             shape(inverse_block.shape[:1] + lower_block.shape[1:], BF16),
@@ -204,7 +216,7 @@
             [pltpu.SemaphoreType.DMA((2,))],
             ANY,
         )(top, bottom)
-        got = [exchange(s, "row", n_row, d) for d, s in enumerate(sends, 1)]
+        got = [exchange(s, "row", n_row, 2 * m) for m, s in enumerate(sends, 1)]
         got, lower_out = lax.optimization_barrier((got, lower_out))
         diag_out = call(last_kernel, shape(diag_inverse.shape, F32), [VMEM] * (2 + len(got)), 4)(diag_inverse, own, *got)
         return lower_out, diag_out

time: 47.4 us -> 47.5 us (level)
    ppermute x15 -> x14, waiting for transfers between devices: 21.4 us -> 21.7 us  [exchange(): return lax.ppermute(array, axis, [(i, i ^ distance) for i in range(n)])]
    ppermute x15 -> x14, starting transfers between devices: 16.5 us -> 16.2 us  [exchange(): return lax.ppermute(array, axis, [(i, i ^ distance) for i in range(n)])]
  transfers between devices with their start and end apart: 15 -> 14, of which waited for: 7 -> 7; matrix products, arithmetic and copies ran while one was open for 4% -> 4% of each run, Pallas kernels for 9% -> 9%
where the time goes in v7:
time: 47.5 us; the launch traced here: 47.3 us
  waiting for transfers between devices  21.7 us (46%)
  starting transfers between devices  16.2 us (34%)
  Pallas kernels  5.71 us (12%)
  local copies, waits for them, and re-layouts  2.87 us (6%)
  between operations  0.71 us (1%)
    ppermute x14, waiting for transfers between devices, exchange(): return lax.ppermute(array, axis, [(i, i ^ distance) for i in range(n)])  21.7 us
    ppermute x14, starting transfers between devices, exchange(): return lax.ppermute(array, axis, [(i, i ^ distance) for i in range(n)])  16.2 us
    pallas_call x1, Pallas kernels, on_device(): call(functools.partial(early_kernel, [(start, d) for start, _, d in other...  1.59 us
    pallas_call x1, Pallas kernels, on_device(): call(functools.partial(place_kernel, [x for _, x in pieces], [(start, d)...  1.17 us
    slice x1, local copies, waits for them, and re-layouts, on_device(): inverse_block[:half]  1.06 us
    unnamed x4, local copies, waits for them, and re-layouts  1.05 us
  transfers between devices with their start and end apart: 14, of which 7 were waited for; matrix products, arithmetic and copies ran while one was open for 4% of the time, Pallas kernels for 9%

profile of v7, /device:TPU:0, one launch (start us, length us, event | category | flops | bytes accessed | tf_op | source)
XLA Modules:
  0.0 47.3 jit_solution(17783551633110315030)
XLA Ops:
  0.6 3.1 %collective-permute-start.1 = (bf16[2,2,256,256]{3,2,1,0:T(8,128)(2,1)}, bf16[2,2,256,256]{3,2,1,0:T(8,128)(2,1)S(1)}, u32[]{:S(2)}, u32[]{:S(2)}) collective-permute-start(bf16[2,2,256,256]{3,2,1,0:T(8,128)(2,1)} %param.4), channel_id=1, source_target_pairs={{0,1},{1,0},{2,3},{3,2},{4,5},{5,4},{6,7},{7,6},{8,9},{9,8},{10,11... | collective-permute-start | bytes 1572872 | tf_op jit(solution)/shard_map/ppermute | solution.py:17
  3.7 1.1 %fusion = (bf16[1,2,256,256]{3,2,1,0:T(8,128)(2,1)S(1)}, bf16[1,2,256,256]{3,2,1,0:T(8,128)(2,1)S(1)}) fusion(bf16[2,2,256,256]{3,2,1,0:T(8,128)(2,1)} %param.4), kind=kLoop, calls=%fused_computation.1 | loop fusion | bytes 1048576 | tf_op jit(solution)/shard_map/slice | solution.py:175
  4.8 2.7 %collective-permute-start.2 = (bf16[1,2,256,256]{3,2,1,0:T(8,128)(2,1)S(1)}, bf16[1,2,256,256]{3,2,1,0:T(8,128)(2,1)S(1)}, u32[]{:S(2)}, u32[]{:S(2)}) collective-permute-start(bf16[1,2,256,256]{3,2,1,0:T(8,128)(2,1)S(1)} %get-tuple-element.42.refs_8_), channel_id=1, source_target_pairs={{0,2},{1,3},{2,0},{3,1},{4,6},{5,7},{6,4},{7,5},{8,10},{9,11},{10,... | collective-permute-start | bytes 786440 | tf_op jit(solution)/shard_map/ppermute | solution.py:17
  7.4 0.0 collective-permute-start.5
  7.4 0.3 collective-permute-start
  7.8 0.8 %reshape.7 = s32[4]{0:T(128)S(1)} reshape(s32[2,2]{1,0:T(2,128)} %param.6) | data formatting | bytes 32 | tf_op jit(solution)/shard_map/reshape | solution.py:174
  8.5 0.1 pad_add_fusion.info
  8.6 0.2 collective-permute-done.5.token
  8.8 1.0 %copy-done = bf16[2,2,256,256]{3,2,1,0:T(8,128)(2,1)S(1)} copy-done((bf16[2,2,256,256]{3,2,1,0:T(8,128)(2,1)S(1)}, bf16[2,2,256,256]{3,2,1,0:T(8,128)(2,1)}, u32[]{:S(2)}) %copy-start) | copy-done | bytes 524312
  9.8 0.6 %shard_map.59 = (bf16[2,256,256]{2,1,0:T(8,128)(2,1)S(1)}, bf16[2,256,256]{2,1,0:T(8,128)(2,1)S(1)}) custom-call(s32[6]{0:T(128)S(1)} %pad_add_fusion.info, s32[2,2]{1,0:T(2,128)S(1)} %collective-permute-done.5.token, bf16[2,2,256,256]{3,2,1,0:T(8,128)(2,1)S(1)} %copy-done), custom_call_target="tpu_custom_call" | custom-call | tf_op jit(solution)/shard_map/pallas_call | solution.py:178
  10.5 1.6 %collective-permute-start.9 = (bf16[2,256,256]{2,1,0:T(8,128)(2,1)S(1)}, bf16[2,256,256]{2,1,0:T(8,128)(2,1)S(1)}, u32[]{:S(2)}, u32[]{:S(2)}) collective-permute-start(bf16[2,256,256]{2,1,0:T(8,128)(2,1)S(1)} %get-tuple-element.25.refs_4_), channel_id=1, source_target_pairs={{0,8},{4,12},{8,0},{12,4},{1,9},{5,13},{9,1},{13,5},{2,10},{6,14},... | collective-permute-start | bytes 786440 | tf_op jit(solution)/shard_map/ppermute | solution.py:17
  12.0 0.5 %collective-permute-start.6 = (bf16[2,256,256]{2,1,0:T(8,128)(2,1)S(1)}, bf16[2,256,256]{2,1,0:T(8,128)(2,1)S(1)}, u32[]{:S(2)}, u32[]{:S(2)}) collective-permute-start(bf16[2,256,256]{2,1,0:T(8,128)(2,1)S(1)} %get-tuple-element.24.refs_0_), channel_id=1, source_target_pairs={{0,8},{4,12},{8,0},{12,4},{1,9},{5,13},{9,1},{13,5},{2,10},{6,14},... | collective-permute-start | bytes 786440 | tf_op jit(solution)/shard_map/ppermute | solution.py:17
  12.6 9.3 %collective-permute-done.2.refs_1_ = bf16[1,2,256,256]{3,2,1,0:T(8,128)(2,1)S(1)} collective-permute-done((bf16[1,2,256,256]{3,2,1,0:T(8,128)(2,1)S(1)}, bf16[1,2,256,256]{3,2,1,0:T(8,128)(2,1)S(1)}, u32[]{:S(2)}, u32[]{:S(2)}) %collective-permute-start.2) | collective-permute-done | bytes 262176 | tf_op jit(solution)/shard_map/ppermute | solution.py:17
  21.9 3.6 %collective-permute-start.3 = (bf16[1,2,256,256]{3,2,1,0:T(8,128)(2,1)S(1)}, bf16[1,2,256,256]{3,2,1,0:T(8,128)(2,1)S(1)}, u32[]{:S(2)}, u32[]{:S(2)}) collective-permute-start(bf16[1,2,256,256]{3,2,1,0:T(8,128)(2,1)S(1)} %collective-permute-done.2.refs_1_), channel_id=1, source_target_pairs={{0,1},{1,0},{2,3},{3,2},{4,5},{5,4},{6,7},{7,6},{8,9},{9,8},{10,11... | collective-permute-start | bytes 786440 | tf_op jit(solution)/shard_map/ppermute | solution.py:17
  25.5 4.9 %collective-permute-done.refs_2_ = bf16[1,2,256,256]{3,2,1,0:T(8,128)(2,1)S(1)} collective-permute-done((bf16[1,2,256,256]{3,2,1,0:T(8,128)(2,1)S(1)}, bf16[1,2,256,256]{3,2,1,0:T(8,128)(2,1)S(1)}, u32[]{:S(2)}, u32[]{:S(2)}) %collective-permute-start) | collective-permute-done | bytes 262176 | tf_op jit(solution)/shard_map/ppermute | solution.py:17
  30.4 0.0 collective-permute-start.10
  30.4 0.5 %collective-permute-start.7 = (bf16[2,256,256]{2,1,0:T(8,128)(2,1)S(1)}, bf16[2,256,256]{2,1,0:T(8,128)(2,1)S(1)}, u32[]{:S(2)}, u32[]{:S(2)}) collective-permute-start(bf16[2,256,256]{2,1,0:T(8,128)(2,1)S(1)} %get-tuple-element.24.refs_0_), channel_id=1, source_target_pairs={{0,4},{4,0},{8,12},{12,8},{1,5},{5,1},{9,13},{13,9},{2,6},{6,2},{1... | collective-permute-start | bytes 786440 | tf_op jit(solution)/shard_map/ppermute | solution.py:17
  30.9 0.1 collective-permute-start.11
  30.9 0.4 collective-permute-start.8
  31.4 1.3 %collective-permute-done.3.refs_3_ = bf16[1,2,256,256]{3,2,1,0:T(8,128)(2,1)S(1)} collective-permute-done((bf16[1,2,256,256]{3,2,1,0:T(8,128)(2,1)S(1)}, bf16[1,2,256,256]{3,2,1,0:T(8,128)(2,1)S(1)}, u32[]{:S(2)}, u32[]{:S(2)}) %collective-permute-start.3) | collective-permute-done | bytes 262176 | tf_op jit(solution)/shard_map/ppermute | solution.py:17
  32.7 1.8 %collective-permute-start.4 = (bf16[1,2,256,256]{3,2,1,0:T(8,128)(2,1)S(1)}, bf16[1,2,256,256]{3,2,1,0:T(8,128)(2,1)S(1)}, u32[]{:S(2)}, u32[]{:S(2)}) collective-permute-start(bf16[1,2,256,256]{3,2,1,0:T(8,128)(2,1)S(1)} %collective-permute-done.refs_2_), channel_id=1, source_target_pairs={{0,1},{1,0},{2,3},{3,2},{4,5},{5,4},{6,7},{7,6},{8,9},{9,8},{10,11... | collective-permute-start | bytes 786440 | tf_op jit(solution)/shard_map/ppermute | solution.py:17
  34.5 1.2 %shard_map.60 = (bf16[4,2,2,256,256]{4,3,2,1,0:T(8,128)(2,1)S(1)}, bf16[1,2,2,256,256]{4,3,2,1,0:T(8,128)(2,1)S(1)}, bf16[2,2,256,256]{3,2,1,0:T(8,128)(2,1)S(1)}, f32[2,2,256,256]{3,2,1,0:T(8,128)S(1)}) custom-call(s32[6]{0:T(128)S(1)} %pad_add_fusion.info, bf16[2,256,256]{2,1,0:T(8,128)(2,1)S(1)} %get-tuple-element.24.refs_0_, ...), custom_call_target="tpu_custom_call" | custom-call | tf_op jit(solution)/shard_map/pallas_call | solution.py:186
  35.7 1.6 %shard_map.61 = (bf16[1,2,256,256]{3,2,1,0:T(8,128)(2,1)S(1)}, f32[1,2,256,256]{3,2,1,0:T(8,128)S(1)}, f32[2,256,256]{2,1,0:T(8,128)S(1)}) custom-call(s32[6]{0:T(128)S(1)} %pad_add_fusion.info, bf16[2,2,256,256]{3,2,1,0:T(8,128)(2,1)S(1)} %collective-permute-done.1.refs_0_, bf16[1,2,256,256]{3,2,1,0:T(8,128)(2,1)S(1)} %collective-permute-done.2.refs_1_, ...), custom_call_target="tpu_custom_call" | custom-call | tf_op jit(solution)/shard_map/pallas_call | solution.py:193
  37.3 0.0 copy-start.1
  37.3 2.7 %collective-permute-done.4.block = bf16[1,2,256,256]{3,2,1,0:T(8,128)(2,1)S(1)} collective-permute-done((bf16[1,2,256,256]{3,2,1,0:T(8,128)(2,1)S(1)}, bf16[1,2,256,256]{3,2,1,0:T(8,128)(2,1)S(1)}, u32[]{:S(2)}, u32[]{:S(2)}) %collective-permute-start.4) | collective-permute-done | bytes 262176 | tf_op jit(solution)/shard_map/ppermute | solution.py:17
  40.0 0.8 %shard_map.62 = (bf16[1,2,256,256]{3,2,1,0:T(8,128)(2,1)S(1)}, f32[2,2,64,256]{3,2,1,0:T(8,128)S(1)}, bf16[2,2,64,256]{3,2,1,0:T(8,128)(2,1)S(1)}) custom-call(bf16[1,2,256,256]{3,2,1,0:T(8,128)(2,1)S(1)} %collective-permute-done.4.block, bf16[1,2,2,256,256]{4,3,2,1,0:T(8,128)(2,1)S(1)} %get-tuple-element.26.final, ...), custom_call_target="tpu_custom_call" | custom-call | tf_op jit(solution)/shard_map/pallas_call | solution.py:202
  40.8 0.1 collective-permute-start.12
  40.9 1.3 %collective-permute-done.12.got = bf16[2,2,64,256]{3,2,1,0:T(8,128)(2,1)S(1)} collective-permute-done((bf16[2,2,64,256]{3,2,1,0:T(8,128)(2,1)S(1)}, bf16[2,2,64,256]{3,2,1,0:T(8,128)(2,1)S(1)}, u32[]{:S(2)}, u32[]{:S(2)}) %collective-permute-start.12) | collective-permute-done | bytes 131104 | tf_op jit(solution)/shard_map/ppermute | solution.py:17
  42.2 1.6 %collective-permute-start.13 = (bf16[2,64,256]{2,1,0:T(8,128)(2,1)S(1)}, bf16[2,64,256]{2,1,0:T(8,128)(2,1)S(1)}, u32[]{:S(2)}, u32[]{:S(2)}) collective-permute-start(bf16[2,64,256]{2,1,0:T(8,128)(2,1)S(1)} %get-tuple-element.36), channel_id=1, source_target_pairs={{0,8},{4,12},{8,0},{12,4},{1,9},{5,13},{9,1},{13,5},{2,10},{6,14},... | collective-permute-start | bytes 196616 | tf_op jit(solution)/shard_map/ppermute | solution.py:17
  43.8 0.8 %shard_map.64 = bf16[2,2,256,256]{3,2,1,0:T(8,128)(2,1)} custom-call(bf16[1,2,256,256]{3,2,1,0:T(8,128)(2,1)S(1)} %get-tuple-element.37.top, bf16[1,2,256,256]{3,2,1,0:T(8,128)(2,1)S(1)} %get-tuple-element.38.bottom), custom_call_target="tpu_custom_call" | custom-call | tf_op jit(solution)/shard_map/pallas_call | solution.py:211
  44.6 1.9 %collective-permute-done.13.refs_2_ = bf16[2,64,256]{2,1,0:T(8,128)(2,1)S(1)} collective-permute-done((bf16[2,64,256]{2,1,0:T(8,128)(2,1)S(1)}, bf16[2,64,256]{2,1,0:T(8,128)(2,1)S(1)}, u32[]{:S(2)}, u32[]{:S(2)}) %collective-permute-start.13) | collective-permute-done | bytes 65568 | tf_op jit(solution)/shard_map/ppermute | solution.py:17
  46.6 0.7 %shard_map.65 = f32[2,64,256]{2,1,0:T(8,128)} custom-call(f32[2,64,256]{2,1,0:T(8,128)S(1)} %copy-done.1, f32[2,64,256]{2,1,0:T(8,128)S(1)} %get-tuple-element.40.refs_1_, bf16[2,64,256]{2,1,0:T(8,128)(2,1)S(1)} %collective-permute-done.13.refs_2_), custom_call_target="tpu_custom_call" | custom-call | tf_op jit(solution)/shard_map/pallas_call | solution.py:221
  (10 shorter events, 0.0 us)
Async XLA Ops:
  0.6 30.3 %collective-permute-start.1 = (bf16[2,2,256,256]{3,2,1,0:T(8,128)(2,1)}, bf16[2,2,256,256]{3,2,1,0:T(8,128)(2,1)S(1)}, u32[]{:S(2)}, u32[]{:S(2)}) collective-permute-start(bf16[2,2,256,256]{3,2,1,0:T(8,128)(2,1)} %param.4), channel_id=1, source_target_pairs={{0,1},{1,0},{2,3},{3,2},{4,5},{5,4},{6,7},{7,6},{8,9},{9,8},{10,11... | collective-permute-start | bytes 1572872 | tf_op jit(solution)/shard_map/ppermute | solution.py:17
  4.8 17.1 %collective-permute-start.2 = (bf16[1,2,256,256]{3,2,1,0:T(8,128)(2,1)S(1)}, bf16[1,2,256,256]{3,2,1,0:T(8,128)(2,1)S(1)}, u32[]{:S(2)}, u32[]{:S(2)}) collective-permute-start(bf16[1,2,256,256]{3,2,1,0:T(8,128)(2,1)S(1)} %get-tuple-element.42.refs_8_), channel_id=1, source_target_pairs={{0,2},{1,3},{2,0},{3,1},{4,6},{5,7},{6,4},{7,5},{8,10},{9,11},{10,... | collective-permute-start | bytes 786440 | tf_op jit(solution)/shard_map/ppermute | solution.py:17
  7.4 1.4 %collective-permute-start.5 = (s32[2,2]{1,0:T(2,128)}, s32[2,2]{1,0:T(2,128)S(1)}, u32[]{:S(2)}, u32[]{:S(2)}) collective-permute-start(s32[2,2]{1,0:T(2,128)} %param.6), channel_id=1, source_target_pairs={{0,4},{4,0},{8,12},{12,8},{1,5},{5,1},{9,13},{13,9},{2,6},{6,2},{1... | collective-permute-start | bytes 56 | tf_op jit(solution)/shard_map/ppermute | solution.py:17
  7.4 22.9 %collective-permute-start = (bf16[1,2,256,256]{3,2,1,0:T(8,128)(2,1)S(1)}, bf16[1,2,256,256]{3,2,1,0:T(8,128)(2,1)S(1)}, u32[]{:S(2)}, u32[]{:S(2)}) collective-permute-start(bf16[1,2,256,256]{3,2,1,0:T(8,128)(2,1)S(1)} %get-tuple-element.43.refs_9_), channel_id=1, source_target_pairs={{0,2},{1,3},{2,0},{3,1},{4,6},{5,7},{6,4},{7,5},{8,10},{9,11},{10,... | collective-permute-start | bytes 786440 | tf_op jit(solution)/shard_map/ppermute | solution.py:17
  8.8 1.0 %copy-start = (bf16[2,2,256,256]{3,2,1,0:T(8,128)(2,1)S(1)}, bf16[2,2,256,256]{3,2,1,0:T(8,128)(2,1)}, u32[]{:S(2)}) copy-start(bf16[2,2,256,256]{3,2,1,0:T(8,128)(2,1)} %lower.1) | copy-start | bytes 1572868
  10.5 19.9 %collective-permute-start.9 = (bf16[2,256,256]{2,1,0:T(8,128)(2,1)S(1)}, bf16[2,256,256]{2,1,0:T(8,128)(2,1)S(1)}, u32[]{:S(2)}, u32[]{:S(2)}) collective-permute-start(bf16[2,256,256]{2,1,0:T(8,128)(2,1)S(1)} %get-tuple-element.25.refs_4_), channel_id=1, source_target_pairs={{0,8},{4,12},{8,0},{12,4},{1,9},{5,13},{9,1},{13,5},{2,10},{6,14},... | collective-permute-start | bytes 786440 | tf_op jit(solution)/shard_map/ppermute | solution.py:17
  12.0 18.8 %collective-permute-start.6 = (bf16[2,256,256]{2,1,0:T(8,128)(2,1)S(1)}, bf16[2,256,256]{2,1,0:T(8,128)(2,1)S(1)}, u32[]{:S(2)}, u32[]{:S(2)}) collective-permute-start(bf16[2,256,256]{2,1,0:T(8,128)(2,1)S(1)} %get-tuple-element.24.refs_0_), channel_id=1, source_target_pairs={{0,8},{4,12},{8,0},{12,4},{1,9},{5,13},{9,1},{13,5},{2,10},{6,14},... | collective-permute-start | bytes 786440 | tf_op jit(solution)/shard_map/ppermute | solution.py:17
  21.9 10.8 %collective-permute-start.3 = (bf16[1,2,256,256]{3,2,1,0:T(8,128)(2,1)S(1)}, bf16[1,2,256,256]{3,2,1,0:T(8,128)(2,1)S(1)}, u32[]{:S(2)}, u32[]{:S(2)}) collective-permute-start(bf16[1,2,256,256]{3,2,1,0:T(8,128)(2,1)S(1)} %collective-permute-done.2.refs_1_), channel_id=1, source_target_pairs={{0,1},{1,0},{2,3},{3,2},{4,5},{5,4},{6,7},{7,6},{8,9},{9,8},{10,11... | collective-permute-start | bytes 786440 | tf_op jit(solution)/shard_map/ppermute | solution.py:17
  30.4 4.1 %collective-permute-start.10 = (bf16[2,256,256]{2,1,0:T(8,128)(2,1)S(1)}, bf16[2,256,256]{2,1,0:T(8,128)(2,1)S(1)}, u32[]{:S(2)}, u32[]{:S(2)}) collective-permute-start(bf16[2,256,256]{2,1,0:T(8,128)(2,1)S(1)} %get-tuple-element.25.refs_4_), channel_id=1, source_target_pairs={{0,4},{4,0},{8,12},{12,8},{1,5},{5,1},{9,13},{13,9},{2,6},{6,2},{1... | collective-permute-start | bytes 786440 | tf_op jit(solution)/shard_map/ppermute | solution.py:17
  30.4 4.1 %collective-permute-start.7 = (bf16[2,256,256]{2,1,0:T(8,128)(2,1)S(1)}, bf16[2,256,256]{2,1,0:T(8,128)(2,1)S(1)}, u32[]{:S(2)}, u32[]{:S(2)}) collective-permute-start(bf16[2,256,256]{2,1,0:T(8,128)(2,1)S(1)} %get-tuple-element.24.refs_0_), channel_id=1, source_target_pairs={{0,4},{4,0},{8,12},{12,8},{1,5},{5,1},{9,13},{13,9},{2,6},{6,2},{1... | collective-permute-start | bytes 786440 | tf_op jit(solution)/shard_map/ppermute | solution.py:17
  30.9 3.6 %collective-permute-start.11 = (bf16[2,256,256]{2,1,0:T(8,128)(2,1)S(1)}, bf16[2,256,256]{2,1,0:T(8,128)(2,1)S(1)}, u32[]{:S(2)}, u32[]{:S(2)}) collective-permute-start(bf16[2,256,256]{2,1,0:T(8,128)(2,1)S(1)} %collective-permute-done.9.refs_5_), channel_id=1, source_target_pairs={{0,4},{4,0},{8,12},{12,8},{1,5},{5,1},{9,13},{13,9},{2,6},{6,2},{1... | collective-permute-start | bytes 786440 | tf_op jit(solution)/shard_map/ppermute | solution.py:17
  30.9 3.6 %collective-permute-start.8 = (bf16[2,256,256]{2,1,0:T(8,128)(2,1)S(1)}, bf16[2,256,256]{2,1,0:T(8,128)(2,1)S(1)}, u32[]{:S(2)}, u32[]{:S(2)}) collective-permute-start(bf16[2,256,256]{2,1,0:T(8,128)(2,1)S(1)} %collective-permute-done.6.refs_1_), channel_id=1, source_target_pairs={{0,4},{4,0},{8,12},{12,8},{1,5},{5,1},{9,13},{13,9},{2,6},{6,2},{1... | collective-permute-start | bytes 786440 | tf_op jit(solution)/shard_map/ppermute | solution.py:17
  32.7 7.3 %collective-permute-start.4 = (bf16[1,2,256,256]{3,2,1,0:T(8,128)(2,1)S(1)}, bf16[1,2,256,256]{3,2,1,0:T(8,128)(2,1)S(1)}, u32[]{:S(2)}, u32[]{:S(2)}) collective-permute-start(bf16[1,2,256,256]{3,2,1,0:T(8,128)(2,1)S(1)} %collective-permute-done.refs_2_), channel_id=1, source_target_pairs={{0,1},{1,0},{2,3},{3,2},{4,5},{5,4},{6,7},{7,6},{8,9},{9,8},{10,11... | collective-permute-start | bytes 786440 | tf_op jit(solution)/shard_map/ppermute | solution.py:17
  37.3 9.3 %copy-start.1 = (f32[2,64,256]{2,1,0:T(8,128)S(1)}, f32[2,64,256]{2,1,0:T(8,128)}, u32[]{:S(2)}) copy-start(f32[2,64,256]{2,1,0:T(8,128)} %refs_0_.1) | copy-start | bytes 393220
  40.8 1.4 %collective-permute-start.12 = (bf16[2,2,64,256]{3,2,1,0:T(8,128)(2,1)S(1)}, bf16[2,2,64,256]{3,2,1,0:T(8,128)(2,1)S(1)}, u32[]{:S(2)}, u32[]{:S(2)}) collective-permute-start(bf16[2,2,64,256]{3,2,1,0:T(8,128)(2,1)S(1)} %get-tuple-element.35), channel_id=1, source_target_pairs={{0,4},{4,0},{8,12},{12,8},{1,5},{5,1},{9,13},{13,9},{2,6},{6,2},{1... | collective-permute-start | bytes 393224 | tf_op jit(solution)/shard_map/ppermute | solution.py:17
  42.2 4.3 %collective-permute-start.13 = (bf16[2,64,256]{2,1,0:T(8,128)(2,1)S(1)}, bf16[2,64,256]{2,1,0:T(8,128)(2,1)S(1)}, u32[]{:S(2)}, u32[]{:S(2)}) collective-permute-start(bf16[2,64,256]{2,1,0:T(8,128)(2,1)S(1)} %get-tuple-element.36), channel_id=1, source_target_pairs={{0,8},{4,12},{8,0},{12,4},{1,9},{5,13},{9,1},{13,5},{2,10},{6,14},... | collective-permute-start | bytes 196616 | tf_op jit(solution)/shard_map/ppermute | solution.py:17
